TPU v7x, 512 devices: a whole 4x8x8 slice. The times are simulated.
512 devices in a mesh: row: 16 (over x_hi, y), col: 32 (over z, x_lo, core).
Axes of the slice: x: 4 (x_hi: 2, x_lo: 2; x = x_hi * 2 + x_lo), y: 8, z: 8, core: 2. Of those that a mesh axis runs over, the one named last changes fastest.
Arguments:
- counts: int32 [16, 32], P('row', 'col'), may hold values from 1 to 3663
- weights: bfloat16 [16, 32, 2048, 512], P('row', 'col'), may hold values from -6 to 6
- hidden: bfloat16 [16, 32, 256, 2048], P('row', 'col'), may hold values from -6 to 6
- queries: bfloat16 [16, 32, 256, 1024], P('row', 'col'), may hold values from -100 to 100
- cotangent: bfloat16 [16, 32, 256, 1024], P('row', 'col'), may hold values from -6 to 6
- first_global: float32 [16, 2048, 256], P('row', 'col'), may hold values from -4 to 4
- first_moment: float32 [16, 2048, 256], P('row', 'col'), may hold values from -1.5 to 1.5
- second_global: float32 [32, 2048, 256], P('col', 'row'), may hold values from -4 to 4
- second_moment: float32 [32, 2048, 256], P('col', 'row'), may hold values from -1.5 to 1.5
Outputs:
- first_new: float32 [16, 2048, 256], P('row', 'col')
- first_moment_new: float32 [16, 2048, 256], P('row', 'col')
- second_new: float32 [32, 2048, 256], P('col', 'row')
- second_moment_new: float32 [32, 2048, 256], P('col', 'row')
All inputs are finite; a program needn't handle non-finite values.
Results may differ from a plain program's by a relative error of at most 0.035.
The roundings to bfloat16 on the way count: a program that leaves them out, or rounds other values in their place, can miss the bound.
Values sent between devices are 32-bit elements; how exact they have to be, the bound alone decides.
No kernel may reach another device: no remote copies, remote signals or barrier semaphores. Data moves between devices by JAX's collectives and lax.ppermute only.
A program may use at most 64 MiB of HBM per device.

v0:
```python
import math

import jax
import jax.numpy as jnp
from jax import lax
from jax.sharding import PartitionSpec as P

HEAD = 64
KVH = 2


inner_rate = 0.3
outer_rate = 0.7
momentum_keep = 0.9


def level_attend(keyval, queries):
    length = keyval.shape[0]
    half = keyval.shape[1] // 2
    rounded = keyval.astype(jnp.bfloat16)
    keys = rounded[:, :half].reshape(length, KVH, HEAD)
    values = rounded[:, half:].reshape(length, KVH, HEAD)
    grouped = queries.reshape(length, KVH, -1, HEAD)
    scores = jnp.einsum("sgqd,tgd->gqst", grouped, keys, preferred_element_type=jnp.float32) * (
        1.0 / math.sqrt(HEAD)
    )
    places = jnp.arange(length)
    causal = places[:, None] >= places[None, :]
    scores = jnp.where(causal, scores, -1e30)
    probs = jax.nn.softmax(scores, axis=-1).astype(jnp.bfloat16)
    attended = jnp.einsum("gqst,tgd->sgqd", probs, values, preferred_element_type=jnp.float32)
    return attended.reshape(length, -1)


def path_grads(weights, hidden, queries, cotangent):
    width = weights.shape[1] // 2
    qwidth = queries.shape[1] // 2
    factor = 1.0 / math.sqrt(hidden.shape[1])

    def forward(keyval):
        return jnp.concatenate(
            [
                level_attend(keyval[:, :width], queries[:, :qwidth]),
                level_attend(keyval[:, width:], queries[:, qwidth:]),
            ],
            axis=1,
        )

    projected = jnp.dot(hidden, weights, preferred_element_type=jnp.float32) * factor
    _, backward = jax.vjp(forward, projected)
    (dkeyval,) = backward(cotangent.astype(jnp.float32))
    return (
        jnp.dot(hidden.T, dkeyval.astype(jnp.bfloat16), preferred_element_type=jnp.float32) * factor
    )


def nesterov(global_part, moment, average):
    outer = global_part - average
    moment_new = momentum_keep * moment + outer
    return (global_part - outer_rate * (outer + momentum_keep * moment_new), moment_new)


def finish_first(level_weights, grads, own_count, total, global_part, moment):
    term = own_count * (level_weights.astype(jnp.float32) - inner_rate * grads)
    rows = global_part.shape[1]
    summed = lax.psum(term, "col")
    share = lax.dynamic_slice_in_dim(summed, lax.axis_index("col") * rows, rows, 0)
    new_global, new_moment = nesterov(global_part[0], moment[0], share / total)
    return (new_global[None], new_moment[None])


def finish_second(level_weights, grads, own_count, total, global_part, moment):
    term = own_count * (level_weights.astype(jnp.float32) - inner_rate * grads)
    rows = global_part.shape[1]
    summed = lax.psum(term, "row")
    share = lax.dynamic_slice_in_dim(summed, lax.axis_index("row") * rows, rows, 0)
    new_global, new_moment = nesterov(global_part[0], moment[0], share / total)
    return (new_global[None], new_moment[None])


def per_device(
    counts,
    weights,
    hidden,
    queries,
    cotangent,
    first_global,
    first_moment,
    second_global,
    second_moment,
):
    path_weights = weights[0, 0]
    path_hidden = hidden[0, 0]
    path_queries = queries[0, 0]
    path_cotangent = cotangent[0, 0]
    own_count = counts[0, 0].astype(jnp.float32)
    width = path_weights.shape[1] // 2
    first_total = lax.psum(own_count, "col")
    second_total = lax.psum(own_count, "row")
    grads = path_grads(path_weights, path_hidden, path_queries, path_cotangent)
    first_new, first_moment_new = finish_first(
        path_weights[:, :width],
        grads[:, :width],
        own_count,
        first_total,
        first_global,
        first_moment,
    )
    second_new, second_moment_new = finish_second(
        path_weights[:, width:],
        grads[:, width:],
        own_count,
        second_total,
        second_global,
        second_moment,
    )
    return (first_new, first_moment_new, second_new, second_moment_new)


def solution(mesh):
    return jax.shard_map(
        per_device,
        mesh=mesh,
        in_specs=(
            P("row", "col"),
            P("row", "col", None, None),
            P("row", "col", None, None),
            P("row", "col", None, None),
            P("row", "col", None, None),
            P("row", "col", None),
            P("row", "col", None),
            P("col", "row", None),
            P("col", "row", None),
        ),
        out_specs=(
            P("row", "col", None),
            P("row", "col", None),
            P("col", "row", None),
            P("col", "row", None),
        ),
        check_vma=False,
    )
```

profile of v0, /device:TPU:6, one launch (start us, length us, event | category | flops | bytes accessed | tf_op | source)
XLA Modules:
  0.0 464.1 jit_solution(4824767022135871319)
XLA Ops:
  7.9 4.1 copy.33
  13.5 1.8 fusion.85
  17.0 0.9 copy.39
  17.9 1.8 copy.40
  19.8 1.6 copy.38
  21.3 1.9 fusion.86
  23.2 1.8 copy.36
  25.0 2.3 fusion.48
  28.2 2.0 fusion.7
  31.3 1.8 copy.41
  33.7 2.9 fusion.49
  37.4 2.6 fusion.15
  40.7 1.0 fusion.45
  42.3 1.0 fusion.42
  44.1 0.9 copy-done.3
  44.9 2.7 fusion.17
  48.5 42.1 %psum.31 = f32[]{:T(128)} all-reduce(f32[]{:T(128)} %bitcast.1), channel_id=1, replica_groups=mesh['row'=16,'col'=32] {'row'}, use_global_device_ids=true, to_apply=%region_9.10 | all-reduce | flops 1 | bytes 8 | tf_op jit(solution)/shard_map/psum | solution.py:99
  90.6 57.3 %psum.29 = f32[]{:T(128)} all-reduce(f32[]{:T(128)} %bitcast.1), channel_id=1, replica_groups=mesh['row'=16,'col'=32] {'col'}, use_global_device_ids=true, to_apply=%region_7.8 | all-reduce | flops 1 | bytes 8 | tf_op jit(solution)/shard_map/psum | solution.py:98
  148.3 70.6 %all-reduce.11.cloned.1.call-done = f32[2048,256]{0,1:T(8,128)} async-done(((f32[2048,256]{0,1:T(8,128)}), f32[2048,256]{0,1:T(8,128)}) %all-reduce.11.cloned.1.call-update) | async-done | bytes 2097168 | tf_op jit(solution)/shard_map/psum | solution.py:75
  218.9 1.6 fusion.73
  220.5 0.8 copy.49
  221.3 0.8 copy.50
  222.0 232.2 %all-reduce.9.cloned.1.call-done = f32[2048,256]{0,1:T(8,128)} async-done(((f32[2048,256]{0,1:T(8,128)}), f32[2048,256]{0,1:T(8,128)}) %all-reduce.9.cloned.1.call-update) | async-done | bytes 2097168 | tf_op jit(solution)/shard_map/psum | solution.py:66
  454.2 1.7 fusion.72
  (74 shorter events, 11.2 us)
Async XLA Ops:
  7.2 4.8 %copy-start = (bf16[1,1,256,2048]{3,2,1,0:T(8,128)(2,1)S(1)}, bf16[1,1,256,2048]{3,2,1,0:T(8,128)(2,1)}, u32[]{:S(2)}) copy-start(bf16[1,1,256,2048]{3,2,1,0:T(8,128)(2,1)} %param.11) | copy-start | bytes 3145732
  7.2 211.7 %all-reduce.11.cloned.1.call-start = ((), (), s32[]{:S(2)}) async-start(), calls=%async_computation.1 | async-start | bytes 4194304 | tf_op jit(solution)/shard_map/psum | solution.py:75
  7.9 4.1 copy-start.4
  25.0 2.3 copy-start.5
  27.3 1.0 copy-start.22
  27.8 3.1 copy-start.1
  30.2 3.5 copy-start.19
  31.3 2.4 copy-start.17
  33.7 2.9 copy-start.8
  37.4 3.3 copy-start.13
  37.4 3.3 copy-start.21
  37.4 3.3 copy-start.23
  40.7 1.6 copy-start.2
  40.7 1.6 copy-start.6
  40.7 1.6 copy-start.18
  40.7 1.6 copy-start.20
  42.3 1.0 copy-start.15
  42.3 1.0 copy-start.16
  43.3 1.6 copy-start.3
  47.7 100.3 %copy-start.9 = (f32[1,128,256]{2,1,0:T(8,128)S(1)}, f32[1,128,256]{2,1,0:T(8,128)}, u32[]{:S(2)}) copy-start(f32[1,128,256]{2,1,0:T(8,128)} %param.16) | copy-start | bytes 393220
  47.7 100.4 %copy-start.10 = (f32[1,128,256]{2,1,0:T(8,128)S(1)}, f32[1,128,256]{2,1,0:T(8,128)}, u32[]{:S(2)}) copy-start(f32[1,128,256]{2,1,0:T(8,128)} %param.17) | copy-start | bytes 393220
  47.7 100.5 %copy-start.11 = (f32[1,64,256]{2,1,0:T(8,128)S(1)}, f32[1,64,256]{2,1,0:T(8,128)}, u32[]{:S(2)}) copy-start(f32[1,64,256]{2,1,0:T(8,128)} %param.14) | copy-start | bytes 196612
  47.7 100.6 %copy-start.12 = (f32[1,64,256]{2,1,0:T(8,128)S(1)}, f32[1,64,256]{2,1,0:T(8,128)}, u32[]{:S(2)}) copy-start(f32[1,64,256]{2,1,0:T(8,128)} %param.15) | copy-start | bytes 196612
  47.7 406.5 %all-reduce.9.cloned.1.call-start = ((), (), s32[]{:S(2)}) async-start(), calls=%async_computation | async-start | bytes 4194304 | tf_op jit(solution)/shard_map/psum | solution.py:66
  (2 other events, 1.9 us)
Sparse Core Ops, SparseCore 0:
  47.8 171.0 all-reduce.10
  221.8 232.2 all-reduce.8
where the time goes:
time: 469 us; the launch traced here: 464 us
  waiting for transfers between devices  303 us (65%)
  blocking collectives  99.5 us (21%)
  local copies, waits for them, and re-layouts  22.5 us (5%)
  between operations  15 us (3%)
  matrix products  14.2 us (3%)
  other arithmetic  9.41 us (2%)
    psum x1, waiting for transfers between devices, finish_first(): summed = lax.psum(term, 'col')  232 us
    psum x1, waiting for transfers between devices, finish_second(): summed = lax.psum(term, 'row')  70.6 us
    psum x1, blocking collectives, per_device(): first_total = lax.psum(own_count, 'col')  57.3 us
    psum x1, blocking collectives, per_device(): second_total = lax.psum(own_count, 'row')  42.1 us
    dot_general x4, matrix products, level_attend(): jnp.einsum('gqst,tgd->sgqd', probs, values, preferred_element_type=jnp.fl...  9.81 us
  transfers between devices with their start and end apart: 2, of which 2 were waited for; matrix products, arithmetic and copies ran while one was open for 1% of the time, Pallas kernels for 0%

commit v1 on v0

v1 whole, which is shorter than its diff:
```python
import functools
import math

import jax
import jax.numpy as jnp
from jax import lax
from jax.experimental import pallas as pl
from jax.experimental.pallas import tpu as pltpu
from jax.sharding import Mesh
from jax.sharding import PartitionSpec as P

HEAD = 64
LOG2E = math.log2(math.e)

inner_rate = 0.3
outer_rate = 0.7
momentum_keep = 0.9


def nt(a, b):
    return lax.dot_general(a, b, (((1,), (1,)), ((), ())), preferred_element_type=jnp.float32)


def tn(a, b):
    return lax.dot_general(a, b, (((0,), (0,)), ((), ())), preferred_element_type=jnp.float32)


def nn(a, b):
    return jnp.dot(a, b, preferred_element_type=jnp.float32)


def level_dkeyval(hidden_ref, weights_ref, queries_ref, cotangent_ref):
    length = hidden_ref.shape[0]
    factor = 1.0 / math.sqrt(hidden_ref.shape[1])
    projected = nn(hidden_ref[...], weights_ref[...]) * factor
    rounded = projected.astype(jnp.bfloat16).astype(jnp.float32)
    low = lax.broadcasted_iota(jnp.int32, (length, 128), 1) < HEAD
    key_place = lax.broadcasted_iota(jnp.int32, (length, length), 0)
    query_place = lax.broadcasted_iota(jnp.int32, (length, length), 1)
    causal = key_place <= query_place

    def placed(pair):
        turned = pltpu.roll(pair, HEAD, 1)
        zero = jnp.zeros_like(pair)
        out = []
        for even, odd in ((pair, turned), (turned, pair)):
            both = jnp.concatenate([jnp.where(low, even, zero), jnp.where(low, zero, odd)], axis=0)
            out.append(both.astype(jnp.bfloat16))
        return out

    keys = placed(rounded[:, :128])
    values = placed(rounded[:, 128:])
    dkeys, dvalues = [], []
    for group in range(2):
        dk = jnp.zeros((length, 128), jnp.float32)
        dv = jnp.zeros((length, 128), jnp.float32)
        for pair in (2 * group, 2 * group + 1):
            q = queries_ref[:, pair * 128 : (pair + 1) * 128]
            do = cotangent_ref[:, pair * 128 : (pair + 1) * 128]
            scores = nt(keys[group], q)
            dprobs = nt(values[group], do)
            heads = []
            for head in range(2):
                s = jnp.where(causal, scores[head * length : (head + 1) * length], -1e30)
                dp = dprobs[head * length : (head + 1) * length]
                top = jnp.max(s, axis=0, keepdims=True)
                e = jnp.exp2((s - top) * (LOG2E / math.sqrt(HEAD)))
                p = e * (1.0 / jnp.sum(e, axis=0, keepdims=True))
                delta = jnp.sum(p * dp, axis=0, keepdims=True)
                ds = p * (dp - delta)
                heads.append((nn(ds.astype(jnp.bfloat16), q), nn(p.astype(jnp.bfloat16), do)))
            dk += jnp.where(low, heads[0][0], heads[1][0])
            dv += jnp.where(low, heads[0][1], heads[1][1])
        dkeys.append(dk + pltpu.roll(dk, HEAD, 1))
        dvalues.append(dv + pltpu.roll(dv, HEAD, 1))
    dkey = jnp.where(low, dkeys[0], dkeys[1]) * (1.0 / math.sqrt(HEAD))
    dvalue = jnp.where(low, dvalues[0], dvalues[1])
    return jnp.concatenate([dkey, dvalue], axis=1).astype(jnp.bfloat16)


def terms(hidden_ref, weights_ref, dkeyval, count, start, rows):
    factor = 1.0 / math.sqrt(hidden_ref.shape[1])
    grads = tn(hidden_ref[:, start : start + rows], dkeyval)
    level_weights = weights_ref[start : start + rows, :].astype(jnp.float32)
    return count * (level_weights - (inner_rate * factor) * grads)


def second_kernel(counts_ref, hidden_ref, weights_ref, queries_ref, cotangent_ref, out_ref):
    count = counts_ref[0, 0].astype(jnp.float32)
    dkeyval = level_dkeyval(hidden_ref, weights_ref, queries_ref, cotangent_ref)
    for y in range(8):
        base = y * 264
        out_ref[base : base + 128, :] = terms(hidden_ref, weights_ref, dkeyval, count, y * 128, 128)
        out_ref[base + 128 : base + 136, :] = jnp.full((8, 256), count, jnp.float32)
        out_ref[base + 136 : base + 264, :] = terms(
            hidden_ref, weights_ref, dkeyval, count, (8 + y) * 128, 128
        )


def first_kernel(
    counts_ref, core_ref, hidden_ref, weights_ref, queries_ref, cotangent_ref, keep_ref, send_ref
):
    count = counts_ref[0, 0].astype(jnp.float32)
    own = core_ref[0, 0] == 0
    dkeyval = level_dkeyval(hidden_ref, weights_ref, queries_ref, cotangent_ref)
    for b in range(16):
        term = terms(hidden_ref, weights_ref, dkeyval, count, b * 128, 128)
        lower, upper = term[:64], term[64:]
        keep_ref[b * 72 : b * 72 + 64, :] = jnp.where(own, lower, upper)
        send_ref[b * 72 : b * 72 + 64, :] = jnp.where(own, upper, lower)
        keep_ref[b * 72 + 64 : b * 72 + 72, :] = jnp.full((8, 256), count, jnp.float32)
        send_ref[b * 72 + 64 : b * 72 + 72, :] = jnp.full((8, 256), count, jnp.float32)


def level_call(kernel, level, scalars, arrays, out_shapes):
    hidden, weights, queries, cotangent = arrays
    tokens, width = hidden.shape
    specs = [pl.BlockSpec(memory_space=pltpu.SMEM)] * len(scalars) + [
        pl.BlockSpec((tokens, width), lambda i: (0, 0)),
        pl.BlockSpec((width, weights.shape[1] // 2), lambda i: (0, level)),
        pl.BlockSpec((tokens, queries.shape[1] // 2), lambda i: (0, level)),
        pl.BlockSpec((tokens, queries.shape[1] // 2), lambda i: (0, level)),
    ]
    return pl.pallas_call(
        kernel,
        grid=(1,),
        in_specs=specs,
        out_specs=[pl.BlockSpec(s.shape, lambda i: (0, 0)) for s in out_shapes],
        out_shape=out_shapes,
        compiler_params=pltpu.CompilerParams(vmem_limit_bytes=40 * 1024 * 1024),
        cost_estimate=pl.CostEstimate(
            flops=2 * 10**9, bytes_accessed=5 * 2**20, transcendentals=2**19
        ),
    )(*scalars, *arrays)


def nesterov(global_part, moment, average):
    outer = global_part - average
    moment_new = momentum_keep * moment + outer
    return (global_part - outer_rate * (outer + momentum_keep * moment_new), moment_new)


def first_finish_kernel(parts_ref, global_ref, moment_ref, new_ref, moment_new_ref):
    total = parts_ref[0:72, :]
    for b in range(1, 16):
        total += parts_ref[b * 72 : (b + 1) * 72, :]
    new_ref[...], moment_new_ref[...] = nesterov(
        global_ref[...], moment_ref[...], total[:64] / total[64:65]
    )


def second_finish_kernel(place_ref, own_ref, other_ref, global_ref, moment_ref, new_ref, moment_new_ref):
    place = place_ref[0, 0]

    def finish(rows, count):
        skip = 8 if rows else 0
        total = own_ref[rows : rows + 128, :] + other_ref[skip : skip + 128, :]
        counts = own_ref[128:136, :] + other_ref[count : count + 8, :]
        new_ref[...], moment_new_ref[...] = nesterov(
            global_ref[...], moment_ref[...], total / counts[0:1]
        )

    @pl.when(place == 0)
    def _():
        finish(0, 128)

    @pl.when(place == 1)
    def _():
        finish(136, 0)


def finish_call(kernel, scalars, arrays, shape):
    vmem = pl.BlockSpec(memory_space=pltpu.VMEM)
    return pl.pallas_call(
        kernel,
        in_specs=[pl.BlockSpec(memory_space=pltpu.SMEM)] * len(scalars) + [vmem] * len(arrays),
        out_specs=[vmem, vmem],
        out_shape=[jax.ShapeDtypeStruct(shape, jnp.float32)] * 2,
    )(*scalars, *arrays)


def per_device(
    counts,
    weights,
    hidden,
    queries,
    cotangent,
    first_global,
    first_moment,
    second_global,
    second_moment,
):
    arrays = (hidden[0, 0], weights[0, 0], queries[0, 0], cotangent[0, 0])
    x_hi = lax.axis_index("x_hi")
    core = lax.axis_index("core")
    f32 = functools.partial(jax.ShapeDtypeStruct, dtype=jnp.float32)

    (second_terms,) = level_call(second_kernel, 1, (counts,), arrays, [f32((8 * 264, 256))])
    second_share = lax.psum_scatter(second_terms, "y", scatter_dimension=0, tiled=True)

    counts_after, _ = lax.optimization_barrier((counts, second_terms))
    keep, send = level_call(
        first_kernel,
        0,
        (counts_after, jnp.full((1, 1), core, jnp.int32)),
        arrays,
        [f32((16 * 72, 256)), f32((16 * 72, 256))],
    )
    pair_terms = keep + lax.ppermute(send, "core", [(0, 1), (1, 0)])
    parts = lax.all_to_all(pair_terms, ("z", "x_lo"), 0, 0, tiled=True)
    first_new, first_moment_new = finish_call(
        first_finish_kernel, (), (parts, first_global[0], first_moment[0]), (64, 256)
    )

    second_share, _ = lax.optimization_barrier((second_share, first_new))
    away = lax.dynamic_slice_in_dim(second_share, (1 - x_hi) * 128, 136, 0)
    other = lax.ppermute(away, "x_hi", [(0, 1), (1, 0)])
    second_new, second_moment_new = finish_call(
        second_finish_kernel,
        (jnp.full((1, 1), x_hi, jnp.int32),),
        (second_share, other, second_global[0], second_moment[0]),
        (128, 256),
    )
    return (first_new[None], first_moment_new[None], second_new[None], second_moment_new[None])


def solution(mesh):
    axes = ("x_hi", "y", "z", "x_lo", "core")
    fine = Mesh(mesh.devices.reshape(2, 8, 8, 2, 2), axes)
    row, col = axes[:2], axes[2:]
    return jax.shard_map(
        per_device,
        mesh=fine,
        in_specs=(
            P(row, col),
            P(row, col, None, None),
            P(row, col, None, None),
            P(row, col, None, None),
            P(row, col, None, None),
            P(row, col, None),
            P(row, col, None),
            P(col, row, None),
            P(col, row, None),
        ),
        out_specs=(
            P(row, col, None),
            P(row, col, None),
            P(col, row, None),
            P(col, row, None),
        ),
        check_vma=False,
    )
```

time: 469 us -> 96.1 us (0.20)
  waiting for transfers between devices: 303 us -> 38.4 us
  blocking collectives: 99.5 us -> 0 us
  starting transfers between devices: 0.08 us -> 17.1 us
  matrix products: 14.2 us -> 0 us
  Pallas kernels: 0 us -> 12.1 us
  local copies, waits for them, and re-layouts: 22.5 us -> 11.1 us
  other arithmetic: 9.41 us -> 1.18 us
    psum x2 -> x0, waiting for transfers between devices: 303 us -> none  [the longest x1 232 us: finish_first(): summed = lax.psum(term, 'col')]
    psum x2 -> x0, blocking collectives: 99.5 us -> none  [the longest x1 57.3 us: per_device(): first_total = lax.psum(own_count, 'col')]
    all_to_all x0 -> x1, waiting for transfers between devices: none -> 30.5 us  [per_device(): parts = lax.all_to_all(pair_terms, ('z', 'x_lo'), 0, 0, tiled=True)]
    dot_general x10 -> x0, matrix products: 14.2 us -> none  [the longest x4 9.81 us: level_attend(): jnp.einsum('gqst,tgd->sgqd', probs, values, preferred_element_type=jnp.fl...]
    pallas_call x0 -> x4, Pallas kernels: none -> 12.1 us  [the longest x2 8.17 us: level_call(): pl.pallas_call(kernel, grid=(1,), in_specs=specs, out_specs=[pl.BlockSpec...]
    all_to_all x0 -> x1, starting transfers between devices: none -> 11.8 us  [per_device(): parts = lax.all_to_all(pair_terms, ('z', 'x_lo'), 0, 0, tiled=True)]
    ppermute x0 -> x2, waiting for transfers between devices: none -> 7.95 us  [the longest x1 5.14 us: per_device(): other = lax.ppermute(away, 'x_hi', [(0, 1), (1, 0)])]
    slice x8 -> x0, local copies, waits for them, and re-layouts: 7.76 us -> none  [the longest x2 2.31 us: level_attend(): values = rounded[:, half:].reshape(length, KVH, HEAD)]
  transfers between devices with their start and end apart: 2 -> 4, of which waited for: 2 -> 3; matrix products, arithmetic and copies ran while one was open for 1% -> 1% of each run, Pallas kernels for 0% -> 6%
where the time goes in v1:
time: 96.1 us; the launch traced here: 94.6 us
  waiting for transfers between devices  38.4 us (40%)
  starting transfers between devices  17.1 us (18%)
  between operations  14.7 us (15%)
  Pallas kernels  12.1 us (13%)
  local copies, waits for them, and re-layouts  11.1 us (12%)
  other arithmetic  1.18 us (1%)
    all_to_all x1, waiting for transfers between devices, per_device(): parts = lax.all_to_all(pair_terms, ('z', 'x_lo'), 0, 0, tiled=True)  30.5 us
    all_to_all x1, starting transfers between devices, per_device(): parts = lax.all_to_all(pair_terms, ('z', 'x_lo'), 0, 0, tiled=True)  11.8 us
    unnamed x20, local copies, waits for them, and re-layouts  10.2 us
    pallas_call x2, Pallas kernels, level_call(): pl.pallas_call(kernel, grid=(1,), in_specs=specs, out_specs=[pl.BlockSpec...  8.17 us
    ppermute x1, waiting for transfers between devices, per_device(): other = lax.ppermute(away, 'x_hi', [(0, 1), (1, 0)])  5.14 us
    pallas_call x2, Pallas kernels, finish_call(): pl.pallas_call(kernel, in_specs=[pl.BlockSpec(memory_space=pltpu.SMEM)] *...  3.9 us
    ppermute x1, starting transfers between devices, per_device(): other = lax.ppermute(away, 'x_hi', [(0, 1), (1, 0)])  3.31 us
    ppermute x1, waiting for transfers between devices, per_device(): pair_terms = keep + lax.ppermute(send, 'core', [(0, 1), (1, 0)])  2.81 us
  transfers between devices with their start and end apart: 4, of which 3 were waited for; matrix products, arithmetic and copies ran while one was open for 1% of the time, Pallas kernels for 6%

profile of v1, /device:TPU:6, one launch (start us, length us, event | category | flops | bytes accessed | tf_op | source)
XLA Modules:
  0.0 94.6 jit_solution(8703019602930056809)
XLA Ops:
  7.2 0.0 reduce-scatter.2.cloned.1.call-start
  7.9 0.0 copy-start
  7.9 1.6 %copy-done = bf16[1,1,2048,512]{3,2,1,0:T(8,128)(2,1)S(1)} copy-done((bf16[1,1,2048,512]{3,2,1,0:T(8,128)(2,1)S(1)}, bf16[1,1,2048,512]{3,2,1,0:T(8,128)(2,1)}, u32[]{:S(2)}) %copy-start) | copy-done | bytes 2097176
  9.5 1.2 %copy-done.2 = bf16[1,1,256,2048]{3,2,1,0:T(8,128)(2,1)S(1)} copy-done((bf16[1,1,256,2048]{3,2,1,0:T(8,128)(2,1)S(1)}, bf16[1,1,256,2048]{3,2,1,0:T(8,128)(2,1)}, u32[]{:S(2)}) %copy-start.2) | copy-done | bytes 1048600
  10.7 1.0 %copy-done.4 = bf16[1,1,256,1024]{3,2,1,0:T(8,128)(2,1)S(1)} copy-done((bf16[1,1,256,1024]{3,2,1,0:T(8,128)(2,1)S(1)}, bf16[1,1,256,1024]{3,2,1,0:T(8,128)(2,1)}, u32[]{:S(2)}) %copy-start.4) | copy-done | bytes 524312
  11.7 1.0 %copy-done.6 = bf16[1,1,256,1024]{3,2,1,0:T(8,128)(2,1)S(1)} copy-done((bf16[1,1,256,1024]{3,2,1,0:T(8,128)(2,1)S(1)}, bf16[1,1,256,1024]{3,2,1,0:T(8,128)(2,1)}, u32[]{:S(2)}) %copy-start.6) | copy-done | bytes 524312
  12.8 4.7 %shard_map.120 = f32[2112,256]{1,0:T(8,128)} custom-call(s32[1,1]{1,0:T(1,128)S(6)} %copy.13.counts_ref, bf16[256,2048]{1,0:T(8,128)(2,1)S(1)} %bitcast.18, bf16[2048,512]{1,0:T(8,128)(2,1)S(1)} %bitcast.16, bf16[256,1024]{1,0:T(8,128)(2,1)S(1)} %bitcast.20, bf16[256,1024]{1,0:T(8,128)(2,1)S(1)} %bitcast.22), custom_call_target="tpu_custom_call" | custom-call | flops 2000000000 | bytes 5242880 | tf_op jit(solution)/shard_map/pallas_call | solution.py:124
  17.5 0.0 reduce-scatter.2.cloned.1.call-update
  17.5 1.6 %copy-done.1 = bf16[1,1,2048,512]{3,2,1,0:T(8,128)(2,1)S(1)} copy-done((bf16[1,1,2048,512]{3,2,1,0:T(8,128)(2,1)S(1)}, bf16[1,1,2048,512]{3,2,1,0:T(8,128)(2,1)}, u32[]{:S(2)}) %copy-start.1) | copy-done | bytes 2097176
  19.1 1.0 %copy-done.5 = bf16[1,1,256,1024]{3,2,1,0:T(8,128)(2,1)S(1)} copy-done((bf16[1,1,256,1024]{3,2,1,0:T(8,128)(2,1)S(1)}, bf16[1,1,256,1024]{3,2,1,0:T(8,128)(2,1)}, u32[]{:S(2)}) %copy-start.5) | copy-done | bytes 524312
  20.1 1.0 %copy-done.7 = bf16[1,1,256,1024]{3,2,1,0:T(8,128)(2,1)S(1)} copy-done((bf16[1,1,256,1024]{3,2,1,0:T(8,128)(2,1)S(1)}, bf16[1,1,256,1024]{3,2,1,0:T(8,128)(2,1)}, u32[]{:S(2)}) %copy-start.7) | copy-done | bytes 524312
  21.1 3.5 %shard_map.121 = (f32[1152,256]{1,0:T(8,128)S(1)}, f32[1152,256]{1,0:T(8,128)S(1)}) custom-call(s32[1,1]{1,0:T(1,128)S(6)} %copy.13.counts_ref, s32[1,1]{1,0:T(1,128)} %bitcast.4.core_ref, bf16[256,2048]{1,0:T(8,128)(2,1)S(1)} %bitcast.19, bf16[2048,512]{1,0:T(8,128)(2,1)S(1)} %bitcast.17, bf16[256,1024]{1,0:T(8,128)(2,1)S(1)} %bitcast.21, ...), custom_call_target="tpu_custom_call" | custom-call | flops 2000000000 | bytes 5242880 | tf_op jit(solution)/shard_map/pallas_call | solution.py:124
  24.6 1.9 %collective-permute-start = (f32[1152,256]{1,0:T(8,128)S(1)}, f32[1152,256]{1,0:T(8,128)S(1)}, u32[]{:S(2)}, u32[]{:S(2)}) collective-permute-start(f32[1152,256]{1,0:T(8,128)S(1)} %get-tuple-element.14), channel_id=1, source_target_pairs={{0,1},{1,0},{2,3},{3,2},{4,5},{5,4},{6,7},{7,6},{8,9},{9,8},{10,11... | collective-permute-start | bytes 3538952 | tf_op jit(solution)/shard_map/ppermute | solution.py:209
  26.5 2.8 %collective-permute-done = f32[1152,256]{1,0:T(8,128)S(1)} collective-permute-done((f32[1152,256]{1,0:T(8,128)S(1)}, f32[1152,256]{1,0:T(8,128)S(1)}, u32[]{:S(2)}, u32[]{:S(2)}) %collective-permute-start) | collective-permute-done | bytes 1179680 | tf_op jit(solution)/shard_map/ppermute | solution.py:209
  29.4 1.2 %add.8 = f32[1152,256]{1,0:T(8,128)} add(f32[1152,256]{1,0:T(8,128)S(1)} %get-tuple-element.13, f32[1152,256]{1,0:T(8,128)S(1)} %collective-permute-done) | non-fusion elementwise | flops 294912 | bytes 3538944 | tf_op jit(solution)/shard_map/add | solution.py:209
  30.5 11.8 %all-to-all-start = ((f32[16,72,256]{2,1,0:T(8,128)}), f32[16,72,256]{2,1,0:T(8,128)S(1)}, u32[]{:S(2)}, u32[]{:S(2)}) async-start(f32[16,72,256]{2,1,0:T(8,128)} %bitcast.5), calls=%async_computation | async-start | bytes 2359296 | tf_op jit(solution)/shard_map/all_to_all | solution.py:210
  42.3 30.5 %all-to-all-done = f32[16,72,256]{2,1,0:T(8,128)S(1)} async-done(((f32[16,72,256]{2,1,0:T(8,128)}), f32[16,72,256]{2,1,0:T(8,128)S(1)}, u32[]{:S(2)}, u32[]{:S(2)}) %all-to-all-start) | async-done | bytes 1179680 | tf_op jit(solution)/shard_map/all_to_all | solution.py:210
  72.8 1.0 %copy-done.8 = f32[16,72,256]{2,1,0:T(8,128)} copy-done((f32[16,72,256]{2,1,0:T(8,128)}, f32[16,72,256]{2,1,0:T(8,128)S(1)}, u32[]{:S(2)}) %copy-start.8) | copy-done | bytes 1179672
  73.8 2.0 %shard_map.122 = (f32[64,256]{1,0:T(8,128)}, f32[64,256]{1,0:T(8,128)}) custom-call(f32[1152,256]{1,0:T(8,128)} %bitcast.24, f32[64,256]{1,0:T(8,128)} %bitcast.27, f32[64,256]{1,0:T(8,128)} %bitcast.28), custom_call_target="tpu_custom_call" | custom-call | tf_op jit(solution)/shard_map/pallas_call | solution.py:174
  75.8 0.9 constant_dynamic-slice_fusion
  76.8 3.3 %collective-permute-start.1 = (f32[136,256]{1,0:T(8,128)S(1)}, f32[136,256]{1,0:T(8,128)S(1)}, u32[]{:S(2)}, u32[]{:S(2)}) collective-permute-start(f32[136,256]{1,0:T(8,128)S(1)} %constant_dynamic-slice_fusion), channel_id=1, source_target_pairs={{0,256},{256,0},{1,257},{257,1},{2,258},{258,2},{3,259},{259,3},{4... | collective-permute-start | bytes 417800 | tf_op jit(solution)/shard_map/ppermute | solution.py:217
  80.1 5.1 %collective-permute-done.1.other_ref = f32[136,256]{1,0:T(8,128)S(1)} collective-permute-done((f32[136,256]{1,0:T(8,128)S(1)}, f32[136,256]{1,0:T(8,128)S(1)}, u32[]{:S(2)}, u32[]{:S(2)}) %collective-permute-start.1) | collective-permute-done | bytes 139296 | tf_op jit(solution)/shard_map/ppermute | solution.py:217
  85.2 0.7 copy-done.9
  85.9 1.9 %shard_map.123 = (f32[128,256]{1,0:T(8,128)}, f32[128,256]{1,0:T(8,128)}) custom-call(s32[1,1]{1,0:T(1,128)} %bitcast.11.place_ref, f32[264,256]{1,0:T(8,128)} %reduce-scatter.2.cloned.1.call-done.own_ref, f32[136,256]{1,0:T(8,128)} %copy-done.9, f32[128,256]{1,0:T(8,128)} %bitcast.25, f32[128,256]{1,0:T(8,128)} %bitcast.26), custom_call_target="tpu_custom_call" | custom-call | tf_op jit(solution)/shard_map/pallas_call | solution.py:174
  (11 shorter events, 0.0 us)
Async XLA Ops:
  7.2 68.7 %reduce-scatter.2.cloned.1.call-start = ((), (), s32[]{:S(2)}) async-start(), calls=%async_computation.2 | async-start | bytes 2433024 | tf_op jit(solution)/shard_map/reduce_scatter | solution.py:199
  7.9 1.6 %copy-start = (bf16[1,1,2048,512]{3,2,1,0:T(8,128)(2,1)S(1)}, bf16[1,1,2048,512]{3,2,1,0:T(8,128)(2,1)}, u32[]{:S(2)}) copy-start(bf16[1,1,2048,512]{3,2,1,0:T(8,128)(2,1)} %param.10) | copy-start | bytes 6291460
  9.4 1.2 %copy-start.2 = (bf16[1,1,256,2048]{3,2,1,0:T(8,128)(2,1)S(1)}, bf16[1,1,256,2048]{3,2,1,0:T(8,128)(2,1)}, u32[]{:S(2)}) copy-start(bf16[1,1,256,2048]{3,2,1,0:T(8,128)(2,1)} %param.11) | copy-start | bytes 3145732
  10.7 1.0 %copy-start.4 = (bf16[1,1,256,1024]{3,2,1,0:T(8,128)(2,1)S(1)}, bf16[1,1,256,1024]{3,2,1,0:T(8,128)(2,1)}, u32[]{:S(2)}) copy-start(bf16[1,1,256,1024]{3,2,1,0:T(8,128)(2,1)} %param.12) | copy-start | bytes 1572868
  11.7 1.0 %copy-start.6 = (bf16[1,1,256,1024]{3,2,1,0:T(8,128)(2,1)S(1)}, bf16[1,1,256,1024]{3,2,1,0:T(8,128)(2,1)}, u32[]{:S(2)}) copy-start(bf16[1,1,256,1024]{3,2,1,0:T(8,128)(2,1)} %param.13) | copy-start | bytes 1572868
  12.8 4.7 %copy-start.3 = (bf16[1,1,256,2048]{3,2,1,0:T(8,128)(2,1)S(1)}, bf16[1,1,256,2048]{3,2,1,0:T(8,128)(2,1)}, u32[]{:S(2)}) copy-start(bf16[1,1,256,2048]{3,2,1,0:T(8,128)(2,1)} %param.11) | copy-start | bytes 3145732
  17.5 1.6 %copy-start.1 = (bf16[1,1,2048,512]{3,2,1,0:T(8,128)(2,1)S(1)}, bf16[1,1,2048,512]{3,2,1,0:T(8,128)(2,1)}, u32[]{:S(2)}) copy-start(bf16[1,1,2048,512]{3,2,1,0:T(8,128)(2,1)} %param.10) | copy-start | bytes 6291460
  19.1 1.0 %copy-start.5 = (bf16[1,1,256,1024]{3,2,1,0:T(8,128)(2,1)S(1)}, bf16[1,1,256,1024]{3,2,1,0:T(8,128)(2,1)}, u32[]{:S(2)}) copy-start(bf16[1,1,256,1024]{3,2,1,0:T(8,128)(2,1)} %param.12) | copy-start | bytes 1572868
  20.1 1.0 %copy-start.7 = (bf16[1,1,256,1024]{3,2,1,0:T(8,128)(2,1)S(1)}, bf16[1,1,256,1024]{3,2,1,0:T(8,128)(2,1)}, u32[]{:S(2)}) copy-start(bf16[1,1,256,1024]{3,2,1,0:T(8,128)(2,1)} %param.13) | copy-start | bytes 1572868
  24.6 4.7 %collective-permute-start = (f32[1152,256]{1,0:T(8,128)S(1)}, f32[1152,256]{1,0:T(8,128)S(1)}, u32[]{:S(2)}, u32[]{:S(2)}) collective-permute-start(f32[1152,256]{1,0:T(8,128)S(1)} %get-tuple-element.14), channel_id=1, source_target_pairs={{0,1},{1,0},{2,3},{3,2},{4,5},{5,4},{6,7},{7,6},{8,9},{9,8},{10,11... | collective-permute-start | bytes 3538952 | tf_op jit(solution)/shard_map/ppermute | solution.py:209
  30.5 42.3 %all-to-all-start = ((f32[16,72,256]{2,1,0:T(8,128)}), f32[16,72,256]{2,1,0:T(8,128)S(1)}, u32[]{:S(2)}, u32[]{:S(2)}) async-start(f32[16,72,256]{2,1,0:T(8,128)} %bitcast.5), calls=%async_computation | async-start | bytes 2359296 | tf_op jit(solution)/shard_map/all_to_all | solution.py:210
  72.8 1.0 %copy-start.8 = (f32[16,72,256]{2,1,0:T(8,128)}, f32[16,72,256]{2,1,0:T(8,128)S(1)}, u32[]{:S(2)}) copy-start(f32[16,72,256]{2,1,0:T(8,128)S(1)} %all-to-all-done) | copy-start | bytes 3538948
  76.8 8.5 %collective-permute-start.1 = (f32[136,256]{1,0:T(8,128)S(1)}, f32[136,256]{1,0:T(8,128)S(1)}, u32[]{:S(2)}, u32[]{:S(2)}) collective-permute-start(f32[136,256]{1,0:T(8,128)S(1)} %constant_dynamic-slice_fusion), channel_id=1, source_target_pairs={{0,256},{256,0},{1,257},{257,1},{2,258},{258,2},{3,259},{259,3},{4... | collective-permute-start | bytes 417800 | tf_op jit(solution)/shard_map/ppermute | solution.py:217
  85.2 0.7 copy-start.9
Sparse Core Ops, SparseCore 0:
  17.6 49.1 reduce-scatter.1

commit v2 on v1

v2 whole, which is shorter than its diff:
```python
import functools
import math

import jax
import jax.numpy as jnp
from jax import lax
from jax.experimental import pallas as pl
from jax.experimental.pallas import tpu as pltpu
from jax.sharding import Mesh
from jax.sharding import PartitionSpec as P

HEAD = 64
PARTS = 4
LOG2E = math.log2(math.e)

inner_rate = 0.3
outer_rate = 0.7
momentum_keep = 0.9


def nt(a, b):
    return lax.dot_general(a, b, (((1,), (1,)), ((), ())), preferred_element_type=jnp.float32)


def tn(a, b):
    return lax.dot_general(a, b, (((0,), (0,)), ((), ())), preferred_element_type=jnp.float32)


def nn(a, b):
    return jnp.dot(a, b, preferred_element_type=jnp.float32)


def level_dkeyval(projected, queries_ref, cotangent_ref):
    length = projected.shape[0]
    rounded = projected.astype(jnp.bfloat16).astype(jnp.float32)
    low = lax.broadcasted_iota(jnp.int32, (length, 128), 1) < HEAD
    key_place = lax.broadcasted_iota(jnp.int32, (length, length), 0)
    query_place = lax.broadcasted_iota(jnp.int32, (length, length), 1)
    causal = key_place <= query_place

    def placed(pair):
        turned = pltpu.roll(pair, HEAD, 1)
        zero = jnp.zeros_like(pair)
        out = []
        for even, odd in ((pair, turned), (turned, pair)):
            both = jnp.concatenate([jnp.where(low, even, zero), jnp.where(low, zero, odd)], axis=0)
            out.append(both.astype(jnp.bfloat16))
        return out

    keys = placed(rounded[:, :128])
    values = placed(rounded[:, 128:])
    dkeys, dvalues = [], []
    for group in range(2):
        dk = jnp.zeros((length, 128), jnp.float32)
        dv = jnp.zeros((length, 128), jnp.float32)
        for pair in (2 * group, 2 * group + 1):
            q = queries_ref[:, pair * 128 : (pair + 1) * 128]
            do = cotangent_ref[:, pair * 128 : (pair + 1) * 128]
            scores = nt(keys[group], q)
            dprobs = nt(values[group], do)
            heads = []
            for head in range(2):
                s = jnp.where(causal, scores[head * length : (head + 1) * length], -1e30)
                dp = dprobs[head * length : (head + 1) * length]
                top = jnp.max(s, axis=0, keepdims=True)
                e = jnp.exp2((s - top) * (LOG2E / math.sqrt(HEAD)))
                p = e * (1.0 / jnp.sum(e, axis=0, keepdims=True))
                delta = jnp.sum(p * dp, axis=0, keepdims=True)
                ds = p * (dp - delta)
                heads.append((nn(ds.astype(jnp.bfloat16), q), nn(p.astype(jnp.bfloat16), do)))
            dk += jnp.where(low, heads[0][0], heads[1][0])
            dv += jnp.where(low, heads[0][1], heads[1][1])
        dkeys.append(dk + pltpu.roll(dk, HEAD, 1))
        dvalues.append(dv + pltpu.roll(dv, HEAD, 1))
    dkey = jnp.where(low, dkeys[0], dkeys[1]) * (1.0 / math.sqrt(HEAD))
    dvalue = jnp.where(low, dvalues[0], dvalues[1])
    return jnp.concatenate([dkey, dvalue], axis=1).astype(jnp.bfloat16)


def terms_kernel(
    counts_ref, hidden, weights, queries, cotangent, second, keep, send, *scratch
):
    (hidden_ref, turned_ref, weights_ref, queries_ref, cotangent_ref) = scratch[:5]
    second_ref, keep_ref, send_ref, arrived, left = scratch[5:]
    width = hidden.shape[1]
    part = width // PARTS
    level = weights.shape[1] // 2
    heads = queries.shape[1] // 2

    copies = []
    for k in range(PARTS):
        rows = pl.ds(k * part, part)
        copies.append((hidden.at[:, rows], hidden_ref.at[:, rows]))
        copies.append((weights.at[rows], weights_ref.at[rows]))
    copies.append((queries, queries_ref))
    copies.append((cotangent, cotangent_ref))
    copies = [pltpu.make_async_copy(a, b, arrived.at[i]) for i, (a, b) in enumerate(copies)]
    for copy in copies:
        copy.start()

    count = counts_ref[0, 0].astype(jnp.float32)
    own = lax.axis_index("core") == 0
    factor = 1.0 / math.sqrt(width)
    scale = count * (inner_rate * factor)
    counts = jnp.full((8, 128), count, jnp.float32)
    for r in range(16):
        second_ref[r * 264 + 256 : r * 264 + 264, :] = counts
        keep_ref[r * 136 + 128 : r * 136 + 136, :] = counts
        send_ref[r * 136 + 128 : r * 136 + 136, :] = counts

    projected = None
    for k in range(PARTS):
        copies[2 * k].wait()
        copies[2 * k + 1].wait()
        rows = pl.ds(k * part, part)
        product = nn(hidden_ref[:, rows], weights_ref[rows, :])
        projected = product if projected is None else projected + product
        turned_ref[rows, :] = hidden_ref[:, rows].T
    projected = projected * factor
    copies[-2].wait()
    copies[-1].wait()

    def dkeyval(number):
        columns = pl.ds(number * heads, heads)
        return level_dkeyval(
            projected[:, number * level : (number + 1) * level],
            queries_ref.at[:, columns],
            cotangent_ref.at[:, columns],
        )

    def term(number, dkv, start, rows):
        grads = nn(turned_ref[start : start + rows, :], dkv)
        own_weights = weights_ref[start : start + rows, number * level : (number + 1) * level]
        return count * own_weights.astype(jnp.float32) - scale * grads

    leaving = []

    def leave(source, target, rows):
        copy = pltpu.make_async_copy(source.at[rows], target.at[rows], left.at[len(leaving)])
        copy.start()
        leaving.append(copy)

    dkv = dkeyval(1)
    for r in range(16):
        base = r * 264
        piece = term(1, dkv, r * 128, 128)
        second_ref[base : base + 128, :] = piece[:, :128]
        second_ref[base + 128 : base + 256, :] = piece[:, 128:]
        if r % 4 == 3:
            leave(second_ref, second, pl.ds((r - 3) * 264, 4 * 264))
    dkv = dkeyval(0)
    for r in range(16):
        piece = term(0, dkv, r * 128, 128)
        lower, upper = piece[:64], piece[64:]
        base = r * 136
        for ref, half in (
            (keep_ref, jnp.where(own, lower, upper)),
            (send_ref, jnp.where(own, upper, lower)),
        ):
            ref[base : base + 64, :] = half[:, :128]
            ref[base + 64 : base + 128, :] = half[:, 128:]
        if r % 4 == 3:
            rows = pl.ds((r - 3) * 136, 4 * 136)
            leave(keep_ref, keep, rows)
            leave(send_ref, send, rows)
    for copy in leaving:
        copy.wait()


SMEM = pl.BlockSpec(memory_space=pltpu.SMEM)
VMEM = pl.BlockSpec(memory_space=pltpu.VMEM)
HBM = pl.BlockSpec(memory_space=pltpu.HBM)
f32 = functools.partial(jax.ShapeDtypeStruct, dtype=jnp.float32)


def level_terms(counts, hidden, weights, queries, cotangent):
    arrays = (hidden, weights, queries, cotangent)
    shapes = [f32((16 * 264, 128)), f32((16 * 136, 128)), f32((16 * 136, 128))]
    return pl.pallas_call(
        terms_kernel,
        in_specs=[SMEM] + [HBM] * 4,
        out_specs=[HBM] * 3,
        out_shape=shapes,
        scratch_shapes=[
            pltpu.VMEM(hidden.shape, jnp.bfloat16),
            pltpu.VMEM(hidden.shape[::-1], jnp.bfloat16),
            pltpu.VMEM(weights.shape, jnp.bfloat16),
            pltpu.VMEM(queries.shape, jnp.bfloat16),
            pltpu.VMEM(cotangent.shape, jnp.bfloat16),
        ]
        + [pltpu.VMEM(s.shape, jnp.float32) for s in shapes]
        + [pltpu.SemaphoreType.DMA((2 * PARTS + 2,)), pltpu.SemaphoreType.DMA((12,))],
        compiler_params=pltpu.CompilerParams(vmem_limit_bytes=62 * 1024 * 1024),
        cost_estimate=pl.CostEstimate(
            flops=2 * 10**9, bytes_accessed=8 * 2**20, transcendentals=2**20
        ),
    )(counts, *arrays)


def pair_kernel(mine_ref, other_ref, keep_refs, send_refs):
    z = lax.axis_index("z")
    step = 1 - 2 * lax.rem(z, 2)
    for x, neighbour in ((0, z + step), (1, z - step)):
        for ref, holder in ((keep_refs[x], z), (send_refs[x], neighbour)):
            for s in range(4):
                start = pl.multiple_of(lax.rem(holder + 2 * s + 8, 8) * 272 + x * 136, 8)
                rows = pl.ds(start, 136)
                ref[s * 136 : (s + 1) * 136, :] = mine_ref[rows, :] + other_ref[rows, :]


def pair_sums(mine, other):
    def kernel(mine_ref, other_ref, a, b, c, d):
        pair_kernel(mine_ref, other_ref, (a, b), (c, d))

    return pl.pallas_call(
        kernel,
        in_specs=[VMEM, VMEM],
        out_specs=[VMEM] * 4,
        out_shape=[f32((4 * 136, 128))] * 4,
    )(mine, other)


def quad_kernel(a_ref, b_ref, a_other_ref, b_other_ref, *out_refs):
    for s in range(4):
        rows = pl.ds(s * 136, 136)
        out_refs[s][:136, :] = a_ref[rows, :] + a_other_ref[rows, :]
        out_refs[s][136:, :] = b_ref[rows, :] + b_other_ref[rows, :]


def quad_sums(*arrays):
    return pl.pallas_call(
        quad_kernel, in_specs=[VMEM] * 4, out_specs=[VMEM] * 4, out_shape=[f32((272, 128))] * 4
    )(*arrays)


def gather_kernel(*refs):
    *parts, own_ref, away_ref = refs
    total = parts[0][...]
    for part in parts[1:]:
        total += part[...]
    low = lax.axis_index("x_lo") == 0
    own_ref[...] = jnp.where(low, total[:136], total[136:])
    away_ref[...] = jnp.where(low, total[136:], total[:136])


def gathered(parts):
    return pl.pallas_call(
        gather_kernel,
        in_specs=[VMEM] * 4,
        out_specs=[VMEM] * 2,
        out_shape=[f32((136, 128))] * 2,
    )(*parts)


def nesterov(global_part, moment, average):
    outer = global_part - average
    moment_new = momentum_keep * moment + outer
    return (global_part - outer_rate * (outer + momentum_keep * moment_new), moment_new)


def finish(total, rows, global_ref, moment_ref, new_ref, moment_new_ref):
    count = total[2 * rows : 2 * rows + 1]
    for half in range(2):
        columns = pl.ds(half * 128, 128)
        new, moment_new = nesterov(
            global_ref[:, columns],
            moment_ref[:, columns],
            total[half * rows : (half + 1) * rows] / count,
        )
        new_ref[:, columns] = new
        moment_new_ref[:, columns] = moment_new


def first_finish_kernel(own_ref, other_ref, *refs):
    finish(own_ref[...] + other_ref[...], 64, *refs)


def second_finish_kernel(parts, global_ref, moment_ref, new_ref, moment_new_ref, parts_ref, arrived):
    copies = []
    for k in range(4):
        rows = pl.ds(k * 4 * 264, 4 * 264)
        copies.append(pltpu.make_async_copy(parts.at[rows], parts_ref.at[rows], arrived.at[k]))
        copies[-1].start()
    total = None
    for k in range(4):
        copies[k].wait()
        for r in range(4 * k, 4 * k + 4):
            part = parts_ref[r * 264 : (r + 1) * 264, :]
            total = part if total is None else total + part
    finish(total, 128, global_ref, moment_ref, new_ref, moment_new_ref)


def finish_call(kernel, specs, arrays, shape, scratch=()):
    return pl.pallas_call(
        kernel,
        in_specs=specs,
        out_specs=[VMEM, VMEM],
        out_shape=[f32(shape)] * 2,
        scratch_shapes=scratch,
    )(*arrays)


def per_device(
    counts,
    weights,
    hidden,
    queries,
    cotangent,
    first_global,
    first_moment,
    second_global,
    second_moment,
):
    second, keep, send = level_terms(
        counts, hidden[0, 0], weights[0, 0], queries[0, 0], cotangent[0, 0]
    )
    other = lax.ppermute(send, "core", [(0, 1), (1, 0)])
    second_parts = lax.all_to_all(second, ("x_hi", "y"), 0, 0, tiled=True)
    keep_a, keep_b, send_a, send_b = pair_sums(keep, other)
    pairs_a = [(i, i + 1 - 2 * (i % 2)) for i in range(8)]
    pairs_b = [(i, (i - 1 + 2 * (i % 2)) % 8) for i in range(8)]
    other_a = lax.ppermute(send_a, "z", pairs_a)
    other_b = lax.ppermute(send_b, "z", pairs_b)
    mine, *sums = quad_sums(keep_a, keep_b, other_a, other_b)
    arrivals = [
        lax.ppermute(sums[s - 1], "z", [(i, (i + 2 * s) % 8) for i in range(8)]) for s in (2, 1, 3)
    ]
    own, away = gathered([mine] + arrivals)
    across = lax.ppermute(away, "x_lo", [(0, 1), (1, 0)])
    first_new, first_moment_new = finish_call(
        first_finish_kernel,
        [VMEM] * 4,
        (own, across, first_global[0], first_moment[0]),
        (64, 256),
    )
    second_new, second_moment_new = finish_call(
        second_finish_kernel,
        [HBM, VMEM, VMEM],
        (second_parts, second_global[0], second_moment[0]),
        (128, 256),
        [pltpu.VMEM((16 * 264, 128), jnp.float32), pltpu.SemaphoreType.DMA((4,))],
    )
    return (first_new[None], first_moment_new[None], second_new[None], second_moment_new[None])


def solution(mesh):
    axes = ("x_hi", "y", "z", "x_lo", "core")
    fine = Mesh(mesh.devices.reshape(2, 8, 8, 2, 2), axes)
    row, col = axes[:2], axes[2:]
    return jax.shard_map(
        per_device,
        mesh=fine,
        in_specs=(
            P(row, col),
            P(row, col, None, None),
            P(row, col, None, None),
            P(row, col, None, None),
            P(row, col, None, None),
            P(row, col, None),
            P(row, col, None),
            P(col, row, None),
            P(col, row, None),
        ),
        out_specs=(
            P(row, col, None),
            P(row, col, None),
            P(col, row, None),
            P(col, row, None),
        ),
        check_vma=False,
    )
```

time: 96.1 us -> 86.6 us (0.901)
  starting transfers between devices: 17.1 us -> 41.8 us
  waiting for transfers between devices: 38.4 us -> 18.4 us
  between operations: 14.7 us -> 1.37 us
  Pallas kernels: 12.1 us -> 20.1 us
  local copies, waits for them, and re-layouts: 11.1 us -> 4.35 us
  other arithmetic: 1.18 us -> 0 us
    all_to_all x1, waiting for transfers between devices: 30.5 us -> 0.01 us  [per_device(): second_parts = lax.all_to_all(second, ('x_hi', 'y'), 0, 0, tiled=True)]
    ppermute x2 -> x7, starting transfers between devices: 5.23 us -> 31.7 us  [the longest x3 13.7 us: per_device(): lax.ppermute(sums[s - 1], 'z', [(i, (i + 2 * s) % 8) for i in range(8)])]
    ppermute x2 -> x7, waiting for transfers between devices: 7.95 us -> 18.4 us  [the longest x1 6.85 us: per_device(): other_b = lax.ppermute(send_b, 'z', pairs_b)]
    pallas_call x4 -> x6, Pallas kernels: 12.1 us -> 20.1 us  [the longest x1 8.64 us: level_terms(): pl.pallas_call(terms_kernel, in_specs=[SMEM] + [HBM] * 4, out_specs=[HBM]...]
    unnamed x20 -> x16, local copies, waits for them, and re-layouts: 10.2 us -> 4.35 us
    all_to_all x1, starting transfers between devices: 11.8 us -> 10.1 us  [per_device(): second_parts = lax.all_to_all(second, ('x_hi', 'y'), 0, 0, tiled=True)]
    add x1 -> x0, other arithmetic: 1.18 us -> none  [per_device(): pair_terms = keep + lax.ppermute(send, 'core', [(0, 1), (1, 0)])]
  transfers between devices with their start and end apart: 4 -> 8, of which waited for: 3 -> 6; matrix products, arithmetic and copies ran while one was open for 1% -> 0% of each run, Pallas kernels for 6% -> 10%
where the time goes in v2:
time: 86.6 us; the launch traced here: 86 us
  starting transfers between devices  41.8 us (48%)
  Pallas kernels  20.1 us (23%)
  waiting for transfers between devices  18.4 us (21%)
  local copies, waits for them, and re-layouts  4.35 us (5%)
  between operations  1.37 us (2%)
    ppermute x3, starting transfers between devices, per_device(): lax.ppermute(sums[s - 1], 'z', [(i, (i + 2 * s) % 8) for i in range(8)])  13.7 us
    all_to_all x1, starting transfers between devices, per_device(): second_parts = lax.all_to_all(second, ('x_hi', 'y'), 0, 0, tiled=True)  10.1 us
    ppermute x1, starting transfers between devices, per_device(): other_b = lax.ppermute(send_b, 'z', pairs_b)  9.1 us
    pallas_call x1, Pallas kernels, level_terms(): pl.pallas_call(terms_kernel, in_specs=[SMEM] + [HBM] * 4, out_specs=[HBM]...  8.64 us
    ppermute x1, waiting for transfers between devices, per_device(): other_b = lax.ppermute(send_b, 'z', pairs_b)  6.85 us
    ppermute x3, waiting for transfers between devices, per_device(): lax.ppermute(sums[s - 1], 'z', [(i, (i + 2 * s) % 8) for i in range(8)])  4.92 us
    pallas_call x2, Pallas kernels, finish_call(): pl.pallas_call(kernel, in_specs=specs, out_specs=[VMEM, VMEM], out_shape=...  4.91 us
    unnamed x16, local copies, waits for them, and re-layouts  4.35 us
  transfers between devices with their start and end apart: 8, of which 6 were waited for; matrix products, arithmetic and copies ran while one was open for 0% of the time, Pallas kernels for 10%

profile of v2, /device:TPU:6, one launch (start us, length us, event | category | flops | bytes accessed | tf_op | source)
XLA Modules:
  0.0 86.0 jit_solution(10862940750868686461)
XLA Ops:
  1.3 8.6 %shard_map.120 = (f32[4224,128]{1,0:T(8,128)}, f32[2176,128]{1,0:T(8,128)}, f32[2176,128]{1,0:T(8,128)}) custom-call(s32[1,1]{1,0:T(1,128)S(6)} %copy.13.counts_ref, bf16[256,2048]{1,0:T(8,128)(2,1)} %bitcast.21, bf16[2048,512]{1,0:T(8,128)(2,1)} %bitcast.20, bf16[256,1024]{1,0:T(8,128)(2,1)} %bitcast.22, bf16[256,1024]{1,0:T(8,128)(2,1)} %bitcast.23), custom_call_target="tpu_custom_call" | custom-call | flops 2000000000 | bytes 8388608 | tf_op jit(solution)/shard_map/pallas_call | solution.py:179
  9.9 10.1 %all-to-all-start = ((f32[16,264,128]{2,1,0:T(8,128)}), f32[16,264,128]{2,1,0:T(8,128)S(1)}, u32[]{:S(2)}, u32[]{:S(2)}) async-start(f32[16,264,128]{2,1,0:T(8,128)} %bitcast.15), calls=%async_computation | async-start | bytes 4325376 | tf_op jit(solution)/shard_map/all_to_all | solution.py:318
  20.0 1.9 %collective-permute-start = (f32[2176,128]{1,0:T(8,128)}, f32[2176,128]{1,0:T(8,128)S(1)}, u32[]{:S(2)}, u32[]{:S(2)}) collective-permute-start(f32[2176,128]{1,0:T(8,128)} %get-tuple-element.22), channel_id=1, source_target_pairs={{0,1},{1,0},{2,3},{3,2},{4,5},{5,4},{6,7},{7,6},{8,9},{9,8},{10,11... | collective-permute-start | bytes 3342344 | tf_op jit(solution)/shard_map/ppermute | solution.py:317
  21.9 2.9 %collective-permute-done.other_ref = f32[2176,128]{1,0:T(8,128)S(1)} collective-permute-done((f32[2176,128]{1,0:T(8,128)}, f32[2176,128]{1,0:T(8,128)S(1)}, u32[]{:S(2)}, u32[]{:S(2)}) %collective-permute-start) | collective-permute-done | bytes 1114144 | tf_op jit(solution)/shard_map/ppermute | solution.py:317
  24.9 1.0 %copy-done.1 = f32[2176,128]{1,0:T(8,128)} copy-done((f32[2176,128]{1,0:T(8,128)}, f32[2176,128]{1,0:T(8,128)S(1)}, u32[]{:S(2)}) %copy-start.1) | copy-done | bytes 1114136
  25.9 2.7 %shard_map.121 = (f32[544,128]{1,0:T(8,128)}, f32[544,128]{1,0:T(8,128)}, f32[544,128]{1,0:T(8,128)}, f32[544,128]{1,0:T(8,128)}) custom-call(f32[2176,128]{1,0:T(8,128)} %get-tuple-element.21.mine_ref, f32[2176,128]{1,0:T(8,128)} %copy-done.1), custom_call_target="tpu_custom_call" | custom-call | tf_op jit(solution)/shard_map/pallas_call | solution.py:215
  28.6 4.3 %collective-permute-start.1 = (f32[544,128]{1,0:T(8,128)}, f32[544,128]{1,0:T(8,128)S(1)}, u32[]{:S(2)}, u32[]{:S(2)}) collective-permute-start(f32[544,128]{1,0:T(8,128)} %get-tuple-element.25), channel_id=1, source_target_pairs={{0,4},{4,0},{8,12},{12,8},{16,20},{20,16},{24,28},{28,24},{1,5},{5... | collective-permute-start | bytes 835592 | tf_op jit(solution)/shard_map/ppermute | solution.py:322
  32.9 9.1 %collective-permute-start.2 = (f32[544,128]{1,0:T(8,128)}, f32[544,128]{1,0:T(8,128)S(1)}, u32[]{:S(2)}, u32[]{:S(2)}) collective-permute-start(f32[544,128]{1,0:T(8,128)} %get-tuple-element.26), channel_id=1, source_target_pairs={{0,28},{4,8},{8,4},{12,16},{16,12},{20,24},{24,20},{28,0},{1,29},{... | collective-permute-start | bytes 835592 | tf_op jit(solution)/shard_map/ppermute | solution.py:323
  42.0 6.9 %collective-permute-done.2.b_other_ref = f32[544,128]{1,0:T(8,128)S(1)} collective-permute-done((f32[544,128]{1,0:T(8,128)}, f32[544,128]{1,0:T(8,128)S(1)}, u32[]{:S(2)}, u32[]{:S(2)}) %collective-permute-start.2) | collective-permute-done | bytes 278560 | tf_op jit(solution)/shard_map/ppermute | solution.py:323
  48.9 0.7 copy-done.3
  49.6 2.1 %shard_map.122 = (f32[272,128]{1,0:T(8,128)}, f32[272,128]{1,0:T(8,128)}, f32[272,128]{1,0:T(8,128)}, f32[272,128]{1,0:T(8,128)}) custom-call(f32[544,128]{1,0:T(8,128)} %get-tuple-element.23.a_ref, f32[544,128]{1,0:T(8,128)} %get-tuple-element.24.b_ref, f32[544,128]{1,0:T(8,128)} %copy-done.2, f32[544,128]{1,0:T(8,128)} %copy-done.3), custom_call_target="tpu_custom_call" | custom-call | tf_op jit(solution)/shard_map/pallas_call | solution.py:231
  51.7 5.7 %collective-permute-start.3 = (f32[272,128]{1,0:T(8,128)}, f32[272,128]{1,0:T(8,128)S(1)}, u32[]{:S(2)}, u32[]{:S(2)}) collective-permute-start(f32[272,128]{1,0:T(8,128)} %get-tuple-element.28), channel_id=1, source_target_pairs={{0,16},{4,20},{8,24},{12,28},{16,0},{20,4},{24,8},{28,12},{1,17},{... | collective-permute-start | bytes 417800 | tf_op jit(solution)/shard_map/ppermute | solution.py:326
  57.4 3.1 %collective-permute-start.4 = (f32[272,128]{1,0:T(8,128)}, f32[272,128]{1,0:T(8,128)S(1)}, u32[]{:S(2)}, u32[]{:S(2)}) collective-permute-start(f32[272,128]{1,0:T(8,128)} %get-tuple-element.29), channel_id=1, source_target_pairs={{0,8},{4,12},{8,16},{12,20},{16,24},{20,28},{24,0},{28,4},{1,9},{5... | collective-permute-start | bytes 417800 | tf_op jit(solution)/shard_map/ppermute | solution.py:326
  60.5 4.9 %collective-permute-start.5 = (f32[272,128]{1,0:T(8,128)}, f32[272,128]{1,0:T(8,128)S(1)}, u32[]{:S(2)}, u32[]{:S(2)}) collective-permute-start(f32[272,128]{1,0:T(8,128)} %get-tuple-element.30), channel_id=1, source_target_pairs={{0,24},{4,28},{8,0},{12,4},{16,8},{20,12},{24,16},{28,20},{1,25},{... | collective-permute-start | bytes 417800 | tf_op jit(solution)/shard_map/ppermute | solution.py:326
  65.4 1.3 %collective-permute-done.3.refs_1_ = f32[272,128]{1,0:T(8,128)S(1)} collective-permute-done((f32[272,128]{1,0:T(8,128)}, f32[272,128]{1,0:T(8,128)S(1)}, u32[]{:S(2)}, u32[]{:S(2)}) %collective-permute-start.3) | collective-permute-done | bytes 139296 | tf_op jit(solution)/shard_map/ppermute | solution.py:326
  66.7 2.0 %collective-permute-done.4.refs_2_ = f32[272,128]{1,0:T(8,128)S(1)} collective-permute-done((f32[272,128]{1,0:T(8,128)}, f32[272,128]{1,0:T(8,128)S(1)}, u32[]{:S(2)}, u32[]{:S(2)}) %collective-permute-start.4) | collective-permute-done | bytes 139296 | tf_op jit(solution)/shard_map/ppermute | solution.py:326
  68.7 1.6 %collective-permute-done.5.refs_3_ = f32[272,128]{1,0:T(8,128)S(1)} collective-permute-done((f32[272,128]{1,0:T(8,128)}, f32[272,128]{1,0:T(8,128)S(1)}, u32[]{:S(2)}, u32[]{:S(2)}) %collective-permute-start.5) | collective-permute-done | bytes 139296 | tf_op jit(solution)/shard_map/ppermute | solution.py:326
  70.3 0.6 copy-done.6
  71.0 1.8 %shard_map.123 = (f32[136,128]{1,0:T(8,128)}, f32[136,128]{1,0:T(8,128)}) custom-call(f32[272,128]{1,0:T(8,128)} %get-tuple-element.27.refs_0_, f32[272,128]{1,0:T(8,128)} %copy-done.4, f32[272,128]{1,0:T(8,128)} %copy-done.5, f32[272,128]{1,0:T(8,128)} %copy-done.6), custom_call_target="tpu_custom_call" | custom-call | tf_op jit(solution)/shard_map/pallas_call | solution.py:247
  72.8 2.7 %collective-permute-start.6 = (f32[136,128]{1,0:T(8,128)}, f32[136,128]{1,0:T(8,128)S(1)}, u32[]{:S(2)}, u32[]{:S(2)}) collective-permute-start(f32[136,128]{1,0:T(8,128)} %get-tuple-element.32), channel_id=1, source_target_pairs={{0,2},{2,0},{1,3},{3,1},{4,6},{6,4},{5,7},{7,5},{8,10},{10,8},{9,1... | collective-permute-start | bytes 208904 | tf_op jit(solution)/shard_map/ppermute | solution.py:329
  75.5 3.7 %collective-permute-done.6.other_ref = f32[136,128]{1,0:T(8,128)S(1)} collective-permute-done((f32[136,128]{1,0:T(8,128)}, f32[136,128]{1,0:T(8,128)S(1)}, u32[]{:S(2)}, u32[]{:S(2)}) %collective-permute-start.6) | collective-permute-done | bytes 69664 | tf_op jit(solution)/shard_map/ppermute | solution.py:329
  79.8 1.6 %shard_map.124 = (f32[64,256]{1,0:T(8,128)}, f32[64,256]{1,0:T(8,128)}) custom-call(f32[136,128]{1,0:T(8,128)} %get-tuple-element.31.own_ref, f32[136,128]{1,0:T(8,128)} %copy-done.7, f32[64,256]{1,0:T(8,128)} %bitcast.18, f32[64,256]{1,0:T(8,128)} %bitcast.19), custom_call_target="tpu_custom_call" | custom-call | tf_op jit(solution)/shard_map/pallas_call | solution.py:294
  81.4 1.3 %copy-done = f32[16,264,128]{2,1,0:T(8,128)} copy-done((f32[16,264,128]{2,1,0:T(8,128)}, f32[16,264,128]{2,1,0:T(8,128)S(1)}, u32[]{:S(2)}) %copy-start) | copy-done | bytes 2162712
  82.8 3.3 %shard_map.125 = (f32[128,256]{1,0:T(8,128)}, f32[128,256]{1,0:T(8,128)}) custom-call(f32[4224,128]{1,0:T(8,128)} %bitcast.14, f32[128,256]{1,0:T(8,128)} %bitcast.16, f32[128,256]{1,0:T(8,128)} %bitcast.17), custom_call_target="tpu_custom_call" | custom-call | tf_op jit(solution)/shard_map/pallas_call | solution.py:294
  (14 shorter events, 0.7 us)
Async XLA Ops:
  9.9 71.5 %all-to-all-start = ((f32[16,264,128]{2,1,0:T(8,128)}), f32[16,264,128]{2,1,0:T(8,128)S(1)}, u32[]{:S(2)}, u32[]{:S(2)}) async-start(f32[16,264,128]{2,1,0:T(8,128)} %bitcast.15), calls=%async_computation | async-start | bytes 4325376 | tf_op jit(solution)/shard_map/all_to_all | solution.py:318
  20.0 4.8 %collective-permute-start = (f32[2176,128]{1,0:T(8,128)}, f32[2176,128]{1,0:T(8,128)S(1)}, u32[]{:S(2)}, u32[]{:S(2)}) collective-permute-start(f32[2176,128]{1,0:T(8,128)} %get-tuple-element.22), channel_id=1, source_target_pairs={{0,1},{1,0},{2,3},{3,2},{4,5},{5,4},{6,7},{7,6},{8,9},{9,8},{10,11... | collective-permute-start | bytes 3342344 | tf_op jit(solution)/shard_map/ppermute | solution.py:317
  24.9 1.0 %copy-start.1 = (f32[2176,128]{1,0:T(8,128)}, f32[2176,128]{1,0:T(8,128)S(1)}, u32[]{:S(2)}) copy-start(f32[2176,128]{1,0:T(8,128)S(1)} %collective-permute-done.other_ref) | copy-start | bytes 3342340
  28.6 13.4 %collective-permute-start.1 = (f32[544,128]{1,0:T(8,128)}, f32[544,128]{1,0:T(8,128)S(1)}, u32[]{:S(2)}, u32[]{:S(2)}) collective-permute-start(f32[544,128]{1,0:T(8,128)} %get-tuple-element.25), channel_id=1, source_target_pairs={{0,4},{4,0},{8,12},{12,8},{16,20},{20,16},{24,28},{28,24},{1,5},{5... | collective-permute-start | bytes 835592 | tf_op jit(solution)/shard_map/ppermute | solution.py:322
  32.9 16.0 %collective-permute-start.2 = (f32[544,128]{1,0:T(8,128)}, f32[544,128]{1,0:T(8,128)S(1)}, u32[]{:S(2)}, u32[]{:S(2)}) collective-permute-start(f32[544,128]{1,0:T(8,128)} %get-tuple-element.26), channel_id=1, source_target_pairs={{0,28},{4,8},{8,4},{12,16},{16,12},{20,24},{24,20},{28,0},{1,29},{... | collective-permute-start | bytes 835592 | tf_op jit(solution)/shard_map/ppermute | solution.py:323
  42.0 6.9 %copy-start.2 = (f32[544,128]{1,0:T(8,128)}, f32[544,128]{1,0:T(8,128)S(1)}, u32[]{:S(2)}) copy-start(f32[544,128]{1,0:T(8,128)S(1)} %collective-permute-done.1.a_other_ref) | copy-start | bytes 835588
  48.9 0.7 copy-start.3
  51.7 15.0 %collective-permute-start.3 = (f32[272,128]{1,0:T(8,128)}, f32[272,128]{1,0:T(8,128)S(1)}, u32[]{:S(2)}, u32[]{:S(2)}) collective-permute-start(f32[272,128]{1,0:T(8,128)} %get-tuple-element.28), channel_id=1, source_target_pairs={{0,16},{4,20},{8,24},{12,28},{16,0},{20,4},{24,8},{28,12},{1,17},{... | collective-permute-start | bytes 417800 | tf_op jit(solution)/shard_map/ppermute | solution.py:326
  57.4 11.3 %collective-permute-start.4 = (f32[272,128]{1,0:T(8,128)}, f32[272,128]{1,0:T(8,128)S(1)}, u32[]{:S(2)}, u32[]{:S(2)}) collective-permute-start(f32[272,128]{1,0:T(8,128)} %get-tuple-element.29), channel_id=1, source_target_pairs={{0,8},{4,12},{8,16},{12,20},{16,24},{20,28},{24,0},{28,4},{1,9},{5... | collective-permute-start | bytes 417800 | tf_op jit(solution)/shard_map/ppermute | solution.py:326
  60.5 9.8 %collective-permute-start.5 = (f32[272,128]{1,0:T(8,128)}, f32[272,128]{1,0:T(8,128)S(1)}, u32[]{:S(2)}, u32[]{:S(2)}) collective-permute-start(f32[272,128]{1,0:T(8,128)} %get-tuple-element.30), channel_id=1, source_target_pairs={{0,24},{4,28},{8,0},{12,4},{16,8},{20,12},{24,16},{28,20},{1,25},{... | collective-permute-start | bytes 417800 | tf_op jit(solution)/shard_map/ppermute | solution.py:326
  66.7 3.6 %copy-start.4 = (f32[272,128]{1,0:T(8,128)}, f32[272,128]{1,0:T(8,128)S(1)}, u32[]{:S(2)}) copy-start(f32[272,128]{1,0:T(8,128)S(1)} %collective-permute-done.3.refs_1_) | copy-start | bytes 417796
  68.7 1.6 %copy-start.5 = (f32[272,128]{1,0:T(8,128)}, f32[272,128]{1,0:T(8,128)S(1)}, u32[]{:S(2)}) copy-start(f32[272,128]{1,0:T(8,128)S(1)} %collective-permute-done.4.refs_2_) | copy-start | bytes 417796
  70.3 0.6 copy-start.6
  72.8 6.4 %collective-permute-start.6 = (f32[136,128]{1,0:T(8,128)}, f32[136,128]{1,0:T(8,128)S(1)}, u32[]{:S(2)}, u32[]{:S(2)}) collective-permute-start(f32[136,128]{1,0:T(8,128)} %get-tuple-element.32), channel_id=1, source_target_pairs={{0,2},{2,0},{1,3},{3,1},{4,6},{6,4},{5,7},{7,5},{8,10},{10,8},{9,1... | collective-permute-start | bytes 208904 | tf_op jit(solution)/shard_map/ppermute | solution.py:329
  79.2 0.6 copy-start.7
  81.4 1.3 %copy-start = (f32[16,264,128]{2,1,0:T(8,128)}, f32[16,264,128]{2,1,0:T(8,128)S(1)}, u32[]{:S(2)}) copy-start(f32[16,264,128]{2,1,0:T(8,128)S(1)} %all-to-all-done) | copy-start | bytes 6488068

commit v3 on v2

--- a/solution.py
+++ b/solution.py
@@ -78,16 +78,16 @@
 
 
 def terms_kernel(
-    counts_ref, hidden, weights, queries, cotangent, second, keep, send, *scratch
+    own_count, hidden, weights, queries, cotangent, second, keep, send, *scratch
 ):
     (hidden_ref, turned_ref, weights_ref, queries_ref, cotangent_ref) = scratch[:5]
-    second_ref, keep_ref, send_ref, arrived, left = scratch[5:]
+    second_ref, keep_ref, send_ref, counts_ref, arrived, left = scratch[5:]
     width = hidden.shape[1]
     part = width // PARTS
     level = weights.shape[1] // 2
     heads = queries.shape[1] // 2
 
-    copies = []
+    copies = [(own_count, counts_ref)]
     for k in range(PARTS):
         rows = pl.ds(k * part, part)
         copies.append((hidden.at[:, rows], hidden_ref.at[:, rows]))
@@ -98,6 +98,7 @@
     for copy in copies:
         copy.start()
 
+    copies[0].wait()
     count = counts_ref[0, 0].astype(jnp.float32)
     own = lax.axis_index("core") == 0
     factor = 1.0 / math.sqrt(width)
@@ -110,8 +111,8 @@
 
     projected = None
     for k in range(PARTS):
-        copies[2 * k].wait()
         copies[2 * k + 1].wait()
+        copies[2 * k + 2].wait()
         rows = pl.ds(k * part, part)
         product = nn(hidden_ref[:, rows], weights_ref[rows, :])
         projected = product if projected is None else projected + product
@@ -167,9 +168,9 @@
         copy.wait()
 
 
-SMEM = pl.BlockSpec(memory_space=pltpu.SMEM)
 VMEM = pl.BlockSpec(memory_space=pltpu.VMEM)
 HBM = pl.BlockSpec(memory_space=pltpu.HBM)
+SMALL = pltpu.CompilerParams(vmem_limit_bytes=16 * 1024 * 1024)
 f32 = functools.partial(jax.ShapeDtypeStruct, dtype=jnp.float32)
 
 
@@ -178,7 +179,7 @@
     shapes = [f32((16 * 264, 128)), f32((16 * 136, 128)), f32((16 * 136, 128))]
     return pl.pallas_call(
         terms_kernel,
-        in_specs=[SMEM] + [HBM] * 4,
+        in_specs=[HBM] * 5,
         out_specs=[HBM] * 3,
         out_shape=shapes,
         scratch_shapes=[
@@ -189,7 +190,11 @@
             pltpu.VMEM(cotangent.shape, jnp.bfloat16),
         ]
         + [pltpu.VMEM(s.shape, jnp.float32) for s in shapes]
-        + [pltpu.SemaphoreType.DMA((2 * PARTS + 2,)), pltpu.SemaphoreType.DMA((12,))],
+        + [
+            pltpu.SMEM((1, 1), jnp.int32),
+            pltpu.SemaphoreType.DMA((2 * PARTS + 3,)),
+            pltpu.SemaphoreType.DMA((12,)),
+        ],
         compiler_params=pltpu.CompilerParams(vmem_limit_bytes=62 * 1024 * 1024),
         cost_estimate=pl.CostEstimate(
             flops=2 * 10**9, bytes_accessed=8 * 2**20, transcendentals=2**20
@@ -217,6 +222,7 @@
         in_specs=[VMEM, VMEM],
         out_specs=[VMEM] * 4,
         out_shape=[f32((4 * 136, 128))] * 4,
+        compiler_params=SMALL,
     )(mine, other)
 
 
@@ -229,7 +235,11 @@
 
 def quad_sums(*arrays):
     return pl.pallas_call(
-        quad_kernel, in_specs=[VMEM] * 4, out_specs=[VMEM] * 4, out_shape=[f32((272, 128))] * 4
+        quad_kernel,
+        in_specs=[VMEM] * 4,
+        out_specs=[VMEM] * 4,
+        out_shape=[f32((272, 128))] * 4,
+        compiler_params=SMALL,
     )(*arrays)
 
 
@@ -249,6 +259,7 @@
         in_specs=[VMEM] * 4,
         out_specs=[VMEM] * 2,
         out_shape=[f32((136, 128))] * 2,
+        compiler_params=SMALL,
     )(*parts)
 
 
@@ -271,32 +282,25 @@
         moment_new_ref[:, columns] = moment_new
 
 
-def first_finish_kernel(own_ref, other_ref, *refs):
-    finish(own_ref[...] + other_ref[...], 64, *refs)
-
-
-def second_finish_kernel(parts, global_ref, moment_ref, new_ref, moment_new_ref, parts_ref, arrived):
-    copies = []
-    for k in range(4):
-        rows = pl.ds(k * 4 * 264, 4 * 264)
-        copies.append(pltpu.make_async_copy(parts.at[rows], parts_ref.at[rows], arrived.at[k]))
-        copies[-1].start()
-    total = None
-    for k in range(4):
-        copies[k].wait()
-        for r in range(4 * k, 4 * k + 4):
-            part = parts_ref[r * 264 : (r + 1) * 264, :]
-            total = part if total is None else total + part
+def first_finish_kernel(own_ref, other_ref, global_ref, moment_ref, ahead, *out_refs):
+    finish(own_ref[...] + other_ref[...], 64, global_ref, moment_ref, *out_refs)
+
+
+def second_finish_kernel(parts_ref, global_ref, moment_ref, new_ref, moment_new_ref, done_ref):
+    total = parts_ref[0:264, :]
+    for r in range(1, 16):
+        total += parts_ref[r * 264 : (r + 1) * 264, :]
     finish(total, 128, global_ref, moment_ref, new_ref, moment_new_ref)
-
-
-def finish_call(kernel, specs, arrays, shape, scratch=()):
+    done_ref[...] = total[256:264]
+
+
+def finish_call(kernel, arrays, shapes):
     return pl.pallas_call(
         kernel,
-        in_specs=specs,
-        out_specs=[VMEM, VMEM],
-        out_shape=[f32(shape)] * 2,
-        scratch_shapes=scratch,
+        in_specs=[VMEM] * len(arrays),
+        out_specs=[VMEM] * len(shapes),
+        out_shape=[f32(s) for s in shapes],
+        compiler_params=SMALL,
     )(*arrays)
 
 
@@ -327,18 +331,15 @@
     ]
     own, away = gathered([mine] + arrivals)
     across = lax.ppermute(away, "x_lo", [(0, 1), (1, 0)])
+    second_new, second_moment_new, done = finish_call(
+        second_finish_kernel,
+        (second_parts, second_global[0], second_moment[0]),
+        [(128, 256), (128, 256), (8, 128)],
+    )
     first_new, first_moment_new = finish_call(
         first_finish_kernel,
-        [VMEM] * 4,
-        (own, across, first_global[0], first_moment[0]),
-        (64, 256),
-    )
-    second_new, second_moment_new = finish_call(
-        second_finish_kernel,
-        [HBM, VMEM, VMEM],
-        (second_parts, second_global[0], second_moment[0]),
-        (128, 256),
-        [pltpu.VMEM((16 * 264, 128), jnp.float32), pltpu.SemaphoreType.DMA((4,))],
+        (own, across, first_global[0], first_moment[0], done),
+        [(64, 256), (64, 256)],
     )
     return (first_new[None], first_moment_new[None], second_new[None], second_moment_new[None])
 

time: 86.6 us -> 73.9 us (0.85)
  the two profiles are of different devices: /device:TPU:6 before, /device:TPU:72 now
where the time goes in v3:
time: 73.9 us; the launch traced here: 73.5 us
  starting transfers between devices  39.6 us (54%)
  waiting for transfers between devices  22.1 us (30%)
  Pallas kernels  10.4 us (14%)
  between operations  1.41 us (2%)
    ppermute x3, starting transfers between devices, per_device(): lax.ppermute(sums[s - 1], 'z', [(i, (i + 2 * s) % 8) for i in range(8)])  16.2 us
    all_to_all x1, starting transfers between devices, per_device(): second_parts = lax.all_to_all(second, ('x_hi', 'y'), 0, 0, tiled=True)  10.2 us
    pallas_call x1, Pallas kernels, level_terms(): pl.pallas_call(terms_kernel, in_specs=[HBM] * 5, out_specs=[HBM] * 3, out...  8.65 us
    ppermute x1, starting transfers between devices, per_device(): other_b = lax.ppermute(send_b, 'z', pairs_b)  6.63 us
    all_to_all x1, waiting for transfers between devices, per_device(): second_parts = lax.all_to_all(second, ('x_hi', 'y'), 0, 0, tiled=True)  6.25 us
    ppermute x3, waiting for transfers between devices, per_device(): lax.ppermute(sums[s - 1], 'z', [(i, (i + 2 * s) % 8) for i in range(8)])  6.24 us
    ppermute x1, waiting for transfers between devices, per_device(): other_b = lax.ppermute(send_b, 'z', pairs_b)  4.64 us
    ppermute x1, waiting for transfers between devices, per_device(): other = lax.ppermute(send, 'core', [(0, 1), (1, 0)])  2.93 us
  transfers between devices with their start and end apart: 8, of which 6 were waited for; matrix products, arithmetic and copies ran while one was open for 0% of the time, Pallas kernels for 1%

profile of v3, /device:TPU:72, one launch (start us, length us, event | category | flops | bytes accessed | tf_op | source)
XLA Modules:
  0.0 73.5 jit_solution(6184495773088324366)
XLA Ops:
  1.3 8.7 %shard_map.120 = (f32[4224,128]{1,0:T(8,128)}, f32[2176,128]{1,0:T(8,128)}, f32[2176,128]{1,0:T(8,128)}) custom-call(s32[1,1]{1,0:T(1,128)S(6)} %copy.13.own_count, bf16[256,2048]{1,0:T(8,128)(2,1)} %bitcast.21, bf16[2048,512]{1,0:T(8,128)(2,1)} %bitcast.20, bf16[256,1024]{1,0:T(8,128)(2,1)} %bitcast.22, bf16[256,1024]{1,0:T(8,128)(2,1)} %bitcast.23), custom_call_target="tpu_custom_call" | custom-call | flops 2000000000 | bytes 8388608 | tf_op jit(solution)/shard_map/pallas_call | solution.py:180
  9.9 10.2 %all-to-all-start = ((f32[16,264,128]{2,1,0:T(8,128)}), f32[16,264,128]{2,1,0:T(8,128)S(1)}, u32[]{:S(2)}, u32[]{:S(2)}) async-start(f32[16,264,128]{2,1,0:T(8,128)} %bitcast.19), calls=%async_computation | async-start | bytes 4325376 | tf_op jit(solution)/shard_map/all_to_all | solution.py:322
  20.1 0.0 copy-start.2
  20.1 2.1 %collective-permute-start = (f32[2176,128]{1,0:T(8,128)}, f32[2176,128]{1,0:T(8,128)S(1)}, u32[]{:S(2)}, u32[]{:S(2)}) collective-permute-start(f32[2176,128]{1,0:T(8,128)} %get-tuple-element.23), channel_id=1, source_target_pairs={{0,1},{1,0},{2,3},{3,2},{4,5},{5,4},{6,7},{7,6},{8,9},{9,8},{10,11... | collective-permute-start | bytes 3342344 | tf_op jit(solution)/shard_map/ppermute | solution.py:321
  22.2 2.9 %collective-permute-done.other_ref = f32[2176,128]{1,0:T(8,128)S(1)} collective-permute-done((f32[2176,128]{1,0:T(8,128)}, f32[2176,128]{1,0:T(8,128)S(1)}, u32[]{:S(2)}, u32[]{:S(2)}) %collective-permute-start) | collective-permute-done | bytes 1114144 | tf_op jit(solution)/shard_map/ppermute | solution.py:321
  25.1 0.1 shard_map.121
  25.2 0.0 copy-start.3
  25.3 0.0 copy-start.4
  25.3 2.1 %collective-permute-start.1 = (f32[544,128]{1,0:T(8,128)S(1)}, f32[544,128]{1,0:T(8,128)S(1)}, u32[]{:S(2)}, u32[]{:S(2)}) collective-permute-start(f32[544,128]{1,0:T(8,128)S(1)} %get-tuple-element.26), channel_id=1, source_target_pairs={{0,4},{4,0},{8,12},{12,8},{16,20},{20,16},{24,28},{28,24},{1,5},{5... | collective-permute-start | bytes 835592 | tf_op jit(solution)/shard_map/ppermute | solution.py:326
  27.3 6.6 %collective-permute-start.2 = (f32[544,128]{1,0:T(8,128)S(1)}, f32[544,128]{1,0:T(8,128)S(1)}, u32[]{:S(2)}, u32[]{:S(2)}) collective-permute-start(f32[544,128]{1,0:T(8,128)S(1)} %get-tuple-element.27), channel_id=1, source_target_pairs={{0,28},{4,8},{8,4},{12,16},{16,12},{20,24},{24,20},{28,0},{1,29},{... | collective-permute-start | bytes 835592 | tf_op jit(solution)/shard_map/ppermute | solution.py:327
  34.0 2.0 %collective-permute-done.1.a_other_ref = f32[544,128]{1,0:T(8,128)S(1)} collective-permute-done((f32[544,128]{1,0:T(8,128)S(1)}, f32[544,128]{1,0:T(8,128)S(1)}, u32[]{:S(2)}, u32[]{:S(2)}) %collective-permute-start.1) | collective-permute-done | bytes 278560 | tf_op jit(solution)/shard_map/ppermute | solution.py:326
  36.0 4.6 %collective-permute-done.2.b_other_ref = f32[544,128]{1,0:T(8,128)S(1)} collective-permute-done((f32[544,128]{1,0:T(8,128)S(1)}, f32[544,128]{1,0:T(8,128)S(1)}, u32[]{:S(2)}, u32[]{:S(2)}) %collective-permute-start.2) | collective-permute-done | bytes 278560 | tf_op jit(solution)/shard_map/ppermute | solution.py:327
  40.6 0.1 shard_map.122
  40.7 8.2 %collective-permute-start.3 = (f32[272,128]{1,0:T(8,128)S(1)}, f32[272,128]{1,0:T(8,128)S(1)}, u32[]{:S(2)}, u32[]{:S(2)}) collective-permute-start(f32[272,128]{1,0:T(8,128)S(1)} %get-tuple-element.29), channel_id=1, source_target_pairs={{0,16},{4,20},{8,24},{12,28},{16,0},{20,4},{24,8},{28,12},{1,17},{... | collective-permute-start | bytes 417800 | tf_op jit(solution)/shard_map/ppermute | solution.py:330
  48.9 4.8 %collective-permute-start.4 = (f32[272,128]{1,0:T(8,128)S(1)}, f32[272,128]{1,0:T(8,128)S(1)}, u32[]{:S(2)}, u32[]{:S(2)}) collective-permute-start(f32[272,128]{1,0:T(8,128)S(1)} %get-tuple-element.30), channel_id=1, source_target_pairs={{0,8},{4,12},{8,16},{12,20},{16,24},{20,28},{24,0},{28,4},{1,9},{5... | collective-permute-start | bytes 417800 | tf_op jit(solution)/shard_map/ppermute | solution.py:330
  53.8 3.1 %collective-permute-start.5 = (f32[272,128]{1,0:T(8,128)S(1)}, f32[272,128]{1,0:T(8,128)S(1)}, u32[]{:S(2)}, u32[]{:S(2)}) collective-permute-start(f32[272,128]{1,0:T(8,128)S(1)} %get-tuple-element.31), channel_id=1, source_target_pairs={{0,24},{4,28},{8,0},{12,4},{16,8},{20,12},{24,16},{28,20},{1,25},{... | collective-permute-start | bytes 417800 | tf_op jit(solution)/shard_map/ppermute | solution.py:330
  56.9 0.0 collective-permute-done.3.refs_1_
  56.9 4.9 %collective-permute-done.4.refs_2_ = f32[272,128]{1,0:T(8,128)S(1)} collective-permute-done((f32[272,128]{1,0:T(8,128)S(1)}, f32[272,128]{1,0:T(8,128)S(1)}, u32[]{:S(2)}, u32[]{:S(2)}) %collective-permute-start.4) | collective-permute-done | bytes 139296 | tf_op jit(solution)/shard_map/ppermute | solution.py:330
  61.8 1.3 %collective-permute-done.5.refs_3_ = f32[272,128]{1,0:T(8,128)S(1)} collective-permute-done((f32[272,128]{1,0:T(8,128)S(1)}, f32[272,128]{1,0:T(8,128)S(1)}, u32[]{:S(2)}, u32[]{:S(2)}) %collective-permute-start.5) | collective-permute-done | bytes 139296 | tf_op jit(solution)/shard_map/ppermute | solution.py:330
  63.2 2.5 %collective-permute-start.6 = (f32[136,128]{1,0:T(8,128)S(1)}, f32[136,128]{1,0:T(8,128)S(1)}, u32[]{:S(2)}, u32[]{:S(2)}) collective-permute-start(f32[136,128]{1,0:T(8,128)S(1)} %get-tuple-element.33), channel_id=1, source_target_pairs={{0,2},{2,0},{1,3},{3,1},{4,6},{6,4},{5,7},{7,5},{8,10},{10,8},{9,1... | collective-permute-start | bytes 208904 | tf_op jit(solution)/shard_map/ppermute | solution.py:333
  65.7 6.3 %all-to-all-done = f32[16,264,128]{2,1,0:T(8,128)S(1)} async-done(((f32[16,264,128]{2,1,0:T(8,128)}), f32[16,264,128]{2,1,0:T(8,128)S(1)}, u32[]{:S(2)}, u32[]{:S(2)}) %all-to-all-start) | async-done | bytes 2162720 | tf_op jit(solution)/shard_map/all_to_all | solution.py:322
  71.9 0.8 %shard_map.124 = (f32[128,256]{1,0:T(8,128)}, f32[128,256]{1,0:T(8,128)}, f32[8,128]{1,0:T(8,128)S(1)}) custom-call(f32[4224,128]{1,0:T(8,128)S(1)} %bitcast.14, f32[128,256]{1,0:T(8,128)S(1)} %bitcast.15, f32[128,256]{1,0:T(8,128)S(1)} %bitcast.16), custom_call_target="tpu_custom_call" | custom-call | tf_op jit(solution)/shard_map/pallas_call | solution.py:298
  72.8 0.0 collective-permute-done.6.other_ref
  72.8 0.7 shard_map.125
  (8 shorter events, 0.1 us)
Async XLA Ops:
  9.9 15.2 %copy-start = (f32[2176,128]{1,0:T(8,128)S(1)}, f32[2176,128]{1,0:T(8,128)}, u32[]{:S(2)}) copy-start(f32[2176,128]{1,0:T(8,128)} %get-tuple-element.22.mine_ref) | copy-start | bytes 3342340
  9.9 62.0 %all-to-all-start = ((f32[16,264,128]{2,1,0:T(8,128)}), f32[16,264,128]{2,1,0:T(8,128)S(1)}, u32[]{:S(2)}, u32[]{:S(2)}) async-start(f32[16,264,128]{2,1,0:T(8,128)} %bitcast.19), calls=%async_computation | async-start | bytes 4325376 | tf_op jit(solution)/shard_map/all_to_all | solution.py:322
  20.1 51.8 %copy-start.1 = (f32[1,128,256]{2,1,0:T(8,128)S(1)}, f32[1,128,256]{2,1,0:T(8,128)}, u32[]{:S(2)}) copy-start(f32[1,128,256]{2,1,0:T(8,128)} %param.16) | copy-start | bytes 393220
  20.1 51.8 %copy-start.2 = (f32[1,128,256]{2,1,0:T(8,128)S(1)}, f32[1,128,256]{2,1,0:T(8,128)}, u32[]{:S(2)}) copy-start(f32[1,128,256]{2,1,0:T(8,128)} %param.17) | copy-start | bytes 393220
  20.1 5.0 %collective-permute-start = (f32[2176,128]{1,0:T(8,128)}, f32[2176,128]{1,0:T(8,128)S(1)}, u32[]{:S(2)}, u32[]{:S(2)}) collective-permute-start(f32[2176,128]{1,0:T(8,128)} %get-tuple-element.23), channel_id=1, source_target_pairs={{0,1},{1,0},{2,3},{3,2},{4,5},{5,4},{6,7},{7,6},{8,9},{9,8},{10,11... | collective-permute-start | bytes 3342344 | tf_op jit(solution)/shard_map/ppermute | solution.py:321
  25.2 47.5 %copy-start.3 = (f32[1,64,256]{2,1,0:T(8,128)S(1)}, f32[1,64,256]{2,1,0:T(8,128)}, u32[]{:S(2)}) copy-start(f32[1,64,256]{2,1,0:T(8,128)} %param.14) | copy-start | bytes 196612
  25.3 47.5 %copy-start.4 = (f32[1,64,256]{2,1,0:T(8,128)S(1)}, f32[1,64,256]{2,1,0:T(8,128)}, u32[]{:S(2)}) copy-start(f32[1,64,256]{2,1,0:T(8,128)} %param.15) | copy-start | bytes 196612
  25.3 10.7 %collective-permute-start.1 = (f32[544,128]{1,0:T(8,128)S(1)}, f32[544,128]{1,0:T(8,128)S(1)}, u32[]{:S(2)}, u32[]{:S(2)}) collective-permute-start(f32[544,128]{1,0:T(8,128)S(1)} %get-tuple-element.26), channel_id=1, source_target_pairs={{0,4},{4,0},{8,12},{12,8},{16,20},{20,16},{24,28},{28,24},{1,5},{5... | collective-permute-start | bytes 835592 | tf_op jit(solution)/shard_map/ppermute | solution.py:326
  27.3 13.3 %collective-permute-start.2 = (f32[544,128]{1,0:T(8,128)S(1)}, f32[544,128]{1,0:T(8,128)S(1)}, u32[]{:S(2)}, u32[]{:S(2)}) collective-permute-start(f32[544,128]{1,0:T(8,128)S(1)} %get-tuple-element.27), channel_id=1, source_target_pairs={{0,28},{4,8},{8,4},{12,16},{16,12},{20,24},{24,20},{28,0},{1,29},{... | collective-permute-start | bytes 835592 | tf_op jit(solution)/shard_map/ppermute | solution.py:327
  40.7 16.2 %collective-permute-start.3 = (f32[272,128]{1,0:T(8,128)S(1)}, f32[272,128]{1,0:T(8,128)S(1)}, u32[]{:S(2)}, u32[]{:S(2)}) collective-permute-start(f32[272,128]{1,0:T(8,128)S(1)} %get-tuple-element.29), channel_id=1, source_target_pairs={{0,16},{4,20},{8,24},{12,28},{16,0},{20,4},{24,8},{28,12},{1,17},{... | collective-permute-start | bytes 417800 | tf_op jit(solution)/shard_map/ppermute | solution.py:330
  48.9 12.9 %collective-permute-start.4 = (f32[272,128]{1,0:T(8,128)S(1)}, f32[272,128]{1,0:T(8,128)S(1)}, u32[]{:S(2)}, u32[]{:S(2)}) collective-permute-start(f32[272,128]{1,0:T(8,128)S(1)} %get-tuple-element.30), channel_id=1, source_target_pairs={{0,8},{4,12},{8,16},{12,20},{16,24},{20,28},{24,0},{28,4},{1,9},{5... | collective-permute-start | bytes 417800 | tf_op jit(solution)/shard_map/ppermute | solution.py:330
  53.8 9.4 %collective-permute-start.5 = (f32[272,128]{1,0:T(8,128)S(1)}, f32[272,128]{1,0:T(8,128)S(1)}, u32[]{:S(2)}, u32[]{:S(2)}) collective-permute-start(f32[272,128]{1,0:T(8,128)S(1)} %get-tuple-element.31), channel_id=1, source_target_pairs={{0,24},{4,28},{8,0},{12,4},{16,8},{20,12},{24,16},{28,20},{1,25},{... | collective-permute-start | bytes 417800 | tf_op jit(solution)/shard_map/ppermute | solution.py:330
  63.2 9.6 %collective-permute-start.6 = (f32[136,128]{1,0:T(8,128)S(1)}, f32[136,128]{1,0:T(8,128)S(1)}, u32[]{:S(2)}, u32[]{:S(2)}) collective-permute-start(f32[136,128]{1,0:T(8,128)S(1)} %get-tuple-element.33), channel_id=1, source_target_pairs={{0,2},{2,0},{1,3},{3,1},{4,6},{6,4},{5,7},{7,5},{8,10},{10,8},{9,1... | collective-permute-start | bytes 208904 | tf_op jit(solution)/shard_map/ppermute | solution.py:333

commit v4 on v3

--- a/solution.py
+++ b/solution.py
@@ -11,6 +11,7 @@
 
 HEAD = 64
 PARTS = 4
+AHEAD = 1
 LOG2E = math.log2(math.e)
 
 inner_rate = 0.3
@@ -30,64 +31,111 @@
     return jnp.dot(a, b, preferred_element_type=jnp.float32)
 
 
-def level_dkeyval(projected, queries_ref, cotangent_ref):
+def placed(pair, low):
+    half = pair.shape[0] // 2
+    turned = pltpu.roll(pair, HEAD, 1)
+    zero = jnp.zeros_like(pair)
+    out = []
+    for even, odd in ((pair, turned), (turned, pair)):
+        even = jnp.where(low, even, zero).astype(jnp.bfloat16)
+        odd = jnp.where(low, zero, odd).astype(jnp.bfloat16)
+        out.append([jnp.concatenate([x[r : r + half] for x in (even, odd)]) for r in (0, half)])
+    return out
+
+
+def over(function, *arrays):
+    return [function(x, axis=0, keepdims=True) for x in arrays]
+
+
+def scored(keys, values, q, do):
+    half = q.shape[0] // 2
+    return nt(keys[0], q), nt(keys[1], q[half:]), nt(values[0], do), nt(values[1], do[half:])
+
+
+def softened(early, late, dearly, dlate, causal):
+    half = causal.shape[0]
+    probs, dscores = [], []
+    for head in range(2):
+        rows = slice(head * half, (head + 1) * half)
+        s = [early[rows, :half], early[rows, half:], late[rows]]
+        dp = [dearly[rows, :half], dearly[rows, half:], dlate[rows]]
+        s[0] = jnp.where(causal, s[0], -1e30)
+        s[2] = jnp.where(causal, s[2], -1e30)
+        tops = over(jnp.max, *s)
+        tops[1] = tops[2] = jnp.maximum(tops[1], tops[2])
+        e = [jnp.exp2((x - t) * (LOG2E / math.sqrt(HEAD))) for x, t in zip(s, tops)]
+        sums = over(jnp.sum, *e)
+        ratios = [1.0 / sums[0], 1.0 / (sums[1] + sums[2])]
+        p = [x * ratios[i] for x, i in zip(e, (0, 1, 1))]
+        deltas = over(jnp.sum, *[x * y for x, y in zip(p, dp)])
+        deltas[1] = deltas[2] = deltas[1] + deltas[2]
+        ds = [x * (y - d) for x, y, d in zip(p, dp, deltas)]
+        probs.append([x.astype(jnp.bfloat16) for x in p])
+        dscores.append([x.astype(jnp.bfloat16) for x in ds])
+    return probs, dscores
+
+
+def back(blocks, other, low):
+    half = other.shape[0] // 2
+    top = jnp.concatenate([jnp.concatenate(b[:2], axis=1) for b in blocks])
+    bottom = jnp.concatenate([b[2] for b in blocks])
+    top, bottom = nn(top, other), nn(bottom, other[half:])
+    even = jnp.concatenate([top[:half], bottom[:half]])
+    odd = jnp.concatenate([top[half:], bottom[half:]])
+    return jnp.where(low, even, odd)
+
+
+def level_dkeyvals(projected, queries_ref, cotangent_ref, levels, ready):
     length = projected.shape[0]
+    half = length // 2
     rounded = projected.astype(jnp.bfloat16).astype(jnp.float32)
     low = lax.broadcasted_iota(jnp.int32, (length, 128), 1) < HEAD
-    key_place = lax.broadcasted_iota(jnp.int32, (length, length), 0)
-    query_place = lax.broadcasted_iota(jnp.int32, (length, length), 1)
+    key_place = lax.broadcasted_iota(jnp.int32, (half, half), 0)
+    query_place = lax.broadcasted_iota(jnp.int32, (half, half), 1)
     causal = key_place <= query_place
-
-    def placed(pair):
-        turned = pltpu.roll(pair, HEAD, 1)
-        zero = jnp.zeros_like(pair)
-        out = []
-        for even, odd in ((pair, turned), (turned, pair)):
-            both = jnp.concatenate([jnp.where(low, even, zero), jnp.where(low, zero, odd)], axis=0)
-            out.append(both.astype(jnp.bfloat16))
-        return out
-
-    keys = placed(rounded[:, :128])
-    values = placed(rounded[:, 128:])
-    dkeys, dvalues = [], []
-    for group in range(2):
-        dk = jnp.zeros((length, 128), jnp.float32)
-        dv = jnp.zeros((length, 128), jnp.float32)
-        for pair in (2 * group, 2 * group + 1):
-            q = queries_ref[:, pair * 128 : (pair + 1) * 128]
-            do = cotangent_ref[:, pair * 128 : (pair + 1) * 128]
-            scores = nt(keys[group], q)
-            dprobs = nt(values[group], do)
-            heads = []
-            for head in range(2):
-                s = jnp.where(causal, scores[head * length : (head + 1) * length], -1e30)
-                dp = dprobs[head * length : (head + 1) * length]
-                top = jnp.max(s, axis=0, keepdims=True)
-                e = jnp.exp2((s - top) * (LOG2E / math.sqrt(HEAD)))
-                p = e * (1.0 / jnp.sum(e, axis=0, keepdims=True))
-                delta = jnp.sum(p * dp, axis=0, keepdims=True)
-                ds = p * (dp - delta)
-                heads.append((nn(ds.astype(jnp.bfloat16), q), nn(p.astype(jnp.bfloat16), do)))
-            dk += jnp.where(low, heads[0][0], heads[1][0])
-            dv += jnp.where(low, heads[0][1], heads[1][1])
-        dkeys.append(dk + pltpu.roll(dk, HEAD, 1))
-        dvalues.append(dv + pltpu.roll(dv, HEAD, 1))
-    dkey = jnp.where(low, dkeys[0], dkeys[1]) * (1.0 / math.sqrt(HEAD))
-    dvalue = jnp.where(low, dvalues[0], dvalues[1])
-    return jnp.concatenate([dkey, dvalue], axis=1).astype(jnp.bfloat16)
-
-
-def terms_kernel(
-    own_count, hidden, weights, queries, cotangent, second, keep, send, *scratch
-):
-    (hidden_ref, turned_ref, weights_ref, queries_ref, cotangent_ref) = scratch[:5]
-    second_ref, keep_ref, send_ref, counts_ref, arrived, left = scratch[5:]
+    laid = {}
+    for level in levels:
+        base = level * 256
+        laid[level] = (
+            placed(rounded[:, base : base + 128], low),
+            placed(rounded[:, base + 128 : base + 256], low),
+        )
+
+    def operands(level, pair):
+        columns = slice((level * 4 + pair) * 128, (level * 4 + pair + 1) * 128)
+        return queries_ref[:, columns], cotangent_ref[:, columns]
+
+    def start(level, pair):
+        keys, values = laid[level]
+        return scored(keys[pair // 2], values[pair // 2], *operands(level, pair))
+
+    steps = [(level, pair) for level in levels for pair in range(4)]
+    ahead = [start(*step) for step in steps[:AHEAD]]
+    gathered = {}
+    for number, (level, pair) in enumerate(steps):
+        if number + AHEAD < len(steps):
+            ahead.append(start(*steps[number + AHEAD]))
+        probs, dscores = softened(*ahead.pop(0), causal)
+        q, do = operands(level, pair)
+        gathered[level, pair] = back(dscores, q, low), back(probs, do, low)
+        if pair == 3:
+            out = []
+            for kind in range(2):
+                groups = [gathered[level, g][kind] + gathered[level, g + 1][kind] for g in (0, 2)]
+                groups = [g + pltpu.roll(g, HEAD, 1) for g in groups]
+                out.append(jnp.where(low, groups[0], groups[1]))
+            dkey = out[0] * (1.0 / math.sqrt(HEAD))
+            ready(level, jnp.concatenate([dkey, out[1]], axis=1).astype(jnp.bfloat16))
+
+
+def terms_kernel(counts_ref, hidden, weights, queries, cotangent, second, keep, send, *scratch):
+    hidden_ref, turned_ref, weights_ref, queries_ref, cotangent_ref = scratch[:5]
+    second_ref, first_ref, arrived, left = scratch[5:]
     width = hidden.shape[1]
     part = width // PARTS
-    level = weights.shape[1] // 2
-    heads = queries.shape[1] // 2
-
-    copies = [(own_count, counts_ref)]
+    level_columns = weights.shape[1] // 2
+
+    copies = []
     for k in range(PARTS):
         rows = pl.ds(k * part, part)
         copies.append((hidden.at[:, rows], hidden_ref.at[:, rows]))
@@ -98,76 +146,63 @@
     for copy in copies:
         copy.start()
 
-    copies[0].wait()
     count = counts_ref[0, 0].astype(jnp.float32)
-    own = lax.axis_index("core") == 0
+    own = lax.axis_index("core")
     factor = 1.0 / math.sqrt(width)
     scale = count * (inner_rate * factor)
     counts = jnp.full((8, 128), count, jnp.float32)
     for r in range(16):
         second_ref[r * 264 + 256 : r * 264 + 264, :] = counts
-        keep_ref[r * 136 + 128 : r * 136 + 136, :] = counts
-        send_ref[r * 136 + 128 : r * 136 + 136, :] = counts
+        for core in range(2):
+            first_ref[core, r * 136 + 128 : r * 136 + 136, :] = counts
 
     projected = None
     for k in range(PARTS):
+        copies[2 * k].wait()
         copies[2 * k + 1].wait()
-        copies[2 * k + 2].wait()
         rows = pl.ds(k * part, part)
         product = nn(hidden_ref[:, rows], weights_ref[rows, :])
         projected = product if projected is None else projected + product
         turned_ref[rows, :] = hidden_ref[:, rows].T
-    projected = projected * factor
     copies[-2].wait()
     copies[-1].wait()
 
-    def dkeyval(number):
-        columns = pl.ds(number * heads, heads)
-        return level_dkeyval(
-            projected[:, number * level : (number + 1) * level],
-            queries_ref.at[:, columns],
-            cotangent_ref.at[:, columns],
-        )
-
-    def term(number, dkv, start, rows):
-        grads = nn(turned_ref[start : start + rows, :], dkv)
-        own_weights = weights_ref[start : start + rows, number * level : (number + 1) * level]
-        return count * own_weights.astype(jnp.float32) - scale * grads
-
     leaving = []
 
-    def leave(source, target, rows):
-        copy = pltpu.make_async_copy(source.at[rows], target.at[rows], left.at[len(leaving)])
+    def leave(source, target):
+        copy = pltpu.make_async_copy(source, target, left.at[len(leaving)])
         copy.start()
         leaving.append(copy)
 
-    dkv = dkeyval(1)
-    for r in range(16):
-        base = r * 264
-        piece = term(1, dkv, r * 128, 128)
-        second_ref[base : base + 128, :] = piece[:, :128]
-        second_ref[base + 128 : base + 256, :] = piece[:, 128:]
-        if r % 4 == 3:
-            leave(second_ref, second, pl.ds((r - 3) * 264, 4 * 264))
-    dkv = dkeyval(0)
-    for r in range(16):
-        piece = term(0, dkv, r * 128, 128)
-        lower, upper = piece[:64], piece[64:]
-        base = r * 136
-        for ref, half in (
-            (keep_ref, jnp.where(own, lower, upper)),
-            (send_ref, jnp.where(own, upper, lower)),
-        ):
-            ref[base : base + 64, :] = half[:, :128]
-            ref[base + 64 : base + 128, :] = half[:, 128:]
-        if r % 4 == 3:
-            rows = pl.ds((r - 3) * 136, 4 * 136)
-            leave(keep_ref, keep, rows)
-            leave(send_ref, send, rows)
+    def ready(level, dkeyval):
+        for r in range(16):
+            rows = slice(r * 128, (r + 1) * 128)
+            own_weights = weights_ref[rows, level * level_columns : (level + 1) * level_columns]
+            piece = count * own_weights.astype(jnp.float32) - scale * nn(turned_ref[rows, :], dkeyval)
+            if level == 1:
+                base = r * 264
+                second_ref[base : base + 128, :] = piece[:, :128]
+                second_ref[base + 128 : base + 256, :] = piece[:, 128:]
+                if r % 4 == 3:
+                    done = pl.ds(base - 3 * 264, 4 * 264)
+                    leave(second_ref.at[done], second.at[done])
+            else:
+                base = r * 136
+                for core in range(2):
+                    half = piece[core * 64 : core * 64 + 64]
+                    first_ref[core, base : base + 64, :] = half[:, :128]
+                    first_ref[core, base + 64 : base + 128, :] = half[:, 128:]
+                if r % 4 == 3:
+                    done = pl.ds(base - 3 * 136, 4 * 136)
+                    leave(first_ref.at[1 - own, done], send.at[done])
+                    leave(first_ref.at[own, done], keep.at[done])
+
+    level_dkeyvals(projected * factor, queries_ref, cotangent_ref, (1, 0), ready)
     for copy in leaving:
         copy.wait()
 
 
+SMEM = pl.BlockSpec(memory_space=pltpu.SMEM)
 VMEM = pl.BlockSpec(memory_space=pltpu.VMEM)
 HBM = pl.BlockSpec(memory_space=pltpu.HBM)
 SMALL = pltpu.CompilerParams(vmem_limit_bytes=16 * 1024 * 1024)
@@ -176,23 +211,19 @@
 
 def level_terms(counts, hidden, weights, queries, cotangent):
     arrays = (hidden, weights, queries, cotangent)
-    shapes = [f32((16 * 264, 128)), f32((16 * 136, 128)), f32((16 * 136, 128))]
     return pl.pallas_call(
         terms_kernel,
-        in_specs=[HBM] * 5,
+        in_specs=[SMEM] + [HBM] * 4,
         out_specs=[HBM] * 3,
-        out_shape=shapes,
+        out_shape=[f32((16 * 264, 128)), f32((16 * 136, 128)), f32((16 * 136, 128))],
         scratch_shapes=[
-            pltpu.VMEM(hidden.shape, jnp.bfloat16),
-            pltpu.VMEM(hidden.shape[::-1], jnp.bfloat16),
-            pltpu.VMEM(weights.shape, jnp.bfloat16),
-            pltpu.VMEM(queries.shape, jnp.bfloat16),
-            pltpu.VMEM(cotangent.shape, jnp.bfloat16),
+            pltpu.VMEM(shape, jnp.bfloat16)
+            for shape in (hidden.shape, hidden.shape[::-1], weights.shape, queries.shape, cotangent.shape)
         ]
-        + [pltpu.VMEM(s.shape, jnp.float32) for s in shapes]
         + [
-            pltpu.SMEM((1, 1), jnp.int32),
-            pltpu.SemaphoreType.DMA((2 * PARTS + 3,)),
+            pltpu.VMEM((16 * 264, 128), jnp.float32),
+            pltpu.VMEM((2, 16 * 136, 128), jnp.float32),
+            pltpu.SemaphoreType.DMA((2 * PARTS + 2,)),
             pltpu.SemaphoreType.DMA((12,)),
         ],
         compiler_params=pltpu.CompilerParams(vmem_limit_bytes=62 * 1024 * 1024),

time: 73.9 us -> 72.4 us (0.980)
  the two profiles are of different devices: /device:TPU:72 before, /device:TPU:8 now
where the time goes in v4:
time: 72.4 us; the launch traced here: 72 us
  starting transfers between devices  41.9 us (58%)
  waiting for transfers between devices  19.7 us (27%)
  Pallas kernels  8.93 us (12%)
  between operations  1.41 us (2%)
    ppermute x3, starting transfers between devices, per_device(): lax.ppermute(sums[s - 1], 'z', [(i, (i + 2 * s) % 8) for i in range(8)])  13.7 us
    all_to_all x1, starting transfers between devices, per_device(): second_parts = lax.all_to_all(second, ('x_hi', 'y'), 0, 0, tiled=True)  10.2 us
    ppermute x1, starting transfers between devices, per_device(): other_b = lax.ppermute(send_b, 'z', pairs_b)  9.13 us
    pallas_call x1, Pallas kernels, level_terms(): pl.pallas_call(terms_kernel, in_specs=[SMEM] + [HBM] * 4, out_specs=[HBM]...  7.21 us
    ppermute x1, waiting for transfers between devices, per_device(): other_b = lax.ppermute(send_b, 'z', pairs_b)  6.65 us
    all_to_all x1, waiting for transfers between devices, per_device(): second_parts = lax.all_to_all(second, ('x_hi', 'y'), 0, 0, tiled=True)  5.42 us
    ppermute x3, waiting for transfers between devices, per_device(): lax.ppermute(sums[s - 1], 'z', [(i, (i + 2 * s) % 8) for i in range(8)])  4.72 us
    ppermute x1, starting transfers between devices, per_device(): other_a = lax.ppermute(send_a, 'z', pairs_a)  4.41 us
  transfers between devices with their start and end apart: 8, of which 6 were waited for; matrix products, arithmetic and copies ran while one was open for 0% of the time, Pallas kernels for 1%

profile of v4, /device:TPU:8, one launch (start us, length us, event | category | flops | bytes accessed | tf_op | source)
XLA Modules:
  0.0 72.0 jit_solution(6272930941432803901)
XLA Ops:
  1.3 7.2 %shard_map.120 = (f32[4224,128]{1,0:T(8,128)}, f32[2176,128]{1,0:T(8,128)}, f32[2176,128]{1,0:T(8,128)}) custom-call(s32[1,1]{1,0:T(1,128)S(6)} %copy.13.counts_ref, bf16[256,2048]{1,0:T(8,128)(2,1)} %bitcast.21, bf16[2048,512]{1,0:T(8,128)(2,1)} %bitcast.20, bf16[256,1024]{1,0:T(8,128)(2,1)} %bitcast.22, bf16[256,1024]{1,0:T(8,128)(2,1)} %bitcast.23), custom_call_target="tpu_custom_call" | custom-call | flops 2000000000 | bytes 8388608 | tf_op jit(solution)/shard_map/pallas_call | solution.py:214
  8.5 10.2 %all-to-all-start = ((f32[16,264,128]{2,1,0:T(8,128)}), f32[16,264,128]{2,1,0:T(8,128)S(1)}, u32[]{:S(2)}, u32[]{:S(2)}) async-start(f32[16,264,128]{2,1,0:T(8,128)} %bitcast.19), calls=%async_computation | async-start | bytes 4325376 | tf_op jit(solution)/shard_map/all_to_all | solution.py:353
  18.7 0.0 copy-start.2
  18.7 2.1 %collective-permute-start = (f32[2176,128]{1,0:T(8,128)}, f32[2176,128]{1,0:T(8,128)S(1)}, u32[]{:S(2)}, u32[]{:S(2)}) collective-permute-start(f32[2176,128]{1,0:T(8,128)} %get-tuple-element.23), channel_id=1, source_target_pairs={{0,1},{1,0},{2,3},{3,2},{4,5},{5,4},{6,7},{7,6},{8,9},{9,8},{10,11... | collective-permute-start | bytes 3342344 | tf_op jit(solution)/shard_map/ppermute | solution.py:352
  20.8 2.9 %collective-permute-done.other_ref = f32[2176,128]{1,0:T(8,128)S(1)} collective-permute-done((f32[2176,128]{1,0:T(8,128)}, f32[2176,128]{1,0:T(8,128)S(1)}, u32[]{:S(2)}, u32[]{:S(2)}) %collective-permute-start) | collective-permute-done | bytes 1114144 | tf_op jit(solution)/shard_map/ppermute | solution.py:352
  23.7 0.1 shard_map.121
  23.8 0.0 copy-start.3
  23.8 0.0 copy-start.4
  23.8 4.4 %collective-permute-start.1 = (f32[544,128]{1,0:T(8,128)S(1)}, f32[544,128]{1,0:T(8,128)S(1)}, u32[]{:S(2)}, u32[]{:S(2)}) collective-permute-start(f32[544,128]{1,0:T(8,128)S(1)} %get-tuple-element.26), channel_id=1, source_target_pairs={{0,4},{4,0},{8,12},{12,8},{16,20},{20,16},{24,28},{28,24},{1,5},{5... | collective-permute-start | bytes 835592 | tf_op jit(solution)/shard_map/ppermute | solution.py:357
  28.2 9.1 %collective-permute-start.2 = (f32[544,128]{1,0:T(8,128)S(1)}, f32[544,128]{1,0:T(8,128)S(1)}, u32[]{:S(2)}, u32[]{:S(2)}) collective-permute-start(f32[544,128]{1,0:T(8,128)S(1)} %get-tuple-element.27), channel_id=1, source_target_pairs={{0,28},{4,8},{8,4},{12,16},{16,12},{20,24},{24,20},{28,0},{1,29},{... | collective-permute-start | bytes 835592 | tf_op jit(solution)/shard_map/ppermute | solution.py:358
  37.4 0.0 collective-permute-done.1.a_other_ref
  37.4 6.7 %collective-permute-done.2.b_other_ref = f32[544,128]{1,0:T(8,128)S(1)} collective-permute-done((f32[544,128]{1,0:T(8,128)S(1)}, f32[544,128]{1,0:T(8,128)S(1)}, u32[]{:S(2)}, u32[]{:S(2)}) %collective-permute-start.2) | collective-permute-done | bytes 278560 | tf_op jit(solution)/shard_map/ppermute | solution.py:358
  44.0 0.1 shard_map.122
  44.1 5.7 %collective-permute-start.3 = (f32[272,128]{1,0:T(8,128)S(1)}, f32[272,128]{1,0:T(8,128)S(1)}, u32[]{:S(2)}, u32[]{:S(2)}) collective-permute-start(f32[272,128]{1,0:T(8,128)S(1)} %get-tuple-element.29), channel_id=1, source_target_pairs={{0,16},{4,20},{8,24},{12,28},{16,0},{20,4},{24,8},{28,12},{1,17},{... | collective-permute-start | bytes 417800 | tf_op jit(solution)/shard_map/ppermute | solution.py:361
  49.9 3.1 %collective-permute-start.4 = (f32[272,128]{1,0:T(8,128)S(1)}, f32[272,128]{1,0:T(8,128)S(1)}, u32[]{:S(2)}, u32[]{:S(2)}) collective-permute-start(f32[272,128]{1,0:T(8,128)S(1)} %get-tuple-element.30), channel_id=1, source_target_pairs={{0,8},{4,12},{8,16},{12,20},{16,24},{20,28},{24,0},{28,4},{1,9},{5... | collective-permute-start | bytes 417800 | tf_op jit(solution)/shard_map/ppermute | solution.py:361
  52.9 4.9 %collective-permute-start.5 = (f32[272,128]{1,0:T(8,128)S(1)}, f32[272,128]{1,0:T(8,128)S(1)}, u32[]{:S(2)}, u32[]{:S(2)}) collective-permute-start(f32[272,128]{1,0:T(8,128)S(1)} %get-tuple-element.31), channel_id=1, source_target_pairs={{0,24},{4,28},{8,0},{12,4},{16,8},{20,12},{24,16},{28,20},{1,25},{... | collective-permute-start | bytes 417800 | tf_op jit(solution)/shard_map/ppermute | solution.py:361
  57.8 1.1 %collective-permute-done.3.refs_1_ = f32[272,128]{1,0:T(8,128)S(1)} collective-permute-done((f32[272,128]{1,0:T(8,128)S(1)}, f32[272,128]{1,0:T(8,128)S(1)}, u32[]{:S(2)}, u32[]{:S(2)}) %collective-permute-start.3) | collective-permute-done | bytes 139296 | tf_op jit(solution)/shard_map/ppermute | solution.py:361
  58.9 2.0 %collective-permute-done.4.refs_2_ = f32[272,128]{1,0:T(8,128)S(1)} collective-permute-done((f32[272,128]{1,0:T(8,128)S(1)}, f32[272,128]{1,0:T(8,128)S(1)}, u32[]{:S(2)}, u32[]{:S(2)}) %collective-permute-start.4) | collective-permute-done | bytes 139296 | tf_op jit(solution)/shard_map/ppermute | solution.py:361
  60.9 1.6 %collective-permute-done.5.refs_3_ = f32[272,128]{1,0:T(8,128)S(1)} collective-permute-done((f32[272,128]{1,0:T(8,128)S(1)}, f32[272,128]{1,0:T(8,128)S(1)}, u32[]{:S(2)}, u32[]{:S(2)}) %collective-permute-start.5) | collective-permute-done | bytes 139296 | tf_op jit(solution)/shard_map/ppermute | solution.py:361
  62.6 2.5 %collective-permute-start.6 = (f32[136,128]{1,0:T(8,128)S(1)}, f32[136,128]{1,0:T(8,128)S(1)}, u32[]{:S(2)}, u32[]{:S(2)}) collective-permute-start(f32[136,128]{1,0:T(8,128)S(1)} %get-tuple-element.33), channel_id=1, source_target_pairs={{0,2},{2,0},{1,3},{3,1},{4,6},{6,4},{5,7},{7,5},{8,10},{10,8},{9,1... | collective-permute-start | bytes 208904 | tf_op jit(solution)/shard_map/ppermute | solution.py:364
  65.1 5.4 %all-to-all-done = f32[16,264,128]{2,1,0:T(8,128)S(1)} async-done(((f32[16,264,128]{2,1,0:T(8,128)}), f32[16,264,128]{2,1,0:T(8,128)S(1)}, u32[]{:S(2)}, u32[]{:S(2)}) %all-to-all-start) | async-done | bytes 2162720 | tf_op jit(solution)/shard_map/all_to_all | solution.py:353
  70.5 0.8 %shard_map.124 = (f32[128,256]{1,0:T(8,128)}, f32[128,256]{1,0:T(8,128)}, f32[8,128]{1,0:T(8,128)S(1)}) custom-call(f32[4224,128]{1,0:T(8,128)S(1)} %bitcast.14, f32[128,256]{1,0:T(8,128)S(1)} %bitcast.15, f32[128,256]{1,0:T(8,128)S(1)} %bitcast.16), custom_call_target="tpu_custom_call" | custom-call | tf_op jit(solution)/shard_map/pallas_call | solution.py:329
  71.3 0.0 collective-permute-done.6.other_ref
  71.3 0.7 shard_map.125
  (8 shorter events, 0.1 us)
Async XLA Ops:
  8.5 15.2 %copy-start = (f32[2176,128]{1,0:T(8,128)S(1)}, f32[2176,128]{1,0:T(8,128)}, u32[]{:S(2)}) copy-start(f32[2176,128]{1,0:T(8,128)} %get-tuple-element.22.mine_ref) | copy-start | bytes 3342340
  8.5 62.0 %all-to-all-start = ((f32[16,264,128]{2,1,0:T(8,128)}), f32[16,264,128]{2,1,0:T(8,128)S(1)}, u32[]{:S(2)}, u32[]{:S(2)}) async-start(f32[16,264,128]{2,1,0:T(8,128)} %bitcast.19), calls=%async_computation | async-start | bytes 4325376 | tf_op jit(solution)/shard_map/all_to_all | solution.py:353
  18.7 51.8 %copy-start.1 = (f32[1,128,256]{2,1,0:T(8,128)S(1)}, f32[1,128,256]{2,1,0:T(8,128)}, u32[]{:S(2)}) copy-start(f32[1,128,256]{2,1,0:T(8,128)} %param.16) | copy-start | bytes 393220
  18.7 51.8 %copy-start.2 = (f32[1,128,256]{2,1,0:T(8,128)S(1)}, f32[1,128,256]{2,1,0:T(8,128)}, u32[]{:S(2)}) copy-start(f32[1,128,256]{2,1,0:T(8,128)} %param.17) | copy-start | bytes 393220
  18.7 5.0 %collective-permute-start = (f32[2176,128]{1,0:T(8,128)}, f32[2176,128]{1,0:T(8,128)S(1)}, u32[]{:S(2)}, u32[]{:S(2)}) collective-permute-start(f32[2176,128]{1,0:T(8,128)} %get-tuple-element.23), channel_id=1, source_target_pairs={{0,1},{1,0},{2,3},{3,2},{4,5},{5,4},{6,7},{7,6},{8,9},{9,8},{10,11... | collective-permute-start | bytes 3342344 | tf_op jit(solution)/shard_map/ppermute | solution.py:352
  23.8 47.5 %copy-start.3 = (f32[1,64,256]{2,1,0:T(8,128)S(1)}, f32[1,64,256]{2,1,0:T(8,128)}, u32[]{:S(2)}) copy-start(f32[1,64,256]{2,1,0:T(8,128)} %param.14) | copy-start | bytes 196612
  23.8 47.5 %copy-start.4 = (f32[1,64,256]{2,1,0:T(8,128)S(1)}, f32[1,64,256]{2,1,0:T(8,128)}, u32[]{:S(2)}) copy-start(f32[1,64,256]{2,1,0:T(8,128)} %param.15) | copy-start | bytes 196612
  23.8 13.6 %collective-permute-start.1 = (f32[544,128]{1,0:T(8,128)S(1)}, f32[544,128]{1,0:T(8,128)S(1)}, u32[]{:S(2)}, u32[]{:S(2)}) collective-permute-start(f32[544,128]{1,0:T(8,128)S(1)} %get-tuple-element.26), channel_id=1, source_target_pairs={{0,4},{4,0},{8,12},{12,8},{16,20},{20,16},{24,28},{28,24},{1,5},{5... | collective-permute-start | bytes 835592 | tf_op jit(solution)/shard_map/ppermute | solution.py:357
  28.2 15.8 %collective-permute-start.2 = (f32[544,128]{1,0:T(8,128)S(1)}, f32[544,128]{1,0:T(8,128)S(1)}, u32[]{:S(2)}, u32[]{:S(2)}) collective-permute-start(f32[544,128]{1,0:T(8,128)S(1)} %get-tuple-element.27), channel_id=1, source_target_pairs={{0,28},{4,8},{8,4},{12,16},{16,12},{20,24},{24,20},{28,0},{1,29},{... | collective-permute-start | bytes 835592 | tf_op jit(solution)/shard_map/ppermute | solution.py:358
  44.1 14.8 %collective-permute-start.3 = (f32[272,128]{1,0:T(8,128)S(1)}, f32[272,128]{1,0:T(8,128)S(1)}, u32[]{:S(2)}, u32[]{:S(2)}) collective-permute-start(f32[272,128]{1,0:T(8,128)S(1)} %get-tuple-element.29), channel_id=1, source_target_pairs={{0,16},{4,20},{8,24},{12,28},{16,0},{20,4},{24,8},{28,12},{1,17},{... | collective-permute-start | bytes 417800 | tf_op jit(solution)/shard_map/ppermute | solution.py:361
  49.9 11.1 %collective-permute-start.4 = (f32[272,128]{1,0:T(8,128)S(1)}, f32[272,128]{1,0:T(8,128)S(1)}, u32[]{:S(2)}, u32[]{:S(2)}) collective-permute-start(f32[272,128]{1,0:T(8,128)S(1)} %get-tuple-element.30), channel_id=1, source_target_pairs={{0,8},{4,12},{8,16},{12,20},{16,24},{20,28},{24,0},{28,4},{1,9},{5... | collective-permute-start | bytes 417800 | tf_op jit(solution)/shard_map/ppermute | solution.py:361
  52.9 9.6 %collective-permute-start.5 = (f32[272,128]{1,0:T(8,128)S(1)}, f32[272,128]{1,0:T(8,128)S(1)}, u32[]{:S(2)}, u32[]{:S(2)}) collective-permute-start(f32[272,128]{1,0:T(8,128)S(1)} %get-tuple-element.31), channel_id=1, source_target_pairs={{0,24},{4,28},{8,0},{12,4},{16,8},{20,12},{24,16},{28,20},{1,25},{... | collective-permute-start | bytes 417800 | tf_op jit(solution)/shard_map/ppermute | solution.py:361
  62.6 8.7 %collective-permute-start.6 = (f32[136,128]{1,0:T(8,128)S(1)}, f32[136,128]{1,0:T(8,128)S(1)}, u32[]{:S(2)}, u32[]{:S(2)}) collective-permute-start(f32[136,128]{1,0:T(8,128)S(1)} %get-tuple-element.33), channel_id=1, source_target_pairs={{0,2},{2,0},{1,3},{3,1},{4,6},{6,4},{5,7},{7,5},{8,10},{10,8},{9,1... | collective-permute-start | bytes 208904 | tf_op jit(solution)/shard_map/ppermute | solution.py:364

commit v5 on v4

--- a/solution.py
+++ b/solution.py
@@ -313,16 +313,15 @@
         moment_new_ref[:, columns] = moment_new
 
 
-def first_finish_kernel(own_ref, other_ref, global_ref, moment_ref, ahead, *out_refs):
+def first_finish_kernel(own_ref, other_ref, global_ref, moment_ref, *out_refs):
     finish(own_ref[...] + other_ref[...], 64, global_ref, moment_ref, *out_refs)
 
 
-def second_finish_kernel(parts_ref, global_ref, moment_ref, new_ref, moment_new_ref, done_ref):
+def second_finish_kernel(parts_ref, *refs):
     total = parts_ref[0:264, :]
     for r in range(1, 16):
         total += parts_ref[r * 264 : (r + 1) * 264, :]
-    finish(total, 128, global_ref, moment_ref, new_ref, moment_new_ref)
-    done_ref[...] = total[256:264]
+    finish(total, 128, *refs)
 
 
 def finish_call(kernel, arrays, shapes):
@@ -362,14 +361,14 @@
     ]
     own, away = gathered([mine] + arrivals)
     across = lax.ppermute(away, "x_lo", [(0, 1), (1, 0)])
-    second_new, second_moment_new, done = finish_call(
+    second_new, second_moment_new = finish_call(
         second_finish_kernel,
         (second_parts, second_global[0], second_moment[0]),
-        [(128, 256), (128, 256), (8, 128)],
+        [(128, 256), (128, 256)],
     )
     first_new, first_moment_new = finish_call(
         first_finish_kernel,
-        (own, across, first_global[0], first_moment[0], done),
+        (own, across, first_global[0], first_moment[0]),
         [(64, 256), (64, 256)],
     )
     return (first_new[None], first_moment_new[None], second_new[None], second_moment_new[None])

time: 72.4 us -> 71.7 us (level)
  the two profiles are of different devices: /device:TPU:8 before, /device:TPU:6 now
where the time goes in v5:
time: 71.7 us; the launch traced here: 70.4 us
  starting transfers between devices  42.1 us (59%)
  waiting for transfers between devices  17.9 us (25%)
  Pallas kernels  8.93 us (12%)
  between operations  1.39 us (2%)
    ppermute x3, starting transfers between devices, per_device(): lax.ppermute(sums[s - 1], 'z', [(i, (i + 2 * s) % 8) for i in range(8)])  13.7 us
    all_to_all x1, starting transfers between devices, per_device(): second_parts = lax.all_to_all(second, ('x_hi', 'y'), 0, 0, tiled=True)  10.2 us
    ppermute x1, starting transfers between devices, per_device(): other_b = lax.ppermute(send_b, 'z', pairs_b)  9.13 us
    pallas_call x1, Pallas kernels, level_terms(): pl.pallas_call(terms_kernel, in_specs=[SMEM] + [HBM] * 4, out_specs=[HBM]...  7.21 us
    ppermute x1, waiting for transfers between devices, per_device(): other_b = lax.ppermute(send_b, 'z', pairs_b)  6.65 us
    ppermute x3, waiting for transfers between devices, per_device(): lax.ppermute(sums[s - 1], 'z', [(i, (i + 2 * s) % 8) for i in range(8)])  4.71 us
    ppermute x1, starting transfers between devices, per_device(): other_a = lax.ppermute(send_a, 'z', pairs_a)  4.29 us
    ppermute x1, waiting for transfers between devices, per_device(): across = lax.ppermute(away, 'x_lo', [(0, 1), (1, 0)])  3.59 us
  transfers between devices with their start and end apart: 8, of which 6 were waited for; matrix products, arithmetic and copies ran while one was open for 0% of the time, Pallas kernels for 1%

profile of v5, /device:TPU:6, one launch (start us, length us, event | category | flops | bytes accessed | tf_op | source)
XLA Modules:
  0.0 70.4 jit_solution(17844797154540393076)
XLA Ops:
  1.3 7.2 %shard_map.120 = (f32[4224,128]{1,0:T(8,128)}, f32[2176,128]{1,0:T(8,128)}, f32[2176,128]{1,0:T(8,128)}) custom-call(s32[1,1]{1,0:T(1,128)S(6)} %copy.13.counts_ref, bf16[256,2048]{1,0:T(8,128)(2,1)} %bitcast.21, bf16[2048,512]{1,0:T(8,128)(2,1)} %bitcast.20, bf16[256,1024]{1,0:T(8,128)(2,1)} %bitcast.22, bf16[256,1024]{1,0:T(8,128)(2,1)} %bitcast.23), custom_call_target="tpu_custom_call" | custom-call | flops 2000000000 | bytes 8388608 | tf_op jit(solution)/shard_map/pallas_call | solution.py:214
  8.5 10.2 %all-to-all-start = ((f32[16,264,128]{2,1,0:T(8,128)}), f32[16,264,128]{2,1,0:T(8,128)S(1)}, u32[]{:S(2)}, u32[]{:S(2)}) async-start(f32[16,264,128]{2,1,0:T(8,128)} %bitcast.19), calls=%async_computation | async-start | bytes 4325376 | tf_op jit(solution)/shard_map/all_to_all | solution.py:352
  18.7 0.0 copy-start.4
  18.7 2.1 %collective-permute-start = (f32[2176,128]{1,0:T(8,128)}, f32[2176,128]{1,0:T(8,128)S(1)}, u32[]{:S(2)}, u32[]{:S(2)}) collective-permute-start(f32[2176,128]{1,0:T(8,128)} %get-tuple-element.22), channel_id=1, source_target_pairs={{0,1},{1,0},{2,3},{3,2},{4,5},{5,4},{6,7},{7,6},{8,9},{9,8},{10,11... | collective-permute-start | bytes 3342344 | tf_op jit(solution)/shard_map/ppermute | solution.py:351
  20.8 2.9 %collective-permute-done.other_ref = f32[2176,128]{1,0:T(8,128)S(1)} collective-permute-done((f32[2176,128]{1,0:T(8,128)}, f32[2176,128]{1,0:T(8,128)S(1)}, u32[]{:S(2)}, u32[]{:S(2)}) %collective-permute-start) | collective-permute-done | bytes 1114144 | tf_op jit(solution)/shard_map/ppermute | solution.py:351
  23.7 0.1 shard_map.121
  23.9 4.3 %collective-permute-start.1 = (f32[544,128]{1,0:T(8,128)S(1)}, f32[544,128]{1,0:T(8,128)S(1)}, u32[]{:S(2)}, u32[]{:S(2)}) collective-permute-start(f32[544,128]{1,0:T(8,128)S(1)} %get-tuple-element.25), channel_id=1, source_target_pairs={{0,4},{4,0},{8,12},{12,8},{16,20},{20,16},{24,28},{28,24},{1,5},{5... | collective-permute-start | bytes 835592 | tf_op jit(solution)/shard_map/ppermute | solution.py:356
  28.2 9.1 %collective-permute-start.2 = (f32[544,128]{1,0:T(8,128)S(1)}, f32[544,128]{1,0:T(8,128)S(1)}, u32[]{:S(2)}, u32[]{:S(2)}) collective-permute-start(f32[544,128]{1,0:T(8,128)S(1)} %get-tuple-element.26), channel_id=1, source_target_pairs={{0,28},{4,8},{8,4},{12,16},{16,12},{20,24},{24,20},{28,0},{1,29},{... | collective-permute-start | bytes 835592 | tf_op jit(solution)/shard_map/ppermute | solution.py:357
  37.3 0.0 collective-permute-done.1.a_other_ref
  37.3 6.7 %collective-permute-done.2.b_other_ref = f32[544,128]{1,0:T(8,128)S(1)} collective-permute-done((f32[544,128]{1,0:T(8,128)S(1)}, f32[544,128]{1,0:T(8,128)S(1)}, u32[]{:S(2)}, u32[]{:S(2)}) %collective-permute-start.2) | collective-permute-done | bytes 278560 | tf_op jit(solution)/shard_map/ppermute | solution.py:357
  44.0 0.1 shard_map.122
  44.0 5.7 %collective-permute-start.3 = (f32[272,128]{1,0:T(8,128)S(1)}, f32[272,128]{1,0:T(8,128)S(1)}, u32[]{:S(2)}, u32[]{:S(2)}) collective-permute-start(f32[272,128]{1,0:T(8,128)S(1)} %get-tuple-element.28), channel_id=1, source_target_pairs={{0,16},{4,20},{8,24},{12,28},{16,0},{20,4},{24,8},{28,12},{1,17},{... | collective-permute-start | bytes 417800 | tf_op jit(solution)/shard_map/ppermute | solution.py:360
  49.8 3.1 %collective-permute-start.4 = (f32[272,128]{1,0:T(8,128)S(1)}, f32[272,128]{1,0:T(8,128)S(1)}, u32[]{:S(2)}, u32[]{:S(2)}) collective-permute-start(f32[272,128]{1,0:T(8,128)S(1)} %get-tuple-element.29), channel_id=1, source_target_pairs={{0,8},{4,12},{8,16},{12,20},{16,24},{20,28},{24,0},{28,4},{1,9},{5... | collective-permute-start | bytes 417800 | tf_op jit(solution)/shard_map/ppermute | solution.py:360
  52.8 4.9 %collective-permute-start.5 = (f32[272,128]{1,0:T(8,128)S(1)}, f32[272,128]{1,0:T(8,128)S(1)}, u32[]{:S(2)}, u32[]{:S(2)}) collective-permute-start(f32[272,128]{1,0:T(8,128)S(1)} %get-tuple-element.30), channel_id=1, source_target_pairs={{0,24},{4,28},{8,0},{12,4},{16,8},{20,12},{24,16},{28,20},{1,25},{... | collective-permute-start | bytes 417800 | tf_op jit(solution)/shard_map/ppermute | solution.py:360
  57.7 1.1 %collective-permute-done.3.refs_1_ = f32[272,128]{1,0:T(8,128)S(1)} collective-permute-done((f32[272,128]{1,0:T(8,128)S(1)}, f32[272,128]{1,0:T(8,128)S(1)}, u32[]{:S(2)}, u32[]{:S(2)}) %collective-permute-start.3) | collective-permute-done | bytes 139296 | tf_op jit(solution)/shard_map/ppermute | solution.py:360
  58.9 2.0 %collective-permute-done.4.refs_2_ = f32[272,128]{1,0:T(8,128)S(1)} collective-permute-done((f32[272,128]{1,0:T(8,128)S(1)}, f32[272,128]{1,0:T(8,128)S(1)}, u32[]{:S(2)}, u32[]{:S(2)}) %collective-permute-start.4) | collective-permute-done | bytes 139296 | tf_op jit(solution)/shard_map/ppermute | solution.py:360
  60.8 1.6 %collective-permute-done.5.refs_3_ = f32[272,128]{1,0:T(8,128)S(1)} collective-permute-done((f32[272,128]{1,0:T(8,128)S(1)}, f32[272,128]{1,0:T(8,128)S(1)}, u32[]{:S(2)}, u32[]{:S(2)}) %collective-permute-start.5) | collective-permute-done | bytes 139296 | tf_op jit(solution)/shard_map/ppermute | solution.py:360
  62.5 2.8 %collective-permute-start.6 = (f32[136,128]{1,0:T(8,128)S(1)}, f32[136,128]{1,0:T(8,128)S(1)}, u32[]{:S(2)}, u32[]{:S(2)}) collective-permute-start(f32[136,128]{1,0:T(8,128)S(1)} %get-tuple-element.32), channel_id=1, source_target_pairs={{0,2},{2,0},{1,3},{3,1},{4,6},{6,4},{5,7},{7,5},{8,10},{10,8},{9,1... | collective-permute-start | bytes 208904 | tf_op jit(solution)/shard_map/ppermute | solution.py:363
  65.2 3.6 %collective-permute-done.6.other_ref = f32[136,128]{1,0:T(8,128)S(1)} collective-permute-done((f32[136,128]{1,0:T(8,128)S(1)}, f32[136,128]{1,0:T(8,128)S(1)}, u32[]{:S(2)}, u32[]{:S(2)}) %collective-permute-start.6) | collective-permute-done | bytes 69664 | tf_op jit(solution)/shard_map/ppermute | solution.py:363
  68.8 0.0 copy-done.4
  68.8 0.7 shard_map.124
  69.5 0.0 all-to-all-done
  69.5 0.0 copy-done.2
  69.5 0.8 %shard_map.125 = (f32[128,256]{1,0:T(8,128)}, f32[128,256]{1,0:T(8,128)}) custom-call(f32[4224,128]{1,0:T(8,128)S(1)} %bitcast.14, f32[128,256]{1,0:T(8,128)S(1)} %bitcast.15, f32[128,256]{1,0:T(8,128)S(1)} %bitcast.16), custom_call_target="tpu_custom_call" | custom-call | tf_op jit(solution)/shard_map/pallas_call | solution.py:328
  (8 shorter events, 0.1 us)
Async XLA Ops:
  8.5 15.2 %copy-start = (f32[2176,128]{1,0:T(8,128)S(1)}, f32[2176,128]{1,0:T(8,128)}, u32[]{:S(2)}) copy-start(f32[2176,128]{1,0:T(8,128)} %get-tuple-element.21.mine_ref) | copy-start | bytes 3342340
  8.5 61.0 %all-to-all-start = ((f32[16,264,128]{2,1,0:T(8,128)}), f32[16,264,128]{2,1,0:T(8,128)S(1)}, u32[]{:S(2)}, u32[]{:S(2)}) async-start(f32[16,264,128]{2,1,0:T(8,128)} %bitcast.19), calls=%async_computation | async-start | bytes 4325376 | tf_op jit(solution)/shard_map/all_to_all | solution.py:352
  18.7 50.1 %copy-start.3 = (f32[1,64,256]{2,1,0:T(8,128)S(1)}, f32[1,64,256]{2,1,0:T(8,128)}, u32[]{:S(2)}) copy-start(f32[1,64,256]{2,1,0:T(8,128)} %param.14) | copy-start | bytes 196612
  18.7 50.1 %copy-start.4 = (f32[1,64,256]{2,1,0:T(8,128)S(1)}, f32[1,64,256]{2,1,0:T(8,128)}, u32[]{:S(2)}) copy-start(f32[1,64,256]{2,1,0:T(8,128)} %param.15) | copy-start | bytes 196612
  18.7 5.0 %collective-permute-start = (f32[2176,128]{1,0:T(8,128)}, f32[2176,128]{1,0:T(8,128)S(1)}, u32[]{:S(2)}, u32[]{:S(2)}) collective-permute-start(f32[2176,128]{1,0:T(8,128)} %get-tuple-element.22), channel_id=1, source_target_pairs={{0,1},{1,0},{2,3},{3,2},{4,5},{5,4},{6,7},{7,6},{8,9},{9,8},{10,11... | collective-permute-start | bytes 3342344 | tf_op jit(solution)/shard_map/ppermute | solution.py:351
  23.7 45.8 %copy-start.1 = (f32[1,128,256]{2,1,0:T(8,128)S(1)}, f32[1,128,256]{2,1,0:T(8,128)}, u32[]{:S(2)}) copy-start(f32[1,128,256]{2,1,0:T(8,128)} %param.16) | copy-start | bytes 393220
  23.7 45.8 %copy-start.2 = (f32[1,128,256]{2,1,0:T(8,128)S(1)}, f32[1,128,256]{2,1,0:T(8,128)}, u32[]{:S(2)}) copy-start(f32[1,128,256]{2,1,0:T(8,128)} %param.17) | copy-start | bytes 393220
  23.9 13.4 %collective-permute-start.1 = (f32[544,128]{1,0:T(8,128)S(1)}, f32[544,128]{1,0:T(8,128)S(1)}, u32[]{:S(2)}, u32[]{:S(2)}) collective-permute-start(f32[544,128]{1,0:T(8,128)S(1)} %get-tuple-element.25), channel_id=1, source_target_pairs={{0,4},{4,0},{8,12},{12,8},{16,20},{20,16},{24,28},{28,24},{1,5},{5... | collective-permute-start | bytes 835592 | tf_op jit(solution)/shard_map/ppermute | solution.py:356
  28.2 15.8 %collective-permute-start.2 = (f32[544,128]{1,0:T(8,128)S(1)}, f32[544,128]{1,0:T(8,128)S(1)}, u32[]{:S(2)}, u32[]{:S(2)}) collective-permute-start(f32[544,128]{1,0:T(8,128)S(1)} %get-tuple-element.26), channel_id=1, source_target_pairs={{0,28},{4,8},{8,4},{12,16},{16,12},{20,24},{24,20},{28,0},{1,29},{... | collective-permute-start | bytes 835592 | tf_op jit(solution)/shard_map/ppermute | solution.py:357
  44.0 14.8 %collective-permute-start.3 = (f32[272,128]{1,0:T(8,128)S(1)}, f32[272,128]{1,0:T(8,128)S(1)}, u32[]{:S(2)}, u32[]{:S(2)}) collective-permute-start(f32[272,128]{1,0:T(8,128)S(1)} %get-tuple-element.28), channel_id=1, source_target_pairs={{0,16},{4,20},{8,24},{12,28},{16,0},{20,4},{24,8},{28,12},{1,17},{... | collective-permute-start | bytes 417800 | tf_op jit(solution)/shard_map/ppermute | solution.py:360
  49.8 11.1 %collective-permute-start.4 = (f32[272,128]{1,0:T(8,128)S(1)}, f32[272,128]{1,0:T(8,128)S(1)}, u32[]{:S(2)}, u32[]{:S(2)}) collective-permute-start(f32[272,128]{1,0:T(8,128)S(1)} %get-tuple-element.29), channel_id=1, source_target_pairs={{0,8},{4,12},{8,16},{12,20},{16,24},{20,28},{24,0},{28,4},{1,9},{5... | collective-permute-start | bytes 417800 | tf_op jit(solution)/shard_map/ppermute | solution.py:360
  52.8 9.6 %collective-permute-start.5 = (f32[272,128]{1,0:T(8,128)S(1)}, f32[272,128]{1,0:T(8,128)S(1)}, u32[]{:S(2)}, u32[]{:S(2)}) collective-permute-start(f32[272,128]{1,0:T(8,128)S(1)} %get-tuple-element.30), channel_id=1, source_target_pairs={{0,24},{4,28},{8,0},{12,4},{16,8},{20,12},{24,16},{28,20},{1,25},{... | collective-permute-start | bytes 417800 | tf_op jit(solution)/shard_map/ppermute | solution.py:360
  62.5 6.4 %collective-permute-start.6 = (f32[136,128]{1,0:T(8,128)S(1)}, f32[136,128]{1,0:T(8,128)S(1)}, u32[]{:S(2)}, u32[]{:S(2)}) collective-permute-start(f32[136,128]{1,0:T(8,128)S(1)} %get-tuple-element.32), channel_id=1, source_target_pairs={{0,2},{2,0},{1,3},{3,1},{4,6},{6,4},{5,7},{7,5},{8,10},{10,8},{9,1... | collective-permute-start | bytes 208904 | tf_op jit(solution)/shard_map/ppermute | solution.py:363

commit v6 on v5

--- a/solution.py
+++ b/solution.py
@@ -152,7 +152,7 @@
     scale = count * (inner_rate * factor)
     counts = jnp.full((8, 128), count, jnp.float32)
     for r in range(16):
-        second_ref[r * 264 + 256 : r * 264 + 264, :] = counts
+        second_ref[r * 258 + 256 : r * 258 + 258, :] = counts[:2]
         for core in range(2):
             first_ref[core, r * 136 + 128 : r * 136 + 136, :] = counts
 
@@ -180,11 +180,11 @@
             own_weights = weights_ref[rows, level * level_columns : (level + 1) * level_columns]
             piece = count * own_weights.astype(jnp.float32) - scale * nn(turned_ref[rows, :], dkeyval)
             if level == 1:
-                base = r * 264
+                base = r * 258
                 second_ref[base : base + 128, :] = piece[:, :128]
                 second_ref[base + 128 : base + 256, :] = piece[:, 128:]
                 if r % 4 == 3:
-                    done = pl.ds(base - 3 * 264, 4 * 264)
+                    done = pl.ds(base - 3 * 258, 4 * 258)
                     leave(second_ref.at[done], second.at[done])
             else:
                 base = r * 136
@@ -215,13 +215,13 @@
         terms_kernel,
         in_specs=[SMEM] + [HBM] * 4,
         out_specs=[HBM] * 3,
-        out_shape=[f32((16 * 264, 128)), f32((16 * 136, 128)), f32((16 * 136, 128))],
+        out_shape=[f32((16 * 258, 128)), f32((16 * 136, 128)), f32((16 * 136, 128))],
         scratch_shapes=[
             pltpu.VMEM(shape, jnp.bfloat16)
             for shape in (hidden.shape, hidden.shape[::-1], weights.shape, queries.shape, cotangent.shape)
         ]
         + [
-            pltpu.VMEM((16 * 264, 128), jnp.float32),
+            pltpu.VMEM((16 * 258, 128), jnp.float32),
             pltpu.VMEM((2, 16 * 136, 128), jnp.float32),
             pltpu.SemaphoreType.DMA((2 * PARTS + 2,)),
             pltpu.SemaphoreType.DMA((12,)),
@@ -318,9 +318,9 @@
 
 
 def second_finish_kernel(parts_ref, *refs):
-    total = parts_ref[0:264, :]
+    total = parts_ref[0:258, :]
     for r in range(1, 16):
-        total += parts_ref[r * 264 : (r + 1) * 264, :]
+        total += parts_ref[r * 258 : (r + 1) * 258, :]
     finish(total, 128, *refs)
 
 
@@ -349,7 +349,9 @@
         counts, hidden[0, 0], weights[0, 0], queries[0, 0], cotangent[0, 0]
     )
     other = lax.ppermute(send, "core", [(0, 1), (1, 0)])
-    second_parts = lax.all_to_all(second, ("x_hi", "y"), 0, 0, tiled=True)
+    second_parts = lax.all_to_all(
+        second.reshape(16 * 129, 2, 128), ("x_hi", "y"), 0, 0, tiled=True
+    ).reshape(16 * 258, 128)
     keep_a, keep_b, send_a, send_b = pair_sums(keep, other)
     pairs_a = [(i, i + 1 - 2 * (i % 2)) for i in range(8)]
     pairs_b = [(i, (i - 1 + 2 * (i % 2)) % 8) for i in range(8)]

time: 71.7 us -> 70.7 us (0.986); the launches traced: 70.4 us -> 70.2 us
  no operation moved by 1% of the time
where the time goes in v6:
time: 70.7 us; the launch traced here: 70.2 us
  starting transfers between devices  42.1 us (60%)
  waiting for transfers between devices  17.7 us (25%)
  Pallas kernels  8.93 us (13%)
  between operations  1.39 us (2%)
    ppermute x3, starting transfers between devices, per_device(): lax.ppermute(sums[s - 1], 'z', [(i, (i + 2 * s) % 8) for i in range(8)])  13.7 us
    all_to_all x1, starting transfers between devices, per_device(): lax.all_to_all(second.reshape(16 * 129, 2, 128), ('x_hi', 'y'), 0, 0, til...  10.2 us
    ppermute x1, starting transfers between devices, per_device(): other_b = lax.ppermute(send_b, 'z', pairs_b)  9.13 us
    pallas_call x1, Pallas kernels, level_terms(): pl.pallas_call(terms_kernel, in_specs=[SMEM] + [HBM] * 4, out_specs=[HBM]...  7.2 us
    ppermute x1, waiting for transfers between devices, per_device(): other_b = lax.ppermute(send_b, 'z', pairs_b)  6.65 us
    ppermute x3, waiting for transfers between devices, per_device(): lax.ppermute(sums[s - 1], 'z', [(i, (i + 2 * s) % 8) for i in range(8)])  4.71 us
    ppermute x1, starting transfers between devices, per_device(): other_a = lax.ppermute(send_a, 'z', pairs_a)  4.29 us
    ppermute x1, waiting for transfers between devices, per_device(): across = lax.ppermute(away, 'x_lo', [(0, 1), (1, 0)])  3.44 us
  transfers between devices with their start and end apart: 8, of which 6 were waited for; matrix products, arithmetic and copies ran while one was open for 0% of the time, Pallas kernels for 1%

profile of v6, /device:TPU:6, one launch (start us, length us, event | category | flops | bytes accessed | tf_op | source)
XLA Modules:
  0.0 70.2 jit_solution(2812815297355461148)
XLA Ops:
  1.3 7.2 %shard_map.120 = (f32[4128,128]{1,0:T(8,128)}, f32[2176,128]{1,0:T(8,128)}, f32[2176,128]{1,0:T(8,128)}) custom-call(s32[1,1]{1,0:T(1,128)S(6)} %copy.13.counts_ref, bf16[256,2048]{1,0:T(8,128)(2,1)} %bitcast.21, bf16[2048,512]{1,0:T(8,128)(2,1)} %bitcast.20, bf16[256,1024]{1,0:T(8,128)(2,1)} %bitcast.22, bf16[256,1024]{1,0:T(8,128)(2,1)} %bitcast.23), custom_call_target="tpu_custom_call" | custom-call | flops 2000000000 | bytes 8388608 | tf_op jit(solution)/shard_map/pallas_call | solution.py:214
  8.5 10.2 %all-to-all-start = ((f32[2064,2,128]{2,1,0:T(2,128)}), f32[2064,2,128]{2,1,0:T(2,128)S(1)}, u32[]{:S(2)}, u32[]{:S(2)}) async-start(f32[2064,2,128]{2,1,0:T(2,128)} %bitcast.19), calls=%async_computation | async-start | bytes 4227072 | tf_op jit(solution)/shard_map/all_to_all | solution.py:352
  18.7 0.0 copy-start.4
  18.7 2.1 %collective-permute-start = (f32[2176,128]{1,0:T(8,128)}, f32[2176,128]{1,0:T(8,128)S(1)}, u32[]{:S(2)}, u32[]{:S(2)}) collective-permute-start(f32[2176,128]{1,0:T(8,128)} %get-tuple-element.22), channel_id=1, source_target_pairs={{0,1},{1,0},{2,3},{3,2},{4,5},{5,4},{6,7},{7,6},{8,9},{9,8},{10,11... | collective-permute-start | bytes 3342344 | tf_op jit(solution)/shard_map/ppermute | solution.py:351
  20.8 2.9 %collective-permute-done.other_ref = f32[2176,128]{1,0:T(8,128)S(1)} collective-permute-done((f32[2176,128]{1,0:T(8,128)}, f32[2176,128]{1,0:T(8,128)S(1)}, u32[]{:S(2)}, u32[]{:S(2)}) %collective-permute-start) | collective-permute-done | bytes 1114144 | tf_op jit(solution)/shard_map/ppermute | solution.py:351
  23.7 0.1 shard_map.121
  23.9 4.3 %collective-permute-start.1 = (f32[544,128]{1,0:T(8,128)S(1)}, f32[544,128]{1,0:T(8,128)S(1)}, u32[]{:S(2)}, u32[]{:S(2)}) collective-permute-start(f32[544,128]{1,0:T(8,128)S(1)} %get-tuple-element.25), channel_id=1, source_target_pairs={{0,4},{4,0},{8,12},{12,8},{16,20},{20,16},{24,28},{28,24},{1,5},{5... | collective-permute-start | bytes 835592 | tf_op jit(solution)/shard_map/ppermute | solution.py:358
  28.1 9.1 %collective-permute-start.2 = (f32[544,128]{1,0:T(8,128)S(1)}, f32[544,128]{1,0:T(8,128)S(1)}, u32[]{:S(2)}, u32[]{:S(2)}) collective-permute-start(f32[544,128]{1,0:T(8,128)S(1)} %get-tuple-element.26), channel_id=1, source_target_pairs={{0,28},{4,8},{8,4},{12,16},{16,12},{20,24},{24,20},{28,0},{1,29},{... | collective-permute-start | bytes 835592 | tf_op jit(solution)/shard_map/ppermute | solution.py:359
  37.3 0.0 collective-permute-done.1.a_other_ref
  37.3 6.7 %collective-permute-done.2.b_other_ref = f32[544,128]{1,0:T(8,128)S(1)} collective-permute-done((f32[544,128]{1,0:T(8,128)S(1)}, f32[544,128]{1,0:T(8,128)S(1)}, u32[]{:S(2)}, u32[]{:S(2)}) %collective-permute-start.2) | collective-permute-done | bytes 278560 | tf_op jit(solution)/shard_map/ppermute | solution.py:359
  43.9 0.1 shard_map.122
  44.0 5.7 %collective-permute-start.3 = (f32[272,128]{1,0:T(8,128)S(1)}, f32[272,128]{1,0:T(8,128)S(1)}, u32[]{:S(2)}, u32[]{:S(2)}) collective-permute-start(f32[272,128]{1,0:T(8,128)S(1)} %get-tuple-element.28), channel_id=1, source_target_pairs={{0,16},{4,20},{8,24},{12,28},{16,0},{20,4},{24,8},{28,12},{1,17},{... | collective-permute-start | bytes 417800 | tf_op jit(solution)/shard_map/ppermute | solution.py:362
  49.8 3.1 %collective-permute-start.4 = (f32[272,128]{1,0:T(8,128)S(1)}, f32[272,128]{1,0:T(8,128)S(1)}, u32[]{:S(2)}, u32[]{:S(2)}) collective-permute-start(f32[272,128]{1,0:T(8,128)S(1)} %get-tuple-element.29), channel_id=1, source_target_pairs={{0,8},{4,12},{8,16},{12,20},{16,24},{20,28},{24,0},{28,4},{1,9},{5... | collective-permute-start | bytes 417800 | tf_op jit(solution)/shard_map/ppermute | solution.py:362
  52.8 4.9 %collective-permute-start.5 = (f32[272,128]{1,0:T(8,128)S(1)}, f32[272,128]{1,0:T(8,128)S(1)}, u32[]{:S(2)}, u32[]{:S(2)}) collective-permute-start(f32[272,128]{1,0:T(8,128)S(1)} %get-tuple-element.30), channel_id=1, source_target_pairs={{0,24},{4,28},{8,0},{12,4},{16,8},{20,12},{24,16},{28,20},{1,25},{... | collective-permute-start | bytes 417800 | tf_op jit(solution)/shard_map/ppermute | solution.py:362
  57.7 1.1 %collective-permute-done.3.refs_1_ = f32[272,128]{1,0:T(8,128)S(1)} collective-permute-done((f32[272,128]{1,0:T(8,128)S(1)}, f32[272,128]{1,0:T(8,128)S(1)}, u32[]{:S(2)}, u32[]{:S(2)}) %collective-permute-start.3) | collective-permute-done | bytes 139296 | tf_op jit(solution)/shard_map/ppermute | solution.py:362
  58.8 2.0 %collective-permute-done.4.refs_2_ = f32[272,128]{1,0:T(8,128)S(1)} collective-permute-done((f32[272,128]{1,0:T(8,128)S(1)}, f32[272,128]{1,0:T(8,128)S(1)}, u32[]{:S(2)}, u32[]{:S(2)}) %collective-permute-start.4) | collective-permute-done | bytes 139296 | tf_op jit(solution)/shard_map/ppermute | solution.py:362
  60.8 1.6 %collective-permute-done.5.refs_3_ = f32[272,128]{1,0:T(8,128)S(1)} collective-permute-done((f32[272,128]{1,0:T(8,128)S(1)}, f32[272,128]{1,0:T(8,128)S(1)}, u32[]{:S(2)}, u32[]{:S(2)}) %collective-permute-start.5) | collective-permute-done | bytes 139296 | tf_op jit(solution)/shard_map/ppermute | solution.py:362
  62.5 2.8 %collective-permute-start.6 = (f32[136,128]{1,0:T(8,128)S(1)}, f32[136,128]{1,0:T(8,128)S(1)}, u32[]{:S(2)}, u32[]{:S(2)}) collective-permute-start(f32[136,128]{1,0:T(8,128)S(1)} %get-tuple-element.32), channel_id=1, source_target_pairs={{0,2},{2,0},{1,3},{3,1},{4,6},{6,4},{5,7},{7,5},{8,10},{10,8},{9,1... | collective-permute-start | bytes 208904 | tf_op jit(solution)/shard_map/ppermute | solution.py:365
  65.2 3.4 %collective-permute-done.6.other_ref = f32[136,128]{1,0:T(8,128)S(1)} collective-permute-done((f32[136,128]{1,0:T(8,128)S(1)}, f32[136,128]{1,0:T(8,128)S(1)}, u32[]{:S(2)}, u32[]{:S(2)}) %collective-permute-start.6) | collective-permute-done | bytes 69664 | tf_op jit(solution)/shard_map/ppermute | solution.py:365
  68.7 0.0 copy-done.3
  68.7 0.7 shard_map.124
  69.4 0.0 all-to-all-done
  69.4 0.0 copy-done.1
  69.4 0.8 %shard_map.125 = (f32[128,256]{1,0:T(8,128)}, f32[128,256]{1,0:T(8,128)}) custom-call(f32[4128,128]{1,0:T(8,128)S(1)} %bitcast.14, f32[128,256]{1,0:T(8,128)S(1)} %bitcast.15, f32[128,256]{1,0:T(8,128)S(1)} %bitcast.16), custom_call_target="tpu_custom_call" | custom-call | tf_op jit(solution)/shard_map/pallas_call | solution.py:328
  (8 shorter events, 0.1 us)
Async XLA Ops:
  8.5 15.2 %copy-start = (f32[2176,128]{1,0:T(8,128)S(1)}, f32[2176,128]{1,0:T(8,128)}, u32[]{:S(2)}) copy-start(f32[2176,128]{1,0:T(8,128)} %get-tuple-element.21.mine_ref) | copy-start | bytes 3342340
  8.5 60.9 %all-to-all-start = ((f32[2064,2,128]{2,1,0:T(2,128)}), f32[2064,2,128]{2,1,0:T(2,128)S(1)}, u32[]{:S(2)}, u32[]{:S(2)}) async-start(f32[2064,2,128]{2,1,0:T(2,128)} %bitcast.19), calls=%async_computation | async-start | bytes 4227072 | tf_op jit(solution)/shard_map/all_to_all | solution.py:352
  18.7 50.0 %copy-start.3 = (f32[1,64,256]{2,1,0:T(8,128)S(1)}, f32[1,64,256]{2,1,0:T(8,128)}, u32[]{:S(2)}) copy-start(f32[1,64,256]{2,1,0:T(8,128)} %param.14) | copy-start | bytes 196612
  18.7 49.9 %copy-start.4 = (f32[1,64,256]{2,1,0:T(8,128)S(1)}, f32[1,64,256]{2,1,0:T(8,128)}, u32[]{:S(2)}) copy-start(f32[1,64,256]{2,1,0:T(8,128)} %param.15) | copy-start | bytes 196612
  18.7 5.0 %collective-permute-start = (f32[2176,128]{1,0:T(8,128)}, f32[2176,128]{1,0:T(8,128)S(1)}, u32[]{:S(2)}, u32[]{:S(2)}) collective-permute-start(f32[2176,128]{1,0:T(8,128)} %get-tuple-element.22), channel_id=1, source_target_pairs={{0,1},{1,0},{2,3},{3,2},{4,5},{5,4},{6,7},{7,6},{8,9},{9,8},{10,11... | collective-permute-start | bytes 3342344 | tf_op jit(solution)/shard_map/ppermute | solution.py:351
  23.7 45.6 %copy-start.1 = (f32[1,128,256]{2,1,0:T(8,128)S(1)}, f32[1,128,256]{2,1,0:T(8,128)}, u32[]{:S(2)}) copy-start(f32[1,128,256]{2,1,0:T(8,128)} %param.16) | copy-start | bytes 393220
  23.7 45.6 %copy-start.2 = (f32[1,128,256]{2,1,0:T(8,128)S(1)}, f32[1,128,256]{2,1,0:T(8,128)}, u32[]{:S(2)}) copy-start(f32[1,128,256]{2,1,0:T(8,128)} %param.17) | copy-start | bytes 393220
  23.9 13.4 %collective-permute-start.1 = (f32[544,128]{1,0:T(8,128)S(1)}, f32[544,128]{1,0:T(8,128)S(1)}, u32[]{:S(2)}, u32[]{:S(2)}) collective-permute-start(f32[544,128]{1,0:T(8,128)S(1)} %get-tuple-element.25), channel_id=1, source_target_pairs={{0,4},{4,0},{8,12},{12,8},{16,20},{20,16},{24,28},{28,24},{1,5},{5... | collective-permute-start | bytes 835592 | tf_op jit(solution)/shard_map/ppermute | solution.py:358
  28.1 15.8 %collective-permute-start.2 = (f32[544,128]{1,0:T(8,128)S(1)}, f32[544,128]{1,0:T(8,128)S(1)}, u32[]{:S(2)}, u32[]{:S(2)}) collective-permute-start(f32[544,128]{1,0:T(8,128)S(1)} %get-tuple-element.26), channel_id=1, source_target_pairs={{0,28},{4,8},{8,4},{12,16},{16,12},{20,24},{24,20},{28,0},{1,29},{... | collective-permute-start | bytes 835592 | tf_op jit(solution)/shard_map/ppermute | solution.py:359
  44.0 14.8 %collective-permute-start.3 = (f32[272,128]{1,0:T(8,128)S(1)}, f32[272,128]{1,0:T(8,128)S(1)}, u32[]{:S(2)}, u32[]{:S(2)}) collective-permute-start(f32[272,128]{1,0:T(8,128)S(1)} %get-tuple-element.28), channel_id=1, source_target_pairs={{0,16},{4,20},{8,24},{12,28},{16,0},{20,4},{24,8},{28,12},{1,17},{... | collective-permute-start | bytes 417800 | tf_op jit(solution)/shard_map/ppermute | solution.py:362
  49.8 11.1 %collective-permute-start.4 = (f32[272,128]{1,0:T(8,128)S(1)}, f32[272,128]{1,0:T(8,128)S(1)}, u32[]{:S(2)}, u32[]{:S(2)}) collective-permute-start(f32[272,128]{1,0:T(8,128)S(1)} %get-tuple-element.29), channel_id=1, source_target_pairs={{0,8},{4,12},{8,16},{12,20},{16,24},{20,28},{24,0},{28,4},{1,9},{5... | collective-permute-start | bytes 417800 | tf_op jit(solution)/shard_map/ppermute | solution.py:362
  52.8 9.6 %collective-permute-start.5 = (f32[272,128]{1,0:T(8,128)S(1)}, f32[272,128]{1,0:T(8,128)S(1)}, u32[]{:S(2)}, u32[]{:S(2)}) collective-permute-start(f32[272,128]{1,0:T(8,128)S(1)} %get-tuple-element.30), channel_id=1, source_target_pairs={{0,24},{4,28},{8,0},{12,4},{16,8},{20,12},{24,16},{28,20},{1,25},{... | collective-permute-start | bytes 417800 | tf_op jit(solution)/shard_map/ppermute | solution.py:362
  62.5 6.2 %collective-permute-start.6 = (f32[136,128]{1,0:T(8,128)S(1)}, f32[136,128]{1,0:T(8,128)S(1)}, u32[]{:S(2)}, u32[]{:S(2)}) collective-permute-start(f32[136,128]{1,0:T(8,128)S(1)} %get-tuple-element.32), channel_id=1, source_target_pairs={{0,2},{2,0},{1,3},{3,1},{4,6},{6,4},{5,7},{7,5},{8,10},{10,8},{9,1... | collective-permute-start | bytes 208904 | tf_op jit(solution)/shard_map/ppermute | solution.py:365

commit v7 on v6

--- a/solution.py
+++ b/solution.py
@@ -233,45 +233,40 @@
     )(counts, *arrays)
 
 
-def pair_kernel(mine_ref, other_ref, keep_refs, send_refs):
+def pair_kernel(mine_ref, other_ref, keep_ref, send_ref):
     z = lax.axis_index("z")
-    step = 1 - 2 * lax.rem(z, 2)
-    for x, neighbour in ((0, z + step), (1, z - step)):
-        for ref, holder in ((keep_refs[x], z), (send_refs[x], neighbour)):
-            for s in range(4):
-                start = pl.multiple_of(lax.rem(holder + 2 * s + 8, 8) * 272 + x * 136, 8)
-                rows = pl.ds(start, 136)
-                ref[s * 136 : (s + 1) * 136, :] = mine_ref[rows, :] + other_ref[rows, :]
+    step = (1 - 2 * lax.rem(z, 2)) * (1 - 2 * lax.axis_index("core"))
+    for ref, holder in ((keep_ref, z), (send_ref, z + step)):
+        for s in range(4):
+            start = pl.multiple_of(lax.rem(holder + 2 * s + 8, 8) * 272, 8)
+            rows = pl.ds(start, 272)
+            ref[s * 272 : (s + 1) * 272, :] = mine_ref[rows, :] + other_ref[rows, :]
 
 
 def pair_sums(mine, other):
-    def kernel(mine_ref, other_ref, a, b, c, d):
-        pair_kernel(mine_ref, other_ref, (a, b), (c, d))
-
     return pl.pallas_call(
-        kernel,
+        pair_kernel,
         in_specs=[VMEM, VMEM],
-        out_specs=[VMEM] * 4,
-        out_shape=[f32((4 * 136, 128))] * 4,
+        out_specs=[VMEM] * 2,
+        out_shape=[f32((4 * 272, 128))] * 2,
         compiler_params=SMALL,
     )(mine, other)
 
 
-def quad_kernel(a_ref, b_ref, a_other_ref, b_other_ref, *out_refs):
+def quad_kernel(mine_ref, other_ref, *out_refs):
     for s in range(4):
-        rows = pl.ds(s * 136, 136)
-        out_refs[s][:136, :] = a_ref[rows, :] + a_other_ref[rows, :]
-        out_refs[s][136:, :] = b_ref[rows, :] + b_other_ref[rows, :]
-
-
-def quad_sums(*arrays):
+        rows = pl.ds(s * 272, 272)
+        out_refs[s][...] = mine_ref[rows, :] + other_ref[rows, :]
+
+
+def quad_sums(mine, other):
     return pl.pallas_call(
         quad_kernel,
-        in_specs=[VMEM] * 4,
+        in_specs=[VMEM] * 2,
         out_specs=[VMEM] * 4,
         out_shape=[f32((272, 128))] * 4,
         compiler_params=SMALL,
-    )(*arrays)
+    )(mine, other)
 
 
 def gather_kernel(*refs):
@@ -352,12 +347,13 @@
     second_parts = lax.all_to_all(
         second.reshape(16 * 129, 2, 128), ("x_hi", "y"), 0, 0, tiled=True
     ).reshape(16 * 258, 128)
-    keep_a, keep_b, send_a, send_b = pair_sums(keep, other)
-    pairs_a = [(i, i + 1 - 2 * (i % 2)) for i in range(8)]
-    pairs_b = [(i, (i - 1 + 2 * (i % 2)) % 8) for i in range(8)]
-    other_a = lax.ppermute(send_a, "z", pairs_a)
-    other_b = lax.ppermute(send_b, "z", pairs_b)
-    mine, *sums = quad_sums(keep_a, keep_b, other_a, other_b)
+    kept, sent = pair_sums(keep, other)
+    sides = [
+        (2 * i + c, 2 * ((i + (1 - 2 * (i % 2)) * (1 - 2 * c)) % 8) + c)
+        for i in range(8)
+        for c in range(2)
+    ]
+    mine, *sums = quad_sums(kept, lax.ppermute(sent, ("z", "core"), sides))
     arrivals = [
         lax.ppermute(sums[s - 1], "z", [(i, (i + 2 * s) % 8) for i in range(8)]) for s in (2, 1, 3)
     ]

time: 70.7 us -> 70.7 us (level)
  the two profiles are of different devices: /device:TPU:6 before, /device:TPU:8 now
where the time goes in v7:
time: 70.7 us; the launch traced here: 70.3 us
  starting transfers between devices  37.5 us (53%)
  waiting for transfers between devices  22.4 us (32%)
  Pallas kernels  8.93 us (13%)
  between operations  1.38 us (2%)
    ppermute x3, starting transfers between devices, per_device(): lax.ppermute(sums[s - 1], 'z', [(i, (i + 2 * s) % 8) for i in range(8)])  18.5 us
    all_to_all x1, starting transfers between devices, per_device(): lax.all_to_all(second.reshape(16 * 129, 2, 128), ('x_hi', 'y'), 0, 0, til...  10.2 us
    ppermute x1, waiting for transfers between devices, per_device(): mine, *sums = quad_sums(kept, lax.ppermute(sent, ('z', 'core'), sides))  7.5 us
    pallas_call x1, Pallas kernels, level_terms(): pl.pallas_call(terms_kernel, in_specs=[SMEM] + [HBM] * 4, out_specs=[HBM]...  7.21 us
    ppermute x3, waiting for transfers between devices, per_device(): lax.ppermute(sums[s - 1], 'z', [(i, (i + 2 * s) % 8) for i in range(8)])  6.85 us
    ppermute x1, starting transfers between devices, per_device(): mine, *sums = quad_sums(kept, lax.ppermute(sent, ('z', 'core'), sides))  4.28 us
    ppermute x1, waiting for transfers between devices, per_device(): across = lax.ppermute(away, 'x_lo', [(0, 1), (1, 0)])  3.84 us
    ppermute x1, waiting for transfers between devices, per_device(): other = lax.ppermute(send, 'core', [(0, 1), (1, 0)])  2.93 us
  transfers between devices with their start and end apart: 7, of which 6 were waited for; matrix products, arithmetic and copies ran while one was open for 0% of the time, Pallas kernels for 1%

profile of v7, /device:TPU:8, one launch (start us, length us, event | category | flops | bytes accessed | tf_op | source)
XLA Modules:
  0.0 70.3 jit_solution(2812373868484333625)
XLA Ops:
  1.3 7.2 %shard_map.120 = (f32[4128,128]{1,0:T(8,128)}, f32[2176,128]{1,0:T(8,128)}, f32[2176,128]{1,0:T(8,128)}) custom-call(s32[1,1]{1,0:T(1,128)S(6)} %copy.13.counts_ref, bf16[256,2048]{1,0:T(8,128)(2,1)} %bitcast.21, bf16[2048,512]{1,0:T(8,128)(2,1)} %bitcast.20, bf16[256,1024]{1,0:T(8,128)(2,1)} %bitcast.22, bf16[256,1024]{1,0:T(8,128)(2,1)} %bitcast.23), custom_call_target="tpu_custom_call" | custom-call | flops 2000000000 | bytes 8388608 | tf_op jit(solution)/shard_map/pallas_call | solution.py:214
  8.5 0.0 copy-start
  8.5 10.2 %all-to-all-start = ((f32[2064,2,128]{2,1,0:T(2,128)}), f32[2064,2,128]{2,1,0:T(2,128)S(1)}, u32[]{:S(2)}, u32[]{:S(2)}) async-start(f32[2064,2,128]{2,1,0:T(2,128)} %bitcast.19), calls=%async_computation | async-start | bytes 4227072 | tf_op jit(solution)/shard_map/all_to_all | solution.py:347
  18.7 0.0 copy-start.4
  18.7 2.1 %collective-permute-start = (f32[2176,128]{1,0:T(8,128)}, f32[2176,128]{1,0:T(8,128)S(1)}, u32[]{:S(2)}, u32[]{:S(2)}) collective-permute-start(f32[2176,128]{1,0:T(8,128)} %get-tuple-element.20), channel_id=1, source_target_pairs={{0,1},{1,0},{2,3},{3,2},{4,5},{5,4},{6,7},{7,6},{8,9},{9,8},{10,11... | collective-permute-start | bytes 3342344 | tf_op jit(solution)/shard_map/ppermute | solution.py:346
  20.7 2.9 %collective-permute-done.other_ref = f32[2176,128]{1,0:T(8,128)S(1)} collective-permute-done((f32[2176,128]{1,0:T(8,128)}, f32[2176,128]{1,0:T(8,128)S(1)}, u32[]{:S(2)}, u32[]{:S(2)}) %collective-permute-start) | collective-permute-done | bytes 1114144 | tf_op jit(solution)/shard_map/ppermute | solution.py:346
  23.7 0.0 copy-done
  23.7 0.1 shard_map.121
  23.8 4.3 %collective-permute-start.1 = (f32[1088,128]{1,0:T(8,128)S(1)}, f32[1088,128]{1,0:T(8,128)S(1)}, u32[]{:S(2)}, u32[]{:S(2)}) collective-permute-start(f32[1088,128]{1,0:T(8,128)S(1)} %get-tuple-element.22), channel_id=1, source_target_pairs={{0,4},{1,29},{4,0},{5,9},{8,12},{9,5},{12,8},{13,17},{16,20},{17,1... | collective-permute-start | bytes 1671176 | tf_op jit(solution)/shard_map/ppermute | solution.py:356
  28.1 7.5 %collective-permute-done.1.other_ref = f32[1088,128]{1,0:T(8,128)S(1)} collective-permute-done((f32[1088,128]{1,0:T(8,128)S(1)}, f32[1088,128]{1,0:T(8,128)S(1)}, u32[]{:S(2)}, u32[]{:S(2)}) %collective-permute-start.1) | collective-permute-done | bytes 557088 | tf_op jit(solution)/shard_map/ppermute | solution.py:356
  35.6 0.1 shard_map.122
  35.6 10.6 %collective-permute-start.2 = (f32[272,128]{1,0:T(8,128)S(1)}, f32[272,128]{1,0:T(8,128)S(1)}, u32[]{:S(2)}, u32[]{:S(2)}) collective-permute-start(f32[272,128]{1,0:T(8,128)S(1)} %get-tuple-element.24), channel_id=1, source_target_pairs={{0,16},{4,20},{8,24},{12,28},{16,0},{20,4},{24,8},{28,12},{1,17},{... | collective-permute-start | bytes 417800 | tf_op jit(solution)/shard_map/ppermute | solution.py:358
  46.2 4.3 %collective-permute-start.3 = (f32[272,128]{1,0:T(8,128)S(1)}, f32[272,128]{1,0:T(8,128)S(1)}, u32[]{:S(2)}, u32[]{:S(2)}) collective-permute-start(f32[272,128]{1,0:T(8,128)S(1)} %get-tuple-element.25), channel_id=1, source_target_pairs={{0,8},{4,12},{8,16},{12,20},{16,24},{20,28},{24,0},{28,4},{1,9},{5... | collective-permute-start | bytes 417800 | tf_op jit(solution)/shard_map/ppermute | solution.py:358
  50.5 3.7 %collective-permute-start.4 = (f32[272,128]{1,0:T(8,128)S(1)}, f32[272,128]{1,0:T(8,128)S(1)}, u32[]{:S(2)}, u32[]{:S(2)}) collective-permute-start(f32[272,128]{1,0:T(8,128)S(1)} %get-tuple-element.26), channel_id=1, source_target_pairs={{0,24},{4,28},{8,0},{12,4},{16,8},{20,12},{24,16},{28,20},{1,25},{... | collective-permute-start | bytes 417800 | tf_op jit(solution)/shard_map/ppermute | solution.py:358
  54.2 0.0 collective-permute-done.2.refs_1_
  54.2 2.1 %collective-permute-done.3.refs_2_ = f32[272,128]{1,0:T(8,128)S(1)} collective-permute-done((f32[272,128]{1,0:T(8,128)S(1)}, f32[272,128]{1,0:T(8,128)S(1)}, u32[]{:S(2)}, u32[]{:S(2)}) %collective-permute-start.3) | collective-permute-done | bytes 139296 | tf_op jit(solution)/shard_map/ppermute | solution.py:358
  56.3 4.8 %collective-permute-done.4.refs_3_ = f32[272,128]{1,0:T(8,128)S(1)} collective-permute-done((f32[272,128]{1,0:T(8,128)S(1)}, f32[272,128]{1,0:T(8,128)S(1)}, u32[]{:S(2)}, u32[]{:S(2)}) %collective-permute-start.4) | collective-permute-done | bytes 139296 | tf_op jit(solution)/shard_map/ppermute | solution.py:358
  61.1 2.5 %collective-permute-start.5 = (f32[136,128]{1,0:T(8,128)S(1)}, f32[136,128]{1,0:T(8,128)S(1)}, u32[]{:S(2)}, u32[]{:S(2)}) collective-permute-start(f32[136,128]{1,0:T(8,128)S(1)} %get-tuple-element.28), channel_id=1, source_target_pairs={{0,2},{2,0},{1,3},{3,1},{4,6},{6,4},{5,7},{7,5},{8,10},{10,8},{9,1... | collective-permute-start | bytes 208904 | tf_op jit(solution)/shard_map/ppermute | solution.py:361
  63.6 3.8 %collective-permute-done.5.other_ref = f32[136,128]{1,0:T(8,128)S(1)} collective-permute-done((f32[136,128]{1,0:T(8,128)S(1)}, f32[136,128]{1,0:T(8,128)S(1)}, u32[]{:S(2)}, u32[]{:S(2)}) %collective-permute-start.5) | collective-permute-done | bytes 69664 | tf_op jit(solution)/shard_map/ppermute | solution.py:361
  67.4 0.0 copy-done.4
  67.4 0.7 shard_map.124
  68.1 1.3 %all-to-all-done = f32[2064,2,128]{2,1,0:T(2,128)S(1)} async-done(((f32[2064,2,128]{2,1,0:T(2,128)}), f32[2064,2,128]{2,1,0:T(2,128)S(1)}, u32[]{:S(2)}, u32[]{:S(2)}) %all-to-all-start) | async-done | bytes 2113568 | tf_op jit(solution)/shard_map/all_to_all | solution.py:347
  69.5 0.0 copy-done.2
  69.5 0.8 %shard_map.125 = (f32[128,256]{1,0:T(8,128)}, f32[128,256]{1,0:T(8,128)}) custom-call(f32[4128,128]{1,0:T(8,128)S(1)} %bitcast.14, f32[128,256]{1,0:T(8,128)S(1)} %bitcast.15, f32[128,256]{1,0:T(8,128)S(1)} %bitcast.16), custom_call_target="tpu_custom_call" | custom-call | tf_op jit(solution)/shard_map/pallas_call | solution.py:323
  (6 shorter events, 0.0 us)
Async XLA Ops:
  8.5 15.2 %copy-start = (f32[2176,128]{1,0:T(8,128)S(1)}, f32[2176,128]{1,0:T(8,128)}, u32[]{:S(2)}) copy-start(f32[2176,128]{1,0:T(8,128)} %get-tuple-element.19.mine_ref) | copy-start | bytes 3342340
  8.5 60.9 %all-to-all-start = ((f32[2064,2,128]{2,1,0:T(2,128)}), f32[2064,2,128]{2,1,0:T(2,128)S(1)}, u32[]{:S(2)}, u32[]{:S(2)}) async-start(f32[2064,2,128]{2,1,0:T(2,128)} %bitcast.19), calls=%async_computation | async-start | bytes 4227072 | tf_op jit(solution)/shard_map/all_to_all | solution.py:347
  18.7 48.8 %copy-start.3 = (f32[1,64,256]{2,1,0:T(8,128)S(1)}, f32[1,64,256]{2,1,0:T(8,128)}, u32[]{:S(2)}) copy-start(f32[1,64,256]{2,1,0:T(8,128)} %param.14) | copy-start | bytes 196612
  18.7 48.8 %copy-start.4 = (f32[1,64,256]{2,1,0:T(8,128)S(1)}, f32[1,64,256]{2,1,0:T(8,128)}, u32[]{:S(2)}) copy-start(f32[1,64,256]{2,1,0:T(8,128)} %param.15) | copy-start | bytes 196612
  18.7 5.0 %collective-permute-start = (f32[2176,128]{1,0:T(8,128)}, f32[2176,128]{1,0:T(8,128)S(1)}, u32[]{:S(2)}, u32[]{:S(2)}) collective-permute-start(f32[2176,128]{1,0:T(8,128)} %get-tuple-element.20), channel_id=1, source_target_pairs={{0,1},{1,0},{2,3},{3,2},{4,5},{5,4},{6,7},{7,6},{8,9},{9,8},{10,11... | collective-permute-start | bytes 3342344 | tf_op jit(solution)/shard_map/ppermute | solution.py:346
  23.7 45.8 %copy-start.1 = (f32[1,128,256]{2,1,0:T(8,128)S(1)}, f32[1,128,256]{2,1,0:T(8,128)}, u32[]{:S(2)}) copy-start(f32[1,128,256]{2,1,0:T(8,128)} %param.16) | copy-start | bytes 393220
  23.7 45.8 %copy-start.2 = (f32[1,128,256]{2,1,0:T(8,128)S(1)}, f32[1,128,256]{2,1,0:T(8,128)}, u32[]{:S(2)}) copy-start(f32[1,128,256]{2,1,0:T(8,128)} %param.17) | copy-start | bytes 393220
  23.8 11.8 %collective-permute-start.1 = (f32[1088,128]{1,0:T(8,128)S(1)}, f32[1088,128]{1,0:T(8,128)S(1)}, u32[]{:S(2)}, u32[]{:S(2)}) collective-permute-start(f32[1088,128]{1,0:T(8,128)S(1)} %get-tuple-element.22), channel_id=1, source_target_pairs={{0,4},{1,29},{4,0},{5,9},{8,12},{9,5},{12,8},{13,17},{16,20},{17,1... | collective-permute-start | bytes 1671176 | tf_op jit(solution)/shard_map/ppermute | solution.py:356
  35.6 18.5 %collective-permute-start.2 = (f32[272,128]{1,0:T(8,128)S(1)}, f32[272,128]{1,0:T(8,128)S(1)}, u32[]{:S(2)}, u32[]{:S(2)}) collective-permute-start(f32[272,128]{1,0:T(8,128)S(1)} %get-tuple-element.24), channel_id=1, source_target_pairs={{0,16},{4,20},{8,24},{12,28},{16,0},{20,4},{24,8},{28,12},{1,17},{... | collective-permute-start | bytes 417800 | tf_op jit(solution)/shard_map/ppermute | solution.py:358
  46.2 10.1 %collective-permute-start.3 = (f32[272,128]{1,0:T(8,128)S(1)}, f32[272,128]{1,0:T(8,128)S(1)}, u32[]{:S(2)}, u32[]{:S(2)}) collective-permute-start(f32[272,128]{1,0:T(8,128)S(1)} %get-tuple-element.25), channel_id=1, source_target_pairs={{0,8},{4,12},{8,16},{12,20},{16,24},{20,28},{24,0},{28,4},{1,9},{5... | collective-permute-start | bytes 417800 | tf_op jit(solution)/shard_map/ppermute | solution.py:358
  50.5 10.5 %collective-permute-start.4 = (f32[272,128]{1,0:T(8,128)S(1)}, f32[272,128]{1,0:T(8,128)S(1)}, u32[]{:S(2)}, u32[]{:S(2)}) collective-permute-start(f32[272,128]{1,0:T(8,128)S(1)} %get-tuple-element.26), channel_id=1, source_target_pairs={{0,24},{4,28},{8,0},{12,4},{16,8},{20,12},{24,16},{28,20},{1,25},{... | collective-permute-start | bytes 417800 | tf_op jit(solution)/shard_map/ppermute | solution.py:358
  61.1 6.4 %collective-permute-start.5 = (f32[136,128]{1,0:T(8,128)S(1)}, f32[136,128]{1,0:T(8,128)S(1)}, u32[]{:S(2)}, u32[]{:S(2)}) collective-permute-start(f32[136,128]{1,0:T(8,128)S(1)} %get-tuple-element.28), channel_id=1, source_target_pairs={{0,2},{2,0},{1,3},{3,1},{4,6},{6,4},{5,7},{7,5},{8,10},{10,8},{9,1... | collective-permute-start | bytes 208904 | tf_op jit(solution)/shard_map/ppermute | solution.py:361

commit v8 on v7

--- a/solution.py
+++ b/solution.py
@@ -152,7 +152,7 @@
     scale = count * (inner_rate * factor)
     counts = jnp.full((8, 128), count, jnp.float32)
     for r in range(16):
-        second_ref[r * 258 + 256 : r * 258 + 258, :] = counts[:2]
+        second_ref[r * 257 + 256 : r * 257 + 257, :] = counts[:1]
         for core in range(2):
             first_ref[core, r * 136 + 128 : r * 136 + 136, :] = counts
 
@@ -180,12 +180,11 @@
             own_weights = weights_ref[rows, level * level_columns : (level + 1) * level_columns]
             piece = count * own_weights.astype(jnp.float32) - scale * nn(turned_ref[rows, :], dkeyval)
             if level == 1:
-                base = r * 258
+                base = r * 257
                 second_ref[base : base + 128, :] = piece[:, :128]
                 second_ref[base + 128 : base + 256, :] = piece[:, 128:]
-                if r % 4 == 3:
-                    done = pl.ds(base - 3 * 258, 4 * 258)
-                    leave(second_ref.at[done], second.at[done])
+                if r == 15:
+                    leave(second_ref, second)
             else:
                 base = r * 136
                 for core in range(2):
@@ -215,16 +214,16 @@
         terms_kernel,
         in_specs=[SMEM] + [HBM] * 4,
         out_specs=[HBM] * 3,
-        out_shape=[f32((16 * 258, 128)), f32((16 * 136, 128)), f32((16 * 136, 128))],
+        out_shape=[f32((16 * 257, 128)), f32((16 * 136, 128)), f32((16 * 136, 128))],
         scratch_shapes=[
             pltpu.VMEM(shape, jnp.bfloat16)
             for shape in (hidden.shape, hidden.shape[::-1], weights.shape, queries.shape, cotangent.shape)
         ]
         + [
-            pltpu.VMEM((16 * 258, 128), jnp.float32),
+            pltpu.VMEM((16 * 257, 128), jnp.float32),
             pltpu.VMEM((2, 16 * 136, 128), jnp.float32),
             pltpu.SemaphoreType.DMA((2 * PARTS + 2,)),
-            pltpu.SemaphoreType.DMA((12,)),
+            pltpu.SemaphoreType.DMA((9,)),
         ],
         compiler_params=pltpu.CompilerParams(vmem_limit_bytes=62 * 1024 * 1024),
         cost_estimate=pl.CostEstimate(
@@ -313,9 +312,9 @@
 
 
 def second_finish_kernel(parts_ref, *refs):
-    total = parts_ref[0:258, :]
+    total = parts_ref[0:257, :]
     for r in range(1, 16):
-        total += parts_ref[r * 258 : (r + 1) * 258, :]
+        total += parts_ref[r * 257 : (r + 1) * 257, :]
     finish(total, 128, *refs)
 
 
@@ -345,8 +344,8 @@
     )
     other = lax.ppermute(send, "core", [(0, 1), (1, 0)])
     second_parts = lax.all_to_all(
-        second.reshape(16 * 129, 2, 128), ("x_hi", "y"), 0, 0, tiled=True
-    ).reshape(16 * 258, 128)
+        second.reshape(16 * 257, 1, 128), ("x_hi", "y"), 0, 0, tiled=True
+    ).reshape(16 * 257, 128)
     kept, sent = pair_sums(keep, other)
     sides = [
         (2 * i + c, 2 * ((i + (1 - 2 * (i % 2)) * (1 - 2 * c)) % 8) + c)

time: 70.7 us -> 70.5 us (level)
  the two profiles are of different devices: /device:TPU:8 before, /device:TPU:72 now
where the time goes in v8:
time: 70.5 us; the launch traced here: 70.1 us
  starting transfers between devices  34.6 us (49%)
  waiting for transfers between devices  25.2 us (36%)
  Pallas kernels  8.97 us (13%)
  between operations  1.38 us (2%)
    ppermute x3, starting transfers between devices, per_device(): lax.ppermute(sums[s - 1], 'z', [(i, (i + 2 * s) % 8) for i in range(8)])  18 us
    all_to_all x1, starting transfers between devices, per_device(): lax.all_to_all(second.reshape(16 * 257, 1, 128), ('x_hi', 'y'), 0, 0, til...  10.2 us
    ppermute x1, waiting for transfers between devices, per_device(): mine, *sums = quad_sums(kept, lax.ppermute(sent, ('z', 'core'), sides))  9.5 us
    ppermute x3, waiting for transfers between devices, per_device(): lax.ppermute(sums[s - 1], 'z', [(i, (i + 2 * s) % 8) for i in range(8)])  7.62 us
    pallas_call x1, Pallas kernels, level_terms(): pl.pallas_call(terms_kernel, in_specs=[SMEM] + [HBM] * 4, out_specs=[HBM]...  7.19 us
    ppermute x1, waiting for transfers between devices, per_device(): across = lax.ppermute(away, 'x_lo', [(0, 1), (1, 0)])  3.84 us
    ppermute x1, waiting for transfers between devices, per_device(): other = lax.ppermute(send, 'core', [(0, 1), (1, 0)])  2.93 us
    ppermute x1, starting transfers between devices, per_device(): across = lax.ppermute(away, 'x_lo', [(0, 1), (1, 0)])  2.5 us
  transfers between devices with their start and end apart: 7, of which 6 were waited for; matrix products, arithmetic and copies ran while one was open for 0% of the time, Pallas kernels for 1%

profile of v8, /device:TPU:72, one launch (start us, length us, event | category | flops | bytes accessed | tf_op | source)
XLA Modules:
  0.0 70.1 jit_solution(16799150383842206733)
XLA Ops:
  1.3 7.2 %shard_map.120 = (f32[4112,128]{1,0:T(8,128)}, f32[2176,128]{1,0:T(8,128)}, f32[2176,128]{1,0:T(8,128)}) custom-call(s32[1,1]{1,0:T(1,128)S(6)} %copy.14.counts_ref, bf16[256,2048]{1,0:T(8,128)(2,1)} %bitcast.23, bf16[2048,512]{1,0:T(8,128)(2,1)} %bitcast.22, bf16[256,1024]{1,0:T(8,128)(2,1)} %bitcast.24, bf16[256,1024]{1,0:T(8,128)(2,1)} %bitcast.25), custom_call_target="tpu_custom_call" | custom-call | flops 2000000000 | bytes 8388608 | tf_op jit(solution)/shard_map/pallas_call | solution.py:213
  8.5 0.0 copy-start
  8.5 10.2 %all-to-all-start = ((f32[4112,1,128]{2,1,0:T(1,128)}), f32[4112,1,128]{2,1,0:T(1,128)S(1)}, u32[]{:S(2)}, u32[]{:S(2)}) async-start(f32[4112,1,128]{2,1,0:T(1,128)} %bitcast.21), calls=%async_computation | async-start | bytes 4210688 | tf_op jit(solution)/shard_map/all_to_all | solution.py:346
  18.7 0.0 copy-start.4
  18.7 2.1 %collective-permute-start = (f32[2176,128]{1,0:T(8,128)}, f32[2176,128]{1,0:T(8,128)S(1)}, u32[]{:S(2)}, u32[]{:S(2)}) collective-permute-start(f32[2176,128]{1,0:T(8,128)} %get-tuple-element.20), channel_id=1, source_target_pairs={{0,1},{1,0},{2,3},{3,2},{4,5},{5,4},{6,7},{7,6},{8,9},{9,8},{10,11... | collective-permute-start | bytes 3342344 | tf_op jit(solution)/shard_map/ppermute | solution.py:345
  20.7 2.9 %collective-permute-done.other_ref = f32[2176,128]{1,0:T(8,128)S(1)} collective-permute-done((f32[2176,128]{1,0:T(8,128)}, f32[2176,128]{1,0:T(8,128)S(1)}, u32[]{:S(2)}, u32[]{:S(2)}) %collective-permute-start) | collective-permute-done | bytes 1114144 | tf_op jit(solution)/shard_map/ppermute | solution.py:345
  23.7 0.0 copy-done
  23.7 0.1 shard_map.121
  23.8 1.9 %collective-permute-start.1 = (f32[1088,128]{1,0:T(8,128)S(1)}, f32[1088,128]{1,0:T(8,128)S(1)}, u32[]{:S(2)}, u32[]{:S(2)}) collective-permute-start(f32[1088,128]{1,0:T(8,128)S(1)} %get-tuple-element.22), channel_id=1, source_target_pairs={{0,4},{1,29},{4,0},{5,9},{8,12},{9,5},{12,8},{13,17},{16,20},{17,1... | collective-permute-start | bytes 1671176 | tf_op jit(solution)/shard_map/ppermute | solution.py:355
  25.7 9.5 %collective-permute-done.1.other_ref = f32[1088,128]{1,0:T(8,128)S(1)} collective-permute-done((f32[1088,128]{1,0:T(8,128)S(1)}, f32[1088,128]{1,0:T(8,128)S(1)}, u32[]{:S(2)}, u32[]{:S(2)}) %collective-permute-start.1) | collective-permute-done | bytes 557088 | tf_op jit(solution)/shard_map/ppermute | solution.py:355
  35.2 0.1 shard_map.122
  35.3 10.0 %collective-permute-start.2 = (f32[272,128]{1,0:T(8,128)S(1)}, f32[272,128]{1,0:T(8,128)S(1)}, u32[]{:S(2)}, u32[]{:S(2)}) collective-permute-start(f32[272,128]{1,0:T(8,128)S(1)} %get-tuple-element.24), channel_id=1, source_target_pairs={{0,16},{4,20},{8,24},{12,28},{16,0},{20,4},{24,8},{28,12},{1,17},{... | collective-permute-start | bytes 417800 | tf_op jit(solution)/shard_map/ppermute | solution.py:357
  45.3 4.3 %collective-permute-start.3 = (f32[272,128]{1,0:T(8,128)S(1)}, f32[272,128]{1,0:T(8,128)S(1)}, u32[]{:S(2)}, u32[]{:S(2)}) collective-permute-start(f32[272,128]{1,0:T(8,128)S(1)} %get-tuple-element.25), channel_id=1, source_target_pairs={{0,8},{4,12},{8,16},{12,20},{16,24},{20,28},{24,0},{28,4},{1,9},{5... | collective-permute-start | bytes 417800 | tf_op jit(solution)/shard_map/ppermute | solution.py:357
  49.6 3.6 %collective-permute-start.4 = (f32[272,128]{1,0:T(8,128)S(1)}, f32[272,128]{1,0:T(8,128)S(1)}, u32[]{:S(2)}, u32[]{:S(2)}) collective-permute-start(f32[272,128]{1,0:T(8,128)S(1)} %get-tuple-element.26), channel_id=1, source_target_pairs={{0,24},{4,28},{8,0},{12,4},{16,8},{20,12},{24,16},{28,20},{1,25},{... | collective-permute-start | bytes 417800 | tf_op jit(solution)/shard_map/ppermute | solution.py:357
  53.3 0.0 collective-permute-done.2.refs_1_
  53.3 4.2 %collective-permute-done.3.refs_2_ = f32[272,128]{1,0:T(8,128)S(1)} collective-permute-done((f32[272,128]{1,0:T(8,128)S(1)}, f32[272,128]{1,0:T(8,128)S(1)}, u32[]{:S(2)}, u32[]{:S(2)}) %collective-permute-start.3) | collective-permute-done | bytes 139296 | tf_op jit(solution)/shard_map/ppermute | solution.py:357
  57.4 3.5 %collective-permute-done.4.refs_3_ = f32[272,128]{1,0:T(8,128)S(1)} collective-permute-done((f32[272,128]{1,0:T(8,128)S(1)}, f32[272,128]{1,0:T(8,128)S(1)}, u32[]{:S(2)}, u32[]{:S(2)}) %collective-permute-start.4) | collective-permute-done | bytes 139296 | tf_op jit(solution)/shard_map/ppermute | solution.py:357
  61.0 2.5 %collective-permute-start.5 = (f32[136,128]{1,0:T(8,128)S(1)}, f32[136,128]{1,0:T(8,128)S(1)}, u32[]{:S(2)}, u32[]{:S(2)}) collective-permute-start(f32[136,128]{1,0:T(8,128)S(1)} %get-tuple-element.28), channel_id=1, source_target_pairs={{0,2},{2,0},{1,3},{3,1},{4,6},{6,4},{5,7},{7,5},{8,10},{10,8},{9,1... | collective-permute-start | bytes 208904 | tf_op jit(solution)/shard_map/ppermute | solution.py:360
  63.5 3.8 %collective-permute-done.5.other_ref = f32[136,128]{1,0:T(8,128)S(1)} collective-permute-done((f32[136,128]{1,0:T(8,128)S(1)}, f32[136,128]{1,0:T(8,128)S(1)}, u32[]{:S(2)}, u32[]{:S(2)}) %collective-permute-start.5) | collective-permute-done | bytes 69664 | tf_op jit(solution)/shard_map/ppermute | solution.py:360
  67.3 0.0 copy-done.3
  67.3 0.7 shard_map.124
  68.0 1.3 %all-to-all-done = f32[4112,1,128]{2,1,0:T(1,128)S(1)} async-done(((f32[4112,1,128]{2,1,0:T(1,128)}), f32[4112,1,128]{2,1,0:T(1,128)S(1)}, u32[]{:S(2)}, u32[]{:S(2)}) %all-to-all-start) | async-done | bytes 2105376 | tf_op jit(solution)/shard_map/all_to_all | solution.py:346
  69.3 0.0 copy-done.1
  69.3 0.9 %shard_map.125 = (f32[128,256]{1,0:T(8,128)}, f32[128,256]{1,0:T(8,128)}) custom-call(f32[4112,128]{1,0:T(8,128)S(1)} %bitcast.16, f32[128,256]{1,0:T(8,128)S(1)} %bitcast.17, f32[128,256]{1,0:T(8,128)S(1)} %bitcast.18), custom_call_target="tpu_custom_call" | custom-call | tf_op jit(solution)/shard_map/pallas_call | solution.py:322
  (6 shorter events, 0.0 us)
Async XLA Ops:
  8.5 15.2 %copy-start = (f32[2176,128]{1,0:T(8,128)S(1)}, f32[2176,128]{1,0:T(8,128)}, u32[]{:S(2)}) copy-start(f32[2176,128]{1,0:T(8,128)} %get-tuple-element.19.mine_ref) | copy-start | bytes 3342340
  8.5 60.8 %all-to-all-start = ((f32[4112,1,128]{2,1,0:T(1,128)}), f32[4112,1,128]{2,1,0:T(1,128)S(1)}, u32[]{:S(2)}, u32[]{:S(2)}) async-start(f32[4112,1,128]{2,1,0:T(1,128)} %bitcast.21), calls=%async_computation | async-start | bytes 4210688 | tf_op jit(solution)/shard_map/all_to_all | solution.py:346
  18.6 48.7 %copy-start.3 = (f32[1,64,256]{2,1,0:T(8,128)S(1)}, f32[1,64,256]{2,1,0:T(8,128)}, u32[]{:S(2)}) copy-start(f32[1,64,256]{2,1,0:T(8,128)} %param.14) | copy-start | bytes 196612
  18.7 48.6 %copy-start.4 = (f32[1,64,256]{2,1,0:T(8,128)S(1)}, f32[1,64,256]{2,1,0:T(8,128)}, u32[]{:S(2)}) copy-start(f32[1,64,256]{2,1,0:T(8,128)} %param.15) | copy-start | bytes 196612
  18.7 5.0 %collective-permute-start = (f32[2176,128]{1,0:T(8,128)}, f32[2176,128]{1,0:T(8,128)S(1)}, u32[]{:S(2)}, u32[]{:S(2)}) collective-permute-start(f32[2176,128]{1,0:T(8,128)} %get-tuple-element.20), channel_id=1, source_target_pairs={{0,1},{1,0},{2,3},{3,2},{4,5},{5,4},{6,7},{7,6},{8,9},{9,8},{10,11... | collective-permute-start | bytes 3342344 | tf_op jit(solution)/shard_map/ppermute | solution.py:345
  23.7 45.6 %copy-start.1 = (f32[1,128,256]{2,1,0:T(8,128)S(1)}, f32[1,128,256]{2,1,0:T(8,128)}, u32[]{:S(2)}) copy-start(f32[1,128,256]{2,1,0:T(8,128)} %param.16) | copy-start | bytes 393220
  23.7 45.6 %copy-start.2 = (f32[1,128,256]{2,1,0:T(8,128)S(1)}, f32[1,128,256]{2,1,0:T(8,128)}, u32[]{:S(2)}) copy-start(f32[1,128,256]{2,1,0:T(8,128)} %param.17) | copy-start | bytes 393220
  23.8 11.4 %collective-permute-start.1 = (f32[1088,128]{1,0:T(8,128)S(1)}, f32[1088,128]{1,0:T(8,128)S(1)}, u32[]{:S(2)}, u32[]{:S(2)}) collective-permute-start(f32[1088,128]{1,0:T(8,128)S(1)} %get-tuple-element.22), channel_id=1, source_target_pairs={{0,4},{1,29},{4,0},{5,9},{8,12},{9,5},{12,8},{13,17},{16,20},{17,1... | collective-permute-start | bytes 1671176 | tf_op jit(solution)/shard_map/ppermute | solution.py:355
  35.3 18.0 %collective-permute-start.2 = (f32[272,128]{1,0:T(8,128)S(1)}, f32[272,128]{1,0:T(8,128)S(1)}, u32[]{:S(2)}, u32[]{:S(2)}) collective-permute-start(f32[272,128]{1,0:T(8,128)S(1)} %get-tuple-element.24), channel_id=1, source_target_pairs={{0,16},{4,20},{8,24},{12,28},{16,0},{20,4},{24,8},{28,12},{1,17},{... | collective-permute-start | bytes 417800 | tf_op jit(solution)/shard_map/ppermute | solution.py:357
  45.3 12.1 %collective-permute-start.3 = (f32[272,128]{1,0:T(8,128)S(1)}, f32[272,128]{1,0:T(8,128)S(1)}, u32[]{:S(2)}, u32[]{:S(2)}) collective-permute-start(f32[272,128]{1,0:T(8,128)S(1)} %get-tuple-element.25), channel_id=1, source_target_pairs={{0,8},{4,12},{8,16},{12,20},{16,24},{20,28},{24,0},{28,4},{1,9},{5... | collective-permute-start | bytes 417800 | tf_op jit(solution)/shard_map/ppermute | solution.py:357
  49.6 11.3 %collective-permute-start.4 = (f32[272,128]{1,0:T(8,128)S(1)}, f32[272,128]{1,0:T(8,128)S(1)}, u32[]{:S(2)}, u32[]{:S(2)}) collective-permute-start(f32[272,128]{1,0:T(8,128)S(1)} %get-tuple-element.26), channel_id=1, source_target_pairs={{0,24},{4,28},{8,0},{12,4},{16,8},{20,12},{24,16},{28,20},{1,25},{... | collective-permute-start | bytes 417800 | tf_op jit(solution)/shard_map/ppermute | solution.py:357
  61.0 6.3 %collective-permute-start.5 = (f32[136,128]{1,0:T(8,128)S(1)}, f32[136,128]{1,0:T(8,128)S(1)}, u32[]{:S(2)}, u32[]{:S(2)}) collective-permute-start(f32[136,128]{1,0:T(8,128)S(1)} %get-tuple-element.28), channel_id=1, source_target_pairs={{0,2},{2,0},{1,3},{3,1},{4,6},{6,4},{5,7},{7,5},{8,10},{10,8},{9,1... | collective-permute-start | bytes 208904 | tf_op jit(solution)/shard_map/ppermute | solution.py:360
